TPU v7x, 32 devices: a whole 2x2x4 slice. The times are simulated.
32 devices in a mesh: dp: 16 (over z, x, core), tensor: 2 (over y).
Axes of the slice: x: 2, y: 2, z: 4, core: 2. Of those that a mesh axis runs over, the one named last changes fastest.
Arguments:
- inputs: bfloat16 [40960, 1024], P(('dp', 'tensor')), may hold values from -6 to 6
- teacher: bfloat16 [40960, 1024], P(('dp', 'tensor')), may hold values from -6 to 6
- lengths: int32 [128], replicated, may hold values from 200 to 320, as said below
- first_gain: float32 [1024], replicated, may hold values from 0.5 to 1.5
- first_shift: float32 [1024], replicated, may hold values from -0.2 to 0.2
- query_key_value_weight: bfloat16 [3, 1024, 1024], P(None, 'dp', 'tensor'), may hold values from -0.1875 to 0.1875
- heads_bias: float32 [2, 1024], P(None, 'tensor'), may hold values from -0.2 to 0.2
- merge_weight: bfloat16 [1024, 1024], P('dp', 'tensor'), may hold values from -1.5 to 1.5
- merge_bias: float32 [1024], replicated, may hold values from -0.6 to 0.6
- second_gain: float32 [1024], replicated, may hold values from 0.5 to 1.5
- second_shift: float32 [1024], replicated, may hold values from -0.6 to 0.6
- expand_weight: bfloat16 [1024, 4096], P('dp', 'tensor'), may hold values from -0.1875 to 0.1875
- expand_bias: float32 [4096], P('tensor'), may hold values from -0.6 to 0.6
- reduce_weight: bfloat16 [1024, 4096], P('dp', 'tensor'), may hold values from -0.09375 to 0.09375
- reduce_bias: float32 [1024], replicated, may hold values from -0.6 to 0.6
Outputs:
- loss_value: float32 [], replicated
- outputs: bfloat16 [40960, 1024], P(('dp', 'tensor'))
- inputs_grad: float32 [40960, 1024], P(('dp', 'tensor'))
- first_gain_grad: float32 [1024], replicated
- first_shift_grad: float32 [1024], replicated
- heads_weight_grad: float32 [3, 1024, 1024], P(None, 'dp', 'tensor')
- heads_bias_grad: float32 [2, 1024], P(None, 'tensor')
- merge_weight_grad: float32 [1024, 1024], P('dp', 'tensor')
- merge_bias_grad: float32 [1024], replicated
- second_gain_grad: float32 [1024], replicated
- second_shift_grad: float32 [1024], replicated
- expand_weight_grad: float32 [1024, 4096], P('dp', 'tensor')
- expand_bias_grad: float32 [4096], P('tensor')
- reduce_weight_grad: float32 [1024, 4096], P('dp', 'tensor')
- reduce_bias_grad: float32 [1024], replicated
Inputs may be any that keep to these rules, and one draw needn't show every extreme that they name: `lengths`: in every draw some image has all 320 slots valid.
All inputs are finite; a program needn't handle non-finite values.
Results may differ from a plain program's by a relative error of at most 0.0095.
Values may be sent and summed in bfloat16 or wider, within the bound.
A program may use at most 320 MiB of HBM per device.

v0:
```python
from functools import partial
import math

import jax
import jax.numpy as jnp
from jax import lax
from jax.sharding import PartitionSpec as P

HD = 64
SLOTS = 320


EPSILON = 1e-05
MASKED_SCORE = -1e30


def layer_norm(rows, gain, shift):
    centre = jnp.mean(rows, axis=-1, keepdims=True)
    centred = rows - centre
    spread = jnp.mean(centred * centred, axis=-1, keepdims=True)
    return centred * lax.rsqrt(spread + EPSILON) * gain + shift


def gather_rows(values):
    return lax.all_gather(values, "tensor", axis=0, tiled=True)


def reduce_rows(values):
    return lax.psum_scatter(values, "tensor", scatter_dimension=0, tiled=True)


def fetch_mixing(query_key_value_weight, merge_weight):
    return (
        lax.all_gather(query_key_value_weight, "dp", axis=1, tiled=True),
        lax.all_gather(merge_weight, "dp", axis=0, tiled=True),
    )


def fetch_feed(expand_weight, reduce_weight):
    return (
        lax.all_gather(expand_weight, "dp", axis=0, tiled=True),
        lax.all_gather(reduce_weight, "dp", axis=0, tiled=True),
    )


def masked_scores(query_heads, key_heads, key_valid, scale):
    raw_scores = (
        jnp.einsum("bqhe,bkhe->bhqk", query_heads, key_heads, preferred_element_type=jnp.float32)
        * scale
    )
    return jnp.where(key_valid[:, None, None, :], raw_scores, MASKED_SCORE)


def body(
    inputs,
    teacher,
    lengths,
    first_gain,
    first_shift,
    query_key_value_weight,
    heads_bias,
    merge_weight,
    merge_bias,
    second_gain,
    second_shift,
    expand_weight,
    expand_bias,
    reduce_weight,
    reduce_bias,
):
    local_rows = inputs.shape[0]
    group_rows = local_rows * lax.axis_size("tensor")
    images = group_rows // SLOTS
    local_width = query_key_value_weight.shape[2]
    local_heads = local_width // HD
    scale = 1.0 / math.sqrt(HD)
    mine = lax.dynamic_slice_in_dim(lengths, lax.axis_index("dp") * images, images)
    key_valid = jnp.arange(SLOTS, dtype=jnp.int32)[None, :] < mine[:, None]
    row_valid = lax.dynamic_slice_in_dim(
        key_valid.reshape(group_rows), lax.axis_index("tensor") * local_rows, local_rows
    )
    row_valid = row_valid.astype(jnp.float32)[:, None]
    count = jnp.sum(lengths).astype(jnp.float32)
    inputs_f = inputs.astype(jnp.float32)
    normalized_rows, first_back = jax.vjp(layer_norm, inputs_f, first_gain, first_shift)
    normed_b = normalized_rows.astype(jnp.bfloat16)
    normalized_complete = gather_rows(normed_b)
    heads_complete_rows, merge_full = fetch_mixing(query_key_value_weight, merge_weight)
    projected_heads = jnp.einsum(
        "xz,ezi->exi", normalized_complete, heads_complete_rows, preferred_element_type=jnp.float32
    )
    queries = (projected_heads[0] + heads_bias[0]).astype(jnp.bfloat16)
    key_rows = projected_heads[1].astype(jnp.bfloat16)
    value_rows = (projected_heads[2] + heads_bias[1]).astype(jnp.bfloat16)
    query_heads = queries.reshape(images, SLOTS, local_heads, HD)
    key_heads = key_rows.reshape(images, SLOTS, local_heads, HD)
    value_heads = value_rows.reshape(images, SLOTS, local_heads, HD)
    scores = masked_scores(query_heads, key_heads, key_valid, scale)
    highest = jnp.max(scores, axis=-1, keepdims=True)
    expo = jnp.exp(scores - highest)
    totals = jnp.sum(expo, axis=-1, keepdims=True)
    attend = expo / totals
    log_total = highest + jnp.log(totals)
    mixed = jnp.einsum(
        "bhqk,bkhe->bqhe",
        attend.astype(jnp.bfloat16),
        value_heads,
        preferred_element_type=jnp.float32,
    )
    mixed_b = mixed.reshape(group_rows, local_width).astype(jnp.bfloat16)
    branch_part = jnp.einsum("rf,df->rd", mixed_b, merge_full, preferred_element_type=jnp.float32)
    hidden_state = inputs_f + reduce_rows(branch_part) + merge_bias
    second, second_back = jax.vjp(layer_norm, hidden_state, second_gain, second_shift)
    second_b = second.astype(jnp.bfloat16)
    second_full = gather_rows(second_b)
    expand_full, reduce_full = fetch_feed(expand_weight, reduce_weight)
    pre_act = jnp.dot(second_full, expand_full, preferred_element_type=jnp.float32) + expand_bias
    activ, gelu_back = jax.vjp(partial(jax.nn.gelu, approximate=True), pre_act)
    activ_b = activ.astype(jnp.bfloat16)
    feed_part = jnp.einsum("rf,df->rd", activ_b, reduce_full, preferred_element_type=jnp.float32)
    feed_sum = reduce_rows(feed_part)
    result = (hidden_state + feed_sum + reduce_bias) * row_valid
    error = (result - teacher.astype(jnp.float32)) * row_valid
    loss_part = jnp.sum(error * error)
    result_grad = 2.0 * error / count
    expand_back, reduce_back = fetch_feed(expand_weight, reduce_weight)
    second_src = gather_rows(second_b)
    result_full = gather_rows(result_grad.astype(jnp.bfloat16))
    activ_grad = jnp.dot(result_full, reduce_back, preferred_element_type=jnp.float32)
    reduce_grad = jnp.einsum("rd,rf->df", result_full, activ_b, preferred_element_type=jnp.float32)
    pre_grad = gelu_back(activ_grad)[0].astype(jnp.bfloat16)
    expand_bias_grad = jnp.sum(pre_grad, axis=0, dtype=jnp.float32)
    expand_grad = jnp.einsum("rd,rf->df", second_src, pre_grad, preferred_element_type=jnp.float32)
    second_grad = reduce_rows(
        jnp.einsum("rf,df->rd", pre_grad, expand_back, preferred_element_type=jnp.float32)
    )
    hidden_ln_grad, second_gain_grad, second_shift_grad = second_back(second_grad)
    hidden_grad = result_grad + hidden_ln_grad
    reduce_bias_grad = jnp.sum(result_grad, axis=0)
    merge_bias_grad = jnp.sum(hidden_grad, axis=0)
    heads_pullback_rows, merge_back = fetch_mixing(query_key_value_weight, merge_weight)
    normalized_input_rows = gather_rows(normed_b)
    hidden_full = gather_rows(hidden_grad.astype(jnp.bfloat16))
    mixed_grad = jnp.einsum(
        "rd,df->rf", hidden_full, merge_back, preferred_element_type=jnp.float32
    ).astype(jnp.bfloat16)
    merge_grad = jnp.einsum("rd,rf->df", hidden_full, mixed_b, preferred_element_type=jnp.float32)
    mixed_heads = mixed_grad.reshape(images, SLOTS, local_heads, HD)
    attend_again = jnp.exp(masked_scores(query_heads, key_heads, key_valid, scale) - log_total)
    value_grad = jnp.einsum(
        "bhqk,bqhe->bkhe",
        attend_again.astype(jnp.bfloat16),
        mixed_heads,
        preferred_element_type=jnp.float32,
    ).astype(jnp.bfloat16)
    attend_grad = jnp.einsum(
        "bqhe,bkhe->bhqk", mixed_heads, value_heads, preferred_element_type=jnp.float32
    )
    score_grad = attend_again * (
        attend_grad - jnp.sum(attend_again * attend_grad, axis=-1, keepdims=True)
    )
    score_grad = score_grad.astype(jnp.bfloat16)
    query_grad = (
        jnp.einsum("bhqk,bkhe->bqhe", score_grad, key_heads, preferred_element_type=jnp.float32)
        * scale
    ).astype(jnp.bfloat16)
    key_grad = (
        jnp.einsum("bhqk,bqhe->bkhe", score_grad, query_heads, preferred_element_type=jnp.float32)
        * scale
    ).astype(jnp.bfloat16)
    projected_heads_gradient = jnp.stack(
        [
            query_grad.reshape(group_rows, local_width),
            key_grad.reshape(group_rows, local_width),
            value_grad.reshape(group_rows, local_width),
        ]
    )
    heads_bias_grad = jnp.stack(
        [
            jnp.sum(projected_heads_gradient[0], axis=0, dtype=jnp.float32),
            jnp.sum(projected_heads_gradient[2], axis=0, dtype=jnp.float32),
        ]
    )
    heads_grad = jnp.einsum(
        "jb,mjx->mbx",
        normalized_input_rows,
        projected_heads_gradient,
        preferred_element_type=jnp.float32,
    )
    normed_grad = reduce_rows(
        jnp.einsum(
            "mex,mwx->ew",
            projected_heads_gradient,
            heads_pullback_rows,
            preferred_element_type=jnp.float32,
        )
    )
    inputs_ln_grad, first_gain_grad, first_shift_grad = first_back(normed_grad)
    inputs_grad = hidden_grad + inputs_ln_grad
    heads_grad, merge_grad = (
        lax.psum_scatter(
            heads_grad.astype(jnp.bfloat16), "dp", scatter_dimension=1, tiled=True
        ).astype(jnp.float32),
        lax.psum_scatter(
            merge_grad.astype(jnp.bfloat16), "dp", scatter_dimension=0, tiled=True
        ).astype(jnp.float32),
    )
    expand_grad, reduce_grad = (
        lax.psum_scatter(
            expand_grad.astype(jnp.bfloat16), "dp", scatter_dimension=0, tiled=True
        ).astype(jnp.float32),
        lax.psum_scatter(
            reduce_grad.astype(jnp.bfloat16), "dp", scatter_dimension=0, tiled=True
        ).astype(jnp.float32),
    )
    heads_bias_grad, expand_bias_grad = lax.psum((heads_bias_grad, expand_bias_grad), "dp")
    summed = lax.psum(
        (
            first_gain_grad,
            first_shift_grad,
            second_gain_grad,
            second_shift_grad,
            merge_bias_grad,
            reduce_bias_grad,
            loss_part,
        ),
        ("dp", "tensor"),
    )
    loss_value = summed[6] / count
    return (
        loss_value,
        result.astype(jnp.bfloat16),
        inputs_grad,
        summed[0],
        summed[1],
        heads_grad,
        heads_bias_grad,
        merge_grad,
        summed[4],
        summed[2],
        summed[3],
        expand_grad,
        expand_bias_grad,
        reduce_grad,
        summed[5],
    )


def solution(mesh):
    return jax.shard_map(
        body,
        mesh=mesh,
        in_specs=(
            P(("dp", "tensor"), None),
            P(("dp", "tensor"), None),
            P(),
            P(),
            P(),
            P(None, "dp", "tensor"),
            P(None, "tensor"),
            P("dp", "tensor"),
            P(),
            P(),
            P(),
            P("dp", "tensor"),
            P("tensor"),
            P("dp", "tensor"),
            P(),
        ),
        out_specs=(
            P(),
            P(("dp", "tensor"), None),
            P(("dp", "tensor"), None),
            P(),
            P(),
            P(None, "dp", "tensor"),
            P(None, "tensor"),
            P("dp", "tensor"),
            P(),
            P(),
            P(),
            P("dp", "tensor"),
            P("tensor"),
            P("dp", "tensor"),
            P(),
        ),
        check_vma=False,
    )
```

profile of v0, /device:TPU:0, one launch (start us, length us, event | category | flops | bytes accessed | tf_op | source)
XLA Modules:
  0.0 1575.8 jit_solution(5867062736825207133)
XLA Ops:
  17.6 69.5 %all-gather.9.cloned.1.call-done = bf16[2560,1024]{1,0:T(8,128)(2,1)} async-done(((bf16[1280,1024]{1,0:T(8,128)(2,1)}), bf16[2560,1024]{1,0:T(8,128)(2,1)}) %all-gather.9.cloned.1.call-update) | async-done | bytes 5242896 | tf_op jit(solution)/shard_map/all_gather | solution.py:25
  87.2 47.4 %all-gather.11.cloned.1.call-done = bf16[3,1024,512]{2,1,0:T(8,128)(2,1)} async-done(((bf16[3,64,512]{2,1,0:T(8,128)(2,1)}), bf16[3,1024,512]{2,1,0:T(8,128)(2,1)}) %all-gather.11.cloned.1.call-update) | async-done | bytes 3145744 | tf_op jit(solution)/shard_map/all_gather | solution.py:34
  134.6 11.3 convolution_bitcast_fusion
  145.9 5.5 copy-done.13
  153.2 9.3 fusion.60
  162.5 5.9 copy.67
  168.4 7.4 squeeze.7
  175.8 7.4 reshape.163
  183.2 6.9 copy.71
  190.1 5.9 copy.68
  196.0 7.3 squeeze.8
  203.4 4.5 add_convert_fusion.1
  212.2 16.7 %fusion.13 = (f32[8,8,320]{2,1,0:T(8,128)S(1)}, f32[8,8,320,320]{2,3,1,0:T(8,128)}) fusion(pred[8,320]{1,0:T(8,128)(4,1)S(1)} %iota_compare_fusion, bf16[8,320,8,64]{1,3,2,0:T(8,128)(2,1)S(1)} %copy-done.6, bf16[8,320,8,64]{1,0,3,2:T(8,128)(2,1)} %add_convert_fusion), kind=kOutput, calls=%fused_computation.22 | convolution fusion | flops 858501120 | bytes 31541760 | tf_op jit(solution)/shard_map/bqhe,bkhe->bhqk/dot_general | solution.py:48
  228.9 14.1 fusion
  243.0 16.4 %convert_bitcast_fusion.2 = bf16[8,320,8,64]{1,3,2,0:T(8,128)(2,1)} fusion(f32[8,8,320]{2,1,0:T(8,128)S(1)} %fusion, f32[8,8,320]{2,1,0:T(8,128)S(1)} %get-tuple-element.91, f32[8,8,320,320]{2,3,1,0:T(8,128)} %get-tuple-element.92, pred[8,320]{1,0:T(8,128)(4,1)S(1)} %iota_compare_fusion, bf16[8,320,8,64]{1,0,3,2:T(8,128)(2,1)} %add_convert_fusion.1), kind=kOutput, calls=%fused_computation.69 | convolution fusion | flops 872939520 | bytes 31623680 | tf_op jit(solution)/shard_map/bhqk,bkhe->bqhe/dot_general | solution.py:104
  259.5 5.6 copy.74
  265.0 5.9 convert_element_type.131
  270.9 8.8 fusion.61
  280.4 120.2 %reduce-scatter.8.cloned.1.call-done = f32[1280,1024]{1,0:T(8,128)} async-done(((f32[2560,1024]{1,0:T(8,128)}), f32[1280,1024]{1,0:T(8,128)}) %reduce-scatter.8.cloned.1.call-update) | async-done | bytes 5242896 | tf_op jit(solution)/shard_map/reduce_scatter | solution.py:29
  400.6 3.2 fusion.58
  409.3 43.9 %all-gather.17.cloned.1.call-done = bf16[1024,2048]{1,0:T(8,128)(2,1)} async-done(((bf16[64,2048]{1,0:T(8,128)(2,1)}), bf16[1024,2048]{1,0:T(8,128)(2,1)}) %all-gather.17.cloned.1.call-update) | async-done | bytes 4194320 | tf_op jit(solution)/shard_map/all_gather | solution.py:41
  453.2 69.1 %all-gather.15.cloned.1.call-done = bf16[2560,1024]{1,0:T(8,128)(2,1)} async-done(((bf16[1280,1024]{1,0:T(8,128)(2,1)}), bf16[2560,1024]{1,0:T(8,128)(2,1)}) %all-gather.15.cloned.1.call-update) | async-done | bytes 5242896 | tf_op jit(solution)/shard_map/all_gather | solution.py:25
  522.3 23.8 %multiply_convert_fusion.1 = (bf16[2560,2048]{1,0:T(8,128)(2,1)}, f32[2560,2048]{1,0:T(8,128)}) fusion(f32[2048]{0:T(1024)S(1)} %copy-done.43, bf16[2560,1024]{1,0:T(8,128)(2,1)} %all-gather.15.cloned.1.call-done, bf16[1024,2048]{1,0:T(8,128)(2,1)} %all-gather.17.cloned.1.call-done), kind=kOutput, calls=%fused_computation.18 | convolution fusion | flops 10789847040 | bytes 40902656 | tf_op jit(solution)/shard_map/dot_general | solution.py:117
  546.1 29.1 %all-gather.19.cloned.1.call-done = bf16[1024,2048]{1,0:T(8,128)(2,1)} async-done(((bf16[64,2048]{1,0:T(8,128)(2,1)}), bf16[1024,2048]{1,0:T(8,128)(2,1)}) %all-gather.19.cloned.1.call-update) | async-done | bytes 4194320 | tf_op jit(solution)/shard_map/all_gather | solution.py:42
  575.2 16.7 %fusion.62 = f32[2560,1024]{1,0:T(8,128)} fusion(bf16[2560,2048]{1,0:T(8,128)(2,1)} %get-tuple-element.93, bf16[1024,2048]{1,0:T(8,128)(2,1)} %all-gather.19.cloned.1.call-done), kind=kOutput, calls=%fused_computation.111 | convolution fusion | flops 10737418240 | bytes 25165824 | tf_op jit(solution)/shard_map/rf,df->rd/dot_general | solution.py:120
  594.0 118.4 %reduce-scatter.10.cloned.1.call-done = f32[1280,1024]{1,0:T(8,128)} async-done(((f32[2560,1024]{1,0:T(8,128)}), f32[1280,1024]{1,0:T(8,128)}) %reduce-scatter.10.cloned.1.call-update) | async-done | bytes 5242896 | tf_op jit(solution)/shard_map/reduce_scatter | solution.py:29
  712.4 6.3 fusion.54
  718.7 3.6 fusion.55
  726.7 68.7 %all-gather.21.cloned.1.call-done = bf16[2560,1024]{1,0:T(8,128)(2,1)} async-done(((bf16[1280,1024]{1,0:T(8,128)(2,1)}), bf16[2560,1024]{1,0:T(8,128)(2,1)}) %all-gather.21.cloned.1.call-update) | async-done | bytes 5242896 | tf_op jit(solution)/shard_map/all_gather | solution.py:25
  795.3 29.0 %convert_reduce_fusion = (f32[2048]{0:T(1024)}, bf16[2560,2048]{1,0:T(8,128)(2,1)S(1)}) fusion(f32[2560,2048]{1,0:T(8,128)} %get-tuple-element.94, f32[2048]{0:T(1024)S(1)} %copy-done.43, bf16[2560,1024]{1,0:T(8,128)(2,1)} %all-gather.21.cloned.1.call-done, bf16[1024,2048]{1,0:T(8,128)(2,1)} %all-gather.19.cloned.1.call-done), kind=kOutput, calls=%fused_computation.17 | convolution fusion | flops 10858002432 | bytes 40910848 | tf_op jit(solution)/shard_map/dot_general | solution.py:129
  824.3 3.8 copy-done.47
  828.2 14.5 fusion.63
  842.8 122.0 %reduce-scatter.12.cloned.1.call-done = f32[1280,1024]{1,0:T(8,128)} async-done(((f32[2560,1024]{1,0:T(8,128)}), f32[1280,1024]{1,0:T(8,128)}) %reduce-scatter.12.cloned.1.call-update) | async-done | bytes 5242896 | tf_op jit(solution)/shard_map/reduce_scatter | solution.py:29
  964.7 5.8 multiply_reduce_fusion.1
  970.5 3.9 fusion.57
  980.0 17.0 %convolution_convert_fusion.1 = bf16[1024,2048]{1,0:T(8,128)(2,1)} fusion(bf16[2560,1024]{1,0:T(8,128)(2,1)} %all-gather.21.cloned.1.call-done, bf16[2560,2048]{1,0:T(8,128)(2,1)} %get-tuple-element.93), kind=kOutput, calls=%fused_computation.63 | convolution fusion | flops 10739515392 | bytes 19922944 | tf_op jit(solution)/shard_map/rd,rf->df/dot_general | solution.py:130
  997.2 16.8 %convolution_convert_fusion.2 = bf16[1024,2048]{1,0:T(8,128)(2,1)} fusion(bf16[2560,1024]{1,0:T(8,128)(2,1)} %all-gather.15.cloned.1.call-done, bf16[2560,2048]{1,0:T(8,128)(2,1)} %copy-done.47), kind=kOutput, calls=%fused_computation.64 | convolution fusion | flops 10739515392 | bytes 19922944 | tf_op jit(solution)/shard_map/rd,rf->df/dot_general | solution.py:133
  1014.3 34.4 %all-gather.23.cloned.1.call-done = bf16[2560,1024]{1,0:T(8,128)(2,1)} async-done(((bf16[1280,1024]{1,0:T(8,128)(2,1)}), bf16[2560,1024]{1,0:T(8,128)(2,1)}) %all-gather.23.cloned.1.call-update) | async-done | bytes 5242896 | tf_op jit(solution)/shard_map/all_gather | solution.py:25
  1048.7 5.7 convolution_convert_fusion
  1054.3 4.5 reshape.164
  1058.9 7.2 copy.76
  1066.1 24.7 %multiply_reduce_fusion = (f32[8,8,320]{2,1,0:T(8,128)S(1)}, f32[8,8,320,320]{2,3,1,0:T(8,128)}) fusion(f32[8,8,320]{2,1,0:T(8,128)S(1)} %log_add_fusion, f32[8,8,320,320]{2,3,1,0:T(8,128)} %get-tuple-element.92, pred[8,320]{1,0:T(8,128)(4,1)S(1)} %iota_compare_fusion, bf16[8,320,8,64]{1,3,2,0:T(8,128)(2,1)} %copy.76, bf16[8,320,8,64]{1,0,3,2:T(8,128)(2,1)S(1)} %copy-done.11), kind=kOutput, calls=%fused_computation.1 | convolution fusion | flops 871608320 | bytes 57838080 | tf_op jit(solution)/shard_map/bqhe,bkhe->bhqk/dot_general | solution.py:156
  1090.9 26.7 %multiply_convert_fusion = bf16[8,8,320,320]{2,3,1,0:T(8,128)(2,1)} fusion(f32[8,8,320,320]{2,3,1,0:T(8,128)} %get-tuple-element.96, f32[8,8,320]{2,1,0:T(8,128)S(1)} %get-tuple-element.95, f32[8,8,320]{2,1,0:T(8,128)S(1)} %log_add_fusion, f32[8,8,320,320]{2,3,1,0:T(8,128)} %get-tuple-element.92, pred[8,320]{1,0:T(8,128)(4,1)S(1)} %iota_compare_fusion), kind=kLoop, calls=%fused_computation | loop fusion | flops 39321600 | bytes 65702400 | tf_op jit(solution)/shard_map/convert_element_type | solution.py:162
  1117.6 15.0 convert_reduce_fusion.2
  1132.6 6.9 copy.100
  1139.5 8.2 reshape.161
  1147.7 9.9 fusion.30
  1157.6 6.8 copy.99
  1164.4 8.0 reshape.160
  1172.4 10.3 convert_reduce_fusion.3
  1182.7 6.7 copy.98
  1189.5 8.0 reshape.159
  1200.2 3.2 copy-done.19
  1203.4 8.8 convert_bitcast_fusion
  1212.3 5.7 copy.91
  1218.2 7.3 convolution_convert_fusion.3
  1225.7 13.0 convolution_bitcast_fusion.1
  1244.4 61.5 %all-reduce.2 = (f32[2,512]{1,0:T(2,128)}, f32[2048]{0:T(1024)}) all-reduce(f32[2,512]{1,0:T(2,128)S(1)} %pad_maximum_fusion, f32[2048]{0:T(1024)S(1)} %copy-done.35), channel_id=1, replica_groups=mesh['dp'=16,'tensor'=2] {'dp'}, use_global_device_ids=true, to_apply=%region_25.26 | all-reduce | flops 3072 | bytes 24576 | tf_op jit(solution)/shard_map/psum | solution.py:216
  1305.9 24.2 %all-reduce.5.cloned.1.call-done = bf16[3,1024,512]{2,0,1:T(4,128)(2,1)} async-done(((bf16[3,1024,512]{2,0,1:T(4,128)(2,1)}), bf16[3,1024,512]{2,0,1:T(4,128)(2,1)}) %all-reduce.5.cloned.1.call-update) | async-done | bytes 3145744
  1332.0 58.4 %reduce-scatter.16.cloned.1.call-done = bf16[64,512]{1,0:T(8,128)(2,1)} async-done(((bf16[1024,512]{1,0:T(8,128)(2,1)}), bf16[64,512]{1,0:T(8,128)(2,1)}) %reduce-scatter.16.cloned.1.call-update) | async-done | bytes 65552 | tf_op jit(solution)/shard_map/reduce_scatter | solution.py:204
  1391.9 121.6 %reduce-scatter.14.cloned.1.call-done = f32[1280,1024]{1,0:T(8,128)} async-done(((f32[2560,1024]{1,0:T(8,128)}), f32[1280,1024]{1,0:T(8,128)}) %reduce-scatter.14.cloned.1.call-update) | async-done | bytes 5242896 | tf_op jit(solution)/shard_map/reduce_scatter | solution.py:29
  1513.5 3.8 fusion.53
  1520.6 40.2 %all-reduce.1 = (f32[]{:T(128)}, f32[1024]{0:T(1024)}, f32[1024]{0:T(1024)}, f32[1024]{0:T(1024)}, f32[1024]{0:T(1024)}, /*index=5*/f32[1024]{0:T(1024)}, f32[1024]{0:T(1024)}) all-reduce(f32[]{:T(128)} %get-tuple-element.90, f32[1024]{0:T(1024)S(1)} %get-tuple-element.62, ...), channel_id=1, replica_groups=mesh['dp'=16,'tensor'=2] {'dp','tensor'}, use_global_device_ids=true, to_apply=%region_9.10 | all-reduce | flops 6145 | bytes 49160 | tf_op jit(solution)/shard_map/psum | solution.py:217
  1561.4 6.5 add_add_fusion.2
  (178 shorter events, 48.7 us)
Async XLA Ops:
  7.2 6.2 copy-start.1
  7.2 6.2 copy-start.28
  7.2 6.2 copy-start.36
  7.2 80.0 %all-gather.9.cloned.1.call-start = ((), (), s32[]{:S(2)}) async-start(), calls=%async_computation.7 | async-start | bytes 7864320 | tf_op jit(solution)/shard_map/all_gather | solution.py:25
  9.6 3.2 copy-start.22
  9.6 7.7 copy-start.44
  9.6 7.9 copy-start.40
  15.8 118.8 %all-gather.11.cloned.1.call-start = ((), (), s32[]{:S(2)}) async-start(), calls=%async_computation.8 | async-start | bytes 3342336 | tf_op jit(solution)/shard_map/all_gather | solution.py:34
  16.5 254.4 %all-gather.13.cloned.1.call-start = ((), (), s32[]{:S(2)}) async-start(), calls=%async_computation.9 | async-start | bytes 1114112 | tf_op jit(solution)/shard_map/all_gather | solution.py:35
  17.2 383.4 %reduce-scatter.8.cloned.1.call-start = ((), (), s32[]{:S(2)}) async-start(), calls=%async_computation.10 | async-start | bytes 15728640 | tf_op jit(solution)/shard_map/reduce_scatter | solution.py:29
  145.9 5.5 copy-start.13
  203.4 5.8 copy-start.9
  209.1 3.0 copy-start.6
  228.9 14.1 copy-start.17
  243.0 16.5 %copy-start.20 = (f32[8,8,320]{2,1,0:T(8,128)}, f32[8,8,320]{2,1,0:T(8,128)S(1)}, u32[]{:S(2)}) copy-start(f32[8,8,320]{2,1,0:T(8,128)S(1)} %fusion) | copy-start | bytes 245764
  279.7 120.9 %copy-start.37 = (f32[1024]{0:T(1024)S(1)}, f32[1024]{0:T(1024)}, u32[]{:S(2)}) copy-start(f32[1024]{0:T(1024)} %param.23) | copy-start | bytes 12292
  279.8 173.5 %all-gather.17.cloned.1.call-start = ((), (), s32[]{:S(2)}) async-start(), calls=%async_computation.12 | async-start | bytes 4456448 | tf_op jit(solution)/shard_map/all_gather | solution.py:41
  280.4 241.9 %all-gather.15.cloned.1.call-start = ((), (), s32[]{:S(2)}) async-start(), calls=%async_computation.11 | async-start | bytes 7864320 | tf_op jit(solution)/shard_map/all_gather | solution.py:25
  403.9 2.4 copy-start
  403.9 2.4 copy-start.30
  403.9 2.3 copy-start.38
  406.2 116.1 %copy-start.43 = (f32[2048]{0:T(1024)S(1)}, f32[2048]{0:T(1024)}, u32[]{:S(2)}) copy-start(f32[2048]{0:T(1024)} %param.27) | copy-start | bytes 24580
  408.5 166.7 %all-gather.19.cloned.1.call-start = ((), (), s32[]{:S(2)}) async-start(), calls=%async_computation.13 | async-start | bytes 4456448 | tf_op jit(solution)/shard_map/all_gather | solution.py:42
  409.2 303.2 %reduce-scatter.10.cloned.1.call-start = ((), (), s32[]{:S(2)}) async-start(), calls=%async_computation.14 | async-start | bytes 15728640 | tf_op jit(solution)/shard_map/reduce_scatter | solution.py:29
  591.9 120.6 %copy-start.39 = (f32[1024]{0:T(1024)S(1)}, f32[1024]{0:T(1024)}, u32[]{:S(2)}) copy-start(f32[1024]{0:T(1024)} %param.29) | copy-start | bytes 12292
  591.9 203.4 %all-gather.21.cloned.1.call-start = ((), (), s32[]{:S(2)}) async-start(), calls=%async_computation.15 | async-start | bytes 7864320 | tf_op jit(solution)/shard_map/all_gather | solution.py:25
  594.0 124.8 %copy-start.16 = (bf16[1280,1024]{1,0:T(8,128)(2,1)S(1)}, bf16[1280,1024]{1,0:T(8,128)(2,1)}, u32[]{:S(2)}) copy-start(bf16[1280,1024]{1,0:T(8,128)(2,1)} %param.16) | copy-start | bytes 7864324
  722.3 2.4 copy-start.5
  726.6 238.1 %reduce-scatter.12.cloned.1.call-start = ((), (), s32[]{:S(2)}) async-start(), calls=%async_computation.16 | async-start | bytes 15728640 | tf_op jit(solution)/shard_map/reduce_scatter | solution.py:29
  795.3 32.8 %copy-start.41 = (bf16[1024,2048]{1,0:T(8,128)(2,1)S(1)}, bf16[1024,2048]{1,0:T(8,128)(2,1)}, u32[]{:S(2)}) copy-start(bf16[1024,2048]{1,0:T(8,128)(2,1)} %all-gather.17.cloned.1.call-done) | copy-start | bytes 12582916
  824.3 3.9 copy-start.47
  842.7 206.0 %all-gather.23.cloned.1.call-start = ((), (), s32[]{:S(2)}) async-start(), calls=%async_computation.17 | async-start | bytes 7864320 | tf_op jit(solution)/shard_map/all_gather | solution.py:25
  964.7 5.8 copy-start.10
  964.7 9.7 slice-start
  970.5 3.9 slice-start.1
  975.7 2.4 copy-start.3
  980.0 17.2 %copy-start.18 = (f32[8,8,320]{2,1,0:T(8,128)S(1)}, f32[8,8,320]{2,1,0:T(8,128)}, u32[]{:S(2)}) copy-start(f32[8,8,320]{2,1,0:T(8,128)} %copy-done.17) | copy-start | bytes 245764
  980.0 17.2 %copy-start.21 = (f32[8,8,320]{2,1,0:T(8,128)S(1)}, f32[8,8,320]{2,1,0:T(8,128)}, u32[]{:S(2)}) copy-start(f32[8,8,320]{2,1,0:T(8,128)} %copy-done.20) | copy-start | bytes 245764
  980.0 260.6 %reduce-scatter.20.cloned.1.call-start = ((), (), s32[]{:S(2)}) async-start(), calls=%async_computation.21 | async-start | bytes 4456448 | tf_op jit(solution)/shard_map/reduce_scatter | solution.py:212
  997.1 245.3 %reduce-scatter.18.cloned.1.call-start = ((), (), s32[]{:S(2)}) async-start(), calls=%async_computation.20 | async-start | bytes 4456448 | tf_op jit(solution)/shard_map/reduce_scatter | solution.py:209
  1014.1 316.1 %all-reduce.5.cloned.1.call-start = ((), (), s32[]{:S(2)}) async-start(), calls=%async_computation.22 | async-start | bytes 8388608
  1058.9 7.2 copy-start.11
  1090.9 26.7 %copy-start.12 = (bf16[8,320,8,64]{1,3,2,0:T(8,128)(2,1)S(1)}, bf16[8,320,8,64]{1,3,2,0:T(8,128)(2,1)}, u32[]{:S(2)}) copy-start(bf16[8,320,8,64]{1,3,2,0:T(8,128)(2,1)} %copy.76) | copy-start | bytes 7864324
  1139.5 8.2 copy-start.8
  1164.4 8.0 copy-start.7
  1189.5 10.1 copy-start.15
  1197.5 2.6 copy-start.14
  1197.5 5.9 slice-start.2
  1199.6 3.8 slice-start.3
  1200.2 3.2 copy-start.19
  1218.0 7.7 copy-start.42
  1218.0 172.4 %reduce-scatter.16.cloned.1.call-start = ((), (), s32[]{:S(2)}) async-start(), calls=%async_computation.19 | async-start | bytes 1114112 | tf_op jit(solution)/shard_map/reduce_scatter | solution.py:204
  1225.6 287.9 %reduce-scatter.14.cloned.1.call-start = ((), (), s32[]{:S(2)}) async-start(), calls=%async_computation.18 | async-start | bytes 15728640 | tf_op jit(solution)/shard_map/reduce_scatter | solution.py:29
  1238.7 5.7 copy-start.35
  1238.7 274.8 %copy-start.2 = (bf16[1280,1024]{1,0:T(8,128)(2,1)S(1)}, bf16[1280,1024]{1,0:T(8,128)(2,1)}, u32[]{:S(2)}) copy-start(bf16[1280,1024]{1,0:T(8,128)(2,1)} %param.15) | copy-start | bytes 7864324
  1238.7 274.8 %copy-start.23 = (f32[1280]{0:T(1024)S(1)}, f32[1280]{0:T(1024)}, u32[]{:S(2)}) copy-start(f32[1280]{0:T(1024)} %copy-done.22) | copy-start | bytes 15364
  1238.7 274.8 %copy-start.29 = (f32[1024]{0:T(1024)S(1)}, f32[1024]{0:T(1024)}, u32[]{:S(2)}) copy-start(f32[1024]{0:T(1024)} %param.18) | copy-start | bytes 12292
  1242.4 275.0 %copy-start.27 = (f32[1280]{0:T(1024)S(1)}, f32[1280]{0:T(1024)}, u32[]{:S(2)}) copy-start(f32[1280]{0:T(1024)} %copy-done.26) | copy-start | bytes 15364
  1242.4 275.0 %copy-start.25 = (f32[1280]{0:T(1024)S(1)}, f32[1280]{0:T(1024)}, u32[]{:S(2)}) copy-start(f32[1280]{0:T(1024)} %copy-done.24) | copy-start | bytes 15364
  1513.5 4.0 copy-start.4
  1517.3 3.2 copy-start.31
  1517.3 3.2 copy-start.32
  1517.3 3.2 copy-start.33
  1517.3 3.2 copy-start.34
  (4 other events, 2.5 us)
Sparse Core Ops, SparseCore 0:
  15.9 71.2 all-gather.8
  89.4 45.1 all-gather.10
  136.8 36.7 all-gather.12
  279.9 120.7 reduce-scatter.7
  402.7 50.5 all-gather.16
  455.2 67.0 all-gather.14
  524.5 50.7 all-gather.18
  592.0 120.3 reduce-scatter.9
  726.7 68.5 all-gather.20
  842.8 121.8 reduce-scatter.11
  980.1 68.5 all-gather.22
  1052.4 72.4 reduce-scatter.19
  1129.2 71.3 reduce-scatter.17
  1218.1 111.9 all-reduce.4
  1334.0 56.3 reduce-scatter.15
  1392.5 120.8 reduce-scatter.13
where the time goes:
time: 1590 us; the launch traced here: 1580 us
  waiting for transfers between devices  930 us (58%)
  matrix products  266 us (17%)
  local copies, waits for them, and re-layouts  154 us (10%)
  other arithmetic  105 us (7%)
  blocking collectives  102 us (6%)
  between operations  17.8 us (1%)
    reduce_scatter x4, waiting for transfers between devices, reduce_rows(): return lax.psum_scatter(values, 'tensor', scatter_dimension=0, tiled=True)  482 us
    all_gather x4, waiting for transfers between devices, gather_rows(): return lax.all_gather(values, 'tensor', axis=0, tiled=True)  242 us
    psum x1, blocking collectives, body(): lax.psum((heads_bias_grad, expand_bias_grad), 'dp')  61.5 us
    reduce_scatter x1, waiting for transfers between devices, body(): lax.psum_scatter(merge_grad.astype(jnp.bfloat16), 'dp', scatter_dimension...  58.4 us
    all_gather x1, waiting for transfers between devices, fetch_mixing(): lax.all_gather(query_key_value_weight, 'dp', axis=1, tiled=True)  47.4 us
    another operation x7, local copies, waits for them, and re-layouts, body(): jnp.stack([query_grad.reshape(group_rows, local_width), key_grad.reshape(...  44.8 us
    all_gather x1, waiting for transfers between devices, fetch_feed(): lax.all_gather(expand_weight, 'dp', axis=0, tiled=True)  43.9 us
    psum x1, blocking collectives, body(): lax.psum((first_gain_grad, first_shift_grad, second_gain_grad, second_shi...  40.2 us
  transfers between devices with their start and end apart: 16, of which 13 were waited for; matrix products, arithmetic and copies ran while one was open for 25% of the time, Pallas kernels for 0%

commit v1 on v0

v1 whole, which is shorter than its diff:
```python
from functools import partial

import jax
import jax.numpy as jnp
from jax import lax
from jax.experimental import pallas as pl
from jax.experimental.pallas import tpu as pltpu
from jax.sharding import PartitionSpec as P

HD = 64
SLOTS = 320
PAIR = 2 * HD

EPSILON = 1e-05
MASKED_SCORE = -1e30
F32 = jnp.float32
BF16 = jnp.bfloat16
EVERY = ("tensor", "dp")


def layer_norm(rows, gain, shift):
    centre = jnp.mean(rows, axis=-1, keepdims=True)
    centred = rows - centre
    spread = jnp.mean(centred * centred, axis=-1, keepdims=True)
    return centred * lax.rsqrt(spread + EPSILON) * gain + shift


def two_heads(pair):
    first = lax.broadcasted_iota(jnp.int32, pair.shape, 1) < HD
    zero = jnp.zeros_like(pair)
    return jnp.concatenate([jnp.where(first, pair, zero), jnp.where(first, zero, pair)], axis=0)


def one_pair(stacked):
    first = lax.broadcasted_iota(jnp.int32, (SLOTS, PAIR), 1) < HD
    return jnp.where(first, stacked[:SLOTS], stacked[SLOTS:])


def dot(left, right, left_dim, right_dim):
    return lax.dot_general(
        left, right, (((left_dim,), (right_dim,)), ((), ())), preferred_element_type=F32
    )


def masked_scores(query_stack, keys, length):
    scores = dot(keys, query_stack, 1, 1)
    slot = lax.broadcasted_iota(jnp.int32, scores.shape, 0)
    return jnp.where(slot < length, scores, MASKED_SCORE)


def attend_kernel(lengths_ref, qkv_ref, mixed_ref, log_ref):
    length = lengths_ref[pl.program_id(1)]
    query_stack = two_heads(qkv_ref[0] * 0.125)
    scores = masked_scores(query_stack, qkv_ref[1], length)
    highest = jnp.max(scores, axis=0, keepdims=True)
    expo = jnp.exp(scores - highest)
    totals = jnp.sum(expo, axis=0, keepdims=True)
    mixed = dot(qkv_ref[2], expo.astype(BF16), 0, 0) * (1.0 / totals)
    mixed_ref[...] = one_pair(mixed.T).astype(BF16)
    log_ref[0] = highest + jnp.log(totals)


def attend_back_kernel(lengths_ref, qkv_ref, mixed_grad_ref, log_ref, grad_ref, bias_ref):
    image = pl.program_id(1)
    length = lengths_ref[image]
    query_stack = two_heads(qkv_ref[0] * 0.125)
    keys = qkv_ref[1]
    scores = masked_scores(query_stack, keys, length)
    attend = jnp.exp(scores - log_ref[0])
    grad_stack = two_heads(mixed_grad_ref[...])
    attend_grad = dot(qkv_ref[2], grad_stack, 1, 1)
    value_grad = dot(attend.astype(BF16), grad_stack, 1, 0).astype(BF16)
    centre = jnp.sum(attend * attend_grad, axis=0, keepdims=True)
    score_grad = (attend * (attend_grad - centre)).astype(BF16)
    key_grad = dot(score_grad, query_stack, 1, 0).astype(BF16)
    query_grad = dot(keys, score_grad, 0, 0)
    query_grad = (one_pair(query_grad.T) * 0.125).astype(BF16)
    grad_ref[0] = query_grad
    grad_ref[1] = key_grad
    grad_ref[2] = value_grad

    @pl.when(image == 0)
    def _():
        bias_ref[...] = jnp.zeros_like(bias_ref)

    bias_ref[0, 0:1] += jnp.sum(query_grad.astype(F32), axis=0, keepdims=True)
    bias_ref[0, 1:2] += jnp.sum(value_grad.astype(F32), axis=0, keepdims=True)


def attend(lengths, qkv):
    rows, width = qkv.shape[1:]
    images, pairs = rows // SLOTS, width // PAIR
    return pl.pallas_call(
        attend_kernel,
        grid_spec=pltpu.PrefetchScalarGridSpec(
            num_scalar_prefetch=1,
            grid=(pairs, images),
            in_specs=[pl.BlockSpec((3, SLOTS, PAIR), lambda p, i, s: (0, i, p))],
            out_specs=[
                pl.BlockSpec((SLOTS, PAIR), lambda p, i, s: (i, p)),
                pl.BlockSpec((1, 1, 2 * SLOTS), lambda p, i, s: (p * images + i, 0, 0)),
            ],
        ),
        out_shape=[
            jax.ShapeDtypeStruct((rows, width), BF16),
            jax.ShapeDtypeStruct((pairs * images, 1, 2 * SLOTS), F32),
        ],
        compiler_params=pltpu.CompilerParams(vmem_limit_bytes=48 * 2**20),
        cost_estimate=pl.CostEstimate(
            flops=4 * rows * SLOTS * width * 4, bytes_accessed=8 * rows * width,
            transcendentals=rows * SLOTS * width // HD,
        ),
        name="attend",
    )(lengths, qkv)


def attend_back(lengths, qkv, mixed_grad, log_total):
    rows, width = qkv.shape[1:]
    images, pairs = rows // SLOTS, width // PAIR
    return pl.pallas_call(
        attend_back_kernel,
        grid_spec=pltpu.PrefetchScalarGridSpec(
            num_scalar_prefetch=1,
            grid=(pairs, images),
            in_specs=[
                pl.BlockSpec((3, SLOTS, PAIR), lambda p, i, s: (0, i, p)),
                pl.BlockSpec((SLOTS, PAIR), lambda p, i, s: (i, p)),
                pl.BlockSpec((1, 1, 2 * SLOTS), lambda p, i, s: (p * images + i, 0, 0)),
            ],
            out_specs=[
                pl.BlockSpec((3, SLOTS, PAIR), lambda p, i, s: (0, i, p)),
                pl.BlockSpec((1, 2, PAIR), lambda p, i, s: (p, 0, 0)),
            ],
        ),
        out_shape=[
            jax.ShapeDtypeStruct((3, rows, width), BF16),
            jax.ShapeDtypeStruct((pairs, 2, PAIR), F32),
        ],
        compiler_params=pltpu.CompilerParams(vmem_limit_bytes=48 * 2**20),
        cost_estimate=pl.CostEstimate(
            flops=10 * rows * SLOTS * width * 4, bytes_accessed=14 * rows * width,
            transcendentals=rows * SLOTS * width // HD,
        ),
        name="attend_back",
    )(lengths, qkv, mixed_grad, log_total)


def whole(weight, axis):
    full = lax.all_gather(weight, EVERY, axis=axis, tiled=True)
    halves = lax.axis_size("tensor")
    shape = full.shape
    return full.reshape(*shape[:axis], halves, shape[axis] // halves, *shape[axis + 1 :])


def scatter(grad, axis):
    shape = grad.shape
    flat = grad.reshape(*shape[:axis], shape[axis] * shape[axis + 1], *shape[axis + 2 :])
    return lax.psum_scatter(flat, EVERY, scatter_dimension=axis, tiled=True).astype(F32)


def body(
    inputs,
    teacher,
    lengths,
    first_gain,
    first_shift,
    query_key_value_weight,
    heads_bias,
    merge_weight,
    merge_bias,
    second_gain,
    second_shift,
    expand_weight,
    expand_bias,
    reduce_weight,
    reduce_bias,
):
    rows, width = inputs.shape
    images = rows // SLOTS
    halves = lax.axis_size("tensor")
    hidden = expand_weight.shape[1] * halves
    place = lax.axis_index("dp") * halves + lax.axis_index("tensor")
    mine = lax.dynamic_slice_in_dim(lengths, place * images, images)
    row_valid = (jnp.arange(SLOTS, dtype=jnp.int32)[None, :] < mine[:, None]).reshape(rows, 1)
    row_valid = row_valid.astype(F32)
    count = jnp.sum(lengths).astype(F32)

    heads_bias = lax.all_gather(heads_bias, "tensor", axis=1, tiled=True)
    expand_bias = lax.all_gather(expand_bias, "tensor", axis=0, tiled=True)
    qkv_full = whole(query_key_value_weight, 1)
    merge_full = whole(merge_weight, 0)
    expand_full = whole(expand_weight, 0)
    reduce_full = whole(reduce_weight, 0)

    inputs_f = inputs.astype(F32)
    normed, first_back = jax.vjp(layer_norm, inputs_f, first_gain, first_shift)
    normed = normed.astype(BF16)
    qkv_bias = jnp.stack([heads_bias[0], jnp.zeros_like(heads_bias[0]), heads_bias[1]])
    qkv = jnp.einsum("xz,ejzi->exji", normed, qkv_full, preferred_element_type=F32)
    qkv = (qkv.reshape(3, rows, width) + qkv_bias[:, None, :]).astype(BF16)
    mixed, log_total = attend(mine, qkv)
    branch = jnp.einsum(
        "rjf,jdf->rd", mixed.reshape(rows, halves, -1), merge_full, preferred_element_type=F32
    )
    hidden_state = inputs_f + branch + merge_bias
    second, second_back = jax.vjp(layer_norm, hidden_state, second_gain, second_shift)
    second = second.astype(BF16)
    pre_act = jnp.einsum("rd,jdf->rjf", second, expand_full, preferred_element_type=F32)
    pre_act = pre_act + expand_bias.reshape(halves, -1)
    activ, gelu_back = jax.vjp(partial(jax.nn.gelu, approximate=True), pre_act)
    activ = activ.astype(BF16)
    feed = jnp.einsum("rjf,jdf->rd", activ, reduce_full, preferred_element_type=F32)
    result = (hidden_state + feed + reduce_bias) * row_valid
    error = (result - teacher.astype(F32)) * row_valid
    loss_part = jnp.sum(error * error)
    result_grad = 2.0 * error / count

    result_grad_b = result_grad.astype(BF16)
    reduce_grad = scatter(
        jnp.einsum("rd,rjf->jdf", result_grad_b, activ, preferred_element_type=F32).astype(BF16), 0
    )
    activ_grad = jnp.einsum("rd,jdf->rjf", result_grad_b, reduce_full, preferred_element_type=F32)
    pre_grad = gelu_back(activ_grad)[0].astype(BF16)
    expand_bias_grad = jnp.sum(pre_grad, axis=0, dtype=F32).reshape(hidden)
    expand_grad = scatter(
        jnp.einsum("rd,rjf->jdf", second, pre_grad, preferred_element_type=F32).astype(BF16), 0
    )
    second_grad = jnp.einsum("rjf,jdf->rd", pre_grad, expand_full, preferred_element_type=F32)
    hidden_ln_grad, second_gain_grad, second_shift_grad = second_back(second_grad)
    hidden_grad = result_grad + hidden_ln_grad
    reduce_bias_grad = jnp.sum(result_grad, axis=0)
    merge_bias_grad = jnp.sum(hidden_grad, axis=0)
    hidden_grad_b = hidden_grad.astype(BF16)
    merge_grad = scatter(
        jnp.einsum(
            "rd,rjf->jdf", hidden_grad_b, mixed.reshape(rows, halves, -1), preferred_element_type=F32
        ).astype(BF16),
        0,
    )
    mixed_grad = jnp.einsum("rd,jdf->rjf", hidden_grad_b, merge_full, preferred_element_type=F32)
    mixed_grad = mixed_grad.astype(BF16).reshape(rows, width)
    qkv_grad, bias_grad = attend_back(mine, qkv, mixed_grad, log_total)
    heads_bias_grad = jnp.moveaxis(bias_grad, 1, 0).reshape(2, width)
    qkv_grad = qkv_grad.reshape(3, rows, halves, -1)
    heads_grad = scatter(
        jnp.einsum("rb,mrjx->mjbx", normed, qkv_grad, preferred_element_type=F32).astype(BF16), 1
    )
    normed_grad = jnp.einsum("mejx,mjwx->ew", qkv_grad, qkv_full, preferred_element_type=F32)
    inputs_ln_grad, first_gain_grad, first_shift_grad = first_back(normed_grad)
    inputs_grad = hidden_grad + inputs_ln_grad

    small = jnp.concatenate(
        [
            first_gain_grad,
            first_shift_grad,
            second_gain_grad,
            second_shift_grad,
            merge_bias_grad,
            reduce_bias_grad,
            heads_bias_grad.reshape(-1),
            expand_bias_grad,
            loss_part.reshape(1),
        ]
    )
    small = lax.psum(small, EVERY)
    vectors = small[: 6 * width].reshape(6, width)
    tensor = lax.axis_index("tensor")
    heads_bias_sum = lax.dynamic_slice_in_dim(
        small[6 * width : 8 * width].reshape(2, width), tensor * (width // halves), width // halves, 1
    )
    expand_bias_sum = lax.dynamic_slice_in_dim(
        small, 8 * width + tensor * (hidden // halves), hidden // halves
    )
    return (
        small[-1] / count,
        result.astype(BF16),
        inputs_grad,
        vectors[0],
        vectors[1],
        heads_grad,
        heads_bias_sum,
        merge_grad,
        vectors[4],
        vectors[2],
        vectors[3],
        expand_grad,
        expand_bias_sum,
        reduce_grad,
        vectors[5],
    )


def solution(mesh):
    return jax.shard_map(
        body,
        mesh=mesh,
        in_specs=(
            P(("dp", "tensor"), None),
            P(("dp", "tensor"), None),
            P(),
            P(),
            P(),
            P(None, "dp", "tensor"),
            P(None, "tensor"),
            P("dp", "tensor"),
            P(),
            P(),
            P(),
            P("dp", "tensor"),
            P("tensor"),
            P("dp", "tensor"),
            P(),
        ),
        out_specs=(
            P(),
            P(("dp", "tensor"), None),
            P(("dp", "tensor"), None),
            P(),
            P(),
            P(None, "dp", "tensor"),
            P(None, "tensor"),
            P("dp", "tensor"),
            P(),
            P(),
            P(),
            P("dp", "tensor"),
            P("tensor"),
            P("dp", "tensor"),
            P(),
        ),
        check_vma=False,
    )
```

time: 1590 us -> 1000 us (0.63)
  waiting for transfers between devices: 930 us -> 542 us
  local copies, waits for them, and re-layouts: 154 us -> 70.7 us
  Pallas kernels: 0 us -> 63.7 us
  matrix products: 266 us -> 205 us
  other arithmetic: 105 us -> 47.4 us
  blocking collectives: 102 us -> 50.8 us
    all_gather x8 -> x4, waiting for transfers between devices: 362 us -> 166 us  [whole(): full = lax.all_gather(weight, EVERY, axis=axis, tiled=True)]
    reduce_scatter x7 -> x4, waiting for transfers between devices: 541 us -> 374 us  [scatter(): lax.psum_scatter(flat, EVERY, scatter_dimension=axis, tiled=True)]
    pallas_call x0 -> x2, Pallas kernels: none -> 63.7 us  [the longest x1 34.6 us: attend_back(): pl.pallas_call(attend_back_kernel, grid_spec=pltpu.PrefetchScalarGridSpec...]
    dot_general x18 -> x12, matrix products: 266 us -> 205 us  [the longest x1 44.1 us: body(): jnp.einsum('rd,jdf->rjf', result_grad_b, reduce_full, preferred_element_t...]
    psum x2 -> x1, blocking collectives: 102 us -> 41.2 us  [body(): small = lax.psum(small, EVERY)]
    another operation x9 -> x1, local copies, waits for them, and re-layouts: 44.9 us -> 0.07 us  [body(): jnp.stack([heads_bias[0], jnp.zeros_like(heads_bias[0]), heads_bias[1]])]
    convert_element_type x13 -> x6, other arithmetic: 54 us -> 15.7 us  [the longest x1 8.82 us: body(): qkv = (qkv.reshape(3, rows, width) + qkv_bias[:, None, :]).astype(BF16)]
    unnamed x17 -> x8, waiting for transfers between devices: 27 us -> 2.65 us
  transfers between devices with their start and end apart: 16 -> 8, of which waited for: 13 -> 6; matrix products, arithmetic and copies ran while one was open for 25% -> 21% of each run, Pallas kernels for 0% -> 6%
where the time goes in v1:
time: 1000 us; the launch traced here: 998 us
  waiting for transfers between devices  542 us (54%)
  matrix products  205 us (20%)
  local copies, waits for them, and re-layouts  70.7 us (7%)
  Pallas kernels  63.7 us (6%)
  blocking collectives  50.8 us (5%)
  other arithmetic  47.4 us (5%)
  between operations  17.3 us (2%)
    reduce_scatter x4, waiting for transfers between devices, scatter(): lax.psum_scatter(flat, EVERY, scatter_dimension=axis, tiled=True)  374 us
    all_gather x4, waiting for transfers between devices, whole(): full = lax.all_gather(weight, EVERY, axis=axis, tiled=True)  166 us
    dot_general x1, matrix products, body(): jnp.einsum('rd,jdf->rjf', result_grad_b, reduce_full, preferred_element_t...  44.1 us
    psum x1, blocking collectives, body(): small = lax.psum(small, EVERY)  41.2 us
    pallas_call x1, Pallas kernels, attend_back(): pl.pallas_call(attend_back_kernel, grid_spec=pltpu.PrefetchScalarGridSpec...  34.6 us
    pallas_call x1, Pallas kernels, attend(): pl.pallas_call(attend_kernel, grid_spec=pltpu.PrefetchScalarGridSpec(num_...  29.1 us
    dot_general x1, matrix products, body(): jnp.einsum('rjf,jdf->rd', activ, reduce_full, preferred_element_type=F32)  24.1 us
    unnamed x79, local copies, waits for them, and re-layouts  22.4 us
  transfers between devices with their start and end apart: 8, of which 6 were waited for; matrix products, arithmetic and copies ran while one was open for 21% of the time, Pallas kernels for 6%

profile of v1, /device:TPU:0, one launch (start us, length us, event | category | flops | bytes accessed | tf_op | source)
XLA Modules:
  0.0 997.6 jit_solution(9000290426318545814)
XLA Ops:
  7.2 0.7 all-gather.5.cloned.1.call-update
  8.0 0.7 all-gather.7.cloned.1.call-update
  8.7 0.7 all-gather.9.cloned.1.call-update
  9.5 0.5 all-gather.11.cloned.1.call-update
  10.1 3.0 copy.80
  13.1 0.8 reduce_sum.155
  14.7 0.1 reshape.191
  14.8 4.4 copy.87
  19.2 5.3 all_gather.22
  24.5 4.3 all_gather.19
  28.9 0.4 convert_reduce_fusion.1
  29.3 0.7 fusion.23
  30.0 0.6 copy-done.14
  30.7 52.0 %all-gather.5.cloned.1.call-done = bf16[3,2048,512]{2,1,0:T(8,128)(2,1)} async-done(((bf16[3,64,512]{2,1,0:T(8,128)(2,1)}), bf16[3,2048,512]{2,1,0:T(8,128)(2,1)}) %all-gather.5.cloned.1.call-update) | async-done | bytes 6291472 | tf_op jit(solution)/shard_map/all_gather | solution.py:149
  82.7 14.4 %fusion.50 = f32[1280,3,2,512]{0,3,2,1:T(8,128)} fusion(bf16[3,2,1024,512]{3,2,1,0:T(8,128)(2,1)} %bitcast.111, bf16[1280,1024]{0,1:T(8,128)(2,1)S(1)} %copy.80, f32[1024]{0:T(1024)S(1)} %copy-done.26, f32[1024]{0:T(1024)S(1)} %copy-done.16, f32[1280]{0:T(1024)S(1)} %fusion.52, f32[1280]{0:T(1024)S(1)} %broadcast_multiply_fusion.1), kind=kOutput, calls=%fused_computation.67 | convolution fusion | flops 8060928000 | bytes 24659968 | tf_op jit(solution)/shard_map/xz,ejzi->exji/dot_general | solution.py:199
  97.1 15.6 %copy.118 = f32[3,1280,1024]{2,1,0:T(8,128)} copy(f32[3,1280,1024]{1,2,0:T(8,128)} %bitcast.96) | data formatting | bytes 31457280 | tf_op jit(solution)/shard_map/reshape | solution.py:200
  112.7 8.8 add_convert_fusion.qkv_ref
  121.6 29.1 %attend.1 = (bf16[1280,1024]{1,0:T(8,128)(2,1)S(1)}, f32[32,1,640]{2,1,0:T(1,128)S(1)}) custom-call(s32[4]{0:T(128)S(1)} %dynamic_slice.9.lengths_ref, bf16[3,1280,1024]{2,1,0:T(8,128)(2,1)} %add_convert_fusion.qkv_ref), custom_call_target="tpu_custom_call" | custom-call | flops 6710886400 | bytes 10485760 | tf_op jit(solution)/shard_map/attend/pallas_call | solution.py:93
  150.7 2.7 copy.126
  153.4 8.4 fusion.64
  161.9 3.1 multiply_reduce_fusion.3
  165.0 55.0 %all-gather.9.cloned.1.call-done = bf16[2048,2048]{1,0:T(8,128)(2,1)} async-done(((bf16[64,2048]{1,0:T(8,128)(2,1)}), bf16[2048,2048]{1,0:T(8,128)(2,1)}) %all-gather.9.cloned.1.call-update) | async-done | bytes 8388624 | tf_op jit(solution)/shard_map/all_gather | solution.py:149
  220.0 20.2 %fusion.57 = f32[1280,2,2048]{2,0,1:T(8,128)} fusion(bf16[2,1024,2048]{2,1,0:T(8,128)(2,1)} %bitcast.107, f32[1280,1024]{0,1:T(8,128)} %get-tuple-element.89, f32[1024]{0:T(1024)S(1)} %copy-done.28, f32[1024]{0:T(1024)S(1)} %copy-done.18, f32[1280]{0:T(1024)S(1)} %fusion.53, f32[1280]{0:T(1024)S(1)} %broadcast_multiply_fusion), kind=kOutput, calls=%fused_computation.92 | convolution fusion | flops 10743971840 | bytes 34621440 | tf_op jit(solution)/shard_map/rd,jdf->rjf/dot_general | solution.py:208
  240.2 58.6 %all-gather.11.cloned.1.call-done = bf16[2048,2048]{1,0:T(8,128)(2,1)} async-done(((bf16[64,2048]{1,0:T(8,128)(2,1)}), bf16[2048,2048]{1,0:T(8,128)(2,1)}) %all-gather.11.cloned.1.call-update) | async-done | bytes 8388624 | tf_op jit(solution)/shard_map/all_gather | solution.py:149
  298.8 24.1 %fusion.59 = (f32[1024]{0:T(1024)}, f32[1280,1024]{0,1:T(8,128)}, f32[]{:T(128)}, bf16[1280,1024]{0,1:T(8,128)(2,1)}) fusion(f32[]{:T(128)S(6)} %convert_element_type.94, f32[1280]{0:T(1024)S(1)} %reshape.191, bf16[1280,1024]{0,1:T(8,128)(2,1)S(1)} %copy-done.8, f32[1024]{0:T(1024)S(1)} %copy-done.25, f32[1280,1024]{0,1:T(8,128)} %get-tuple-element.89, ...), kind=kOutput, calls=%fused_computation.93 | convolution fusion | flops 10805574656 | bytes 45118472 | tf_op jit(solution)/shard_map/rjf,jdf->rd/dot_general | solution.py:212
  322.9 44.1 %convert_reduce_fusion = (f32[2,2048]{1,0:T(2,128)}, bf16[1280,2,2048]{2,0,1:T(8,128)(2,1)}) fusion(f32[1280,2,2048]{2,0,1:T(8,128)} %fusion.57, f32[2,2048]{1,0:T(2,128)S(1)} %add.126, bf16[2,1024,2048]{2,1,0:T(8,128)(2,1)} %bitcast.110, f32[1280,1024]{0,1:T(8,128)} %get-tuple-element.73), kind=kOutput, calls=%fused_computation.9 | convolution fusion | flops 10859311104 | bytes 45121536 | tf_op jit(solution)/shard_map/rd,jdf->rjf/dot_general | solution.py:222
  367.0 17.8 %fusion.66 = (f32[1024]{0:T(1024)}, f32[1280,1024]{1,0:T(8,128)}) fusion(bf16[1280,2,2048]{2,0,1:T(8,128)(2,1)} %get-tuple-element.96, bf16[2,1024,2048]{2,1,0:T(8,128)(2,1)} %bitcast.108), kind=kOutput, calls=%fused_computation.100 | convolution fusion | flops 10738727936 | bytes 24121344 | tf_op jit(solution)/shard_map/rjf,jdf->rd/dot_general | solution.py:228
  384.8 5.9 copy.89
  390.7 5.0 multiply_reduce_fusion.2
  395.7 0.5 copy-done.6
  396.3 4.4 multiply_reduce_fusion.1
  400.8 4.3 fusion.60
  405.0 2.3 copy-done.7
  407.4 3.1 convert_bitcast_fusion.1
  410.5 2.6 copy.104
  413.2 7.6 convolution_convert_fusion.2
  420.7 3.4 copy.123.mixed_grad_ref
  424.2 34.6 %attend_back.1 = (bf16[3,1280,1024]{2,1,0:T(8,128)(2,1)}, f32[8,2,128]{2,1,0:T(2,128)S(1)}) custom-call(s32[4]{0:T(128)S(1)} %copy-done.1, bf16[3,1280,1024]{2,1,0:T(8,128)(2,1)} %add_convert_fusion.qkv_ref, bf16[1280,1024]{1,0:T(8,128)(2,1)S(1)} %copy.123.mixed_grad_ref, f32[32,1,640]{2,1,0:T(1,128)S(1)} %get-tuple-element.20.log_ref), custom_call_target="tpu_custom_call" | custom-call | flops 16777216000 | bytes 18350080 | tf_op jit(solution)/shard_map/attend_back/pallas_call | solution.py:120
  458.9 14.8 %convert_bitcast_fusion = bf16[3,2,1024,512]{2,3,1,0:T(8,128)(2,1)} fusion(bf16[3,160,2,8,512]{4,3,2,1,0:T(8,128)(2,1)} %bitcast.115, bf16[1280,1024]{0,1:T(8,128)(2,1)S(1)} %copy-done.3, f32[1024]{0:T(1024)S(1)} %copy-done.27, f32[1024]{0:T(1024)S(1)} %copy-done.17, f32[1280]{0:T(1024)S(1)} %copy-done.13, f32[1280]{0:T(1024)S(1)} %copy-done.11), kind=kOutput, calls=%fused_computation.28 | convolution fusion | flops 8064073728 | bytes 16795648 | tf_op jit(solution)/shard_map/rb,mrjx->mjbx/dot_general | solution.py:246
  473.6 8.8 copy.101
  482.5 0.6 copy-done.29
  483.1 17.7 %convolution_convert_fusion.1 = bf16[2,2048,1024]{1,2,0:T(8,128)(2,1)} fusion(bf16[1280,2,2048]{2,0,1:T(8,128)(2,1)} %get-tuple-element.96, f32[1280,1024]{0,1:T(8,128)} %get-tuple-element.89, f32[1024]{0:T(1024)S(1)} %copy-done.29, f32[1024]{0:T(1024)S(1)} %copy-done.18, f32[1280]{0:T(1024)S(1)} %fusion.53, f32[1280]{0:T(1024)S(1)} %broadcast_multiply_fusion), kind=kOutput, calls=%fused_computation.32 | convolution fusion | flops 10748166144 | bytes 24135680 | tf_op jit(solution)/shard_map/rd,rjf->jdf/dot_general | solution.py:226
  500.8 19.2 %convolution_convert_fusion = bf16[2,2048,1024]{1,2,0:T(8,128)(2,1)} fusion(f32[1280,1024]{0,1:T(8,128)} %get-tuple-element.73, f32[1280,2,2048]{2,0,1:T(8,128)} %fusion.57, f32[2,2048]{1,0:T(2,128)S(1)} %add.126), kind=kOutput, calls=%fused_computation.31 | convolution fusion | flops 10795352064 | bytes 34619392 | tf_op jit(solution)/shard_map/rd,rjf->jdf/dot_general | solution.py:220
  520.1 14.0 %fusion.65 = (f32[1024]{0:T(1024)S(1)}, f32[1280,1024]{1,0:T(8,128)}) fusion(bf16[3,2,1024,512]{3,2,1,0:T(8,128)(2,1)} %bitcast.112, bf16[3,160,2,8,512]{4,3,2,1,0:T(8,128)(2,1)} %bitcast.116), kind=kOutput, calls=%fused_computation.99 | convolution fusion | flops 8054373376 | bytes 19402752 | tf_op jit(solution)/shard_map/mejx,mjwx->ew/dot_general | solution.py:248
  534.1 6.0 copy.95
  540.2 3.6 fusion.24
  543.8 0.4 copy-done.5
  544.3 2.6 fusion.48
  547.0 0.6 constant_dynamic-update-slice_fusion
  547.6 41.2 %psum.7 = f32[12289]{0:T(1024)S(1)} all-reduce(f32[12289]{0:T(1024)S(1)} %constant_dynamic-update-slice_fusion), channel_id=1, replica_groups=mesh['dp'=16,'tensor'=2] {'tensor','dp'}, use_global_device_ids=true, to_apply=%region_15.0 | all-reduce | flops 12289 | bytes 98312 | tf_op jit(solution)/shard_map/psum | solution.py:265
  588.8 0.5 slice.55
  590.0 4.4 copy.105
  594.4 6.8 add_add_fusion.2
  601.2 5.9 copy.106
  607.1 0.7 fusion.62
  607.7 0.6 constant_dynamic-slice_fusion
  608.3 0.6 fusion.61
  609.0 1.5 convert_element_type.106
  610.5 82.0 %reduce-scatter.5.cloned.1.call-done = bf16[3,64,512]{2,1,0:T(8,128)(2,1)} async-done(((bf16[3,2048,512]{2,1,0:T(8,128)(2,1)}), bf16[3,64,512]{2,1,0:T(8,128)(2,1)}) %reduce-scatter.5.cloned.1.call-update) | async-done | bytes 196624 | tf_op jit(solution)/shard_map/reduce_scatter | solution.py:158
  692.4 1.7 convert_element_type.103
  694.1 145.7 %reduce-scatter.9.cloned.1.call-done = bf16[64,2048]{1,0:T(8,128)(2,1)} async-done(((bf16[2048,2048]{1,0:T(8,128)(2,1)}), bf16[64,2048]{1,0:T(8,128)(2,1)}) %reduce-scatter.9.cloned.1.call-update) | async-done | bytes 262160 | tf_op jit(solution)/shard_map/reduce_scatter | solution.py:158
  839.9 1.8 convert_element_type.109
  841.7 146.0 %reduce-scatter.11.cloned.1.call-done = bf16[64,2048]{1,0:T(8,128)(2,1)} async-done(((bf16[2048,2048]{1,0:T(8,128)(2,1)}), bf16[64,2048]{1,0:T(8,128)(2,1)}) %reduce-scatter.11.cloned.1.call-update) | async-done | bytes 262160 | tf_op jit(solution)/shard_map/reduce_scatter | solution.py:158
  987.7 1.8 convert_element_type.112
  (100 shorter events, 0.9 us)
Async XLA Ops:
  7.2 5.9 copy-start.30
  7.2 75.5 %all-gather.5.cloned.1.call-start = ((), (), s32[]{:S(2)}) async-start(), calls=%async_computation.4 | async-start | bytes 6488064 | tf_op jit(solution)/shard_map/all_gather | solution.py:149
  7.9 145.5 %all-gather.7.cloned.1.call-start = ((), (), s32[]{:S(2)}) async-start(), calls=%async_computation.5 | async-start | bytes 2162688 | tf_op jit(solution)/shard_map/all_gather | solution.py:149
  8.7 211.3 %all-gather.9.cloned.1.call-start = ((), (), s32[]{:S(2)}) async-start(), calls=%async_computation.6 | async-start | bytes 8650752 | tf_op jit(solution)/shard_map/all_gather | solution.py:149
  9.4 289.4 %all-gather.11.cloned.1.call-start = ((), (), s32[]{:S(2)}) async-start(), calls=%async_computation.7 | async-start | bytes 8650752 | tf_op jit(solution)/shard_map/all_gather | solution.py:149
  10.0 599.0 %reduce-scatter.7.cloned.1.call-start = ((), (), s32[]{:S(2)}) async-start(), calls=%async_computation.9 | async-start | bytes 2162688 | tf_op jit(solution)/shard_map/reduce_scatter | solution.py:158
  10.0 9.1 copy-start.20
  10.0 14.5 %copy-start.21 = (f32[2,512]{1,0:T(2,128)S(1)}, f32[2,512]{1,0:T(2,128)}, u32[]{:S(2)}) copy-start(f32[2,512]{1,0:T(2,128)} %param.21) | copy-start | bytes 12292
  13.1 69.7 %copy-start.2 = (bf16[1280,1024]{0,1:T(8,128)(2,1)}, bf16[1280,1024]{0,1:T(8,128)(2,1)S(1)}, u32[]{:S(2)}) copy-start(bf16[1280,1024]{0,1:T(8,128)(2,1)S(1)} %copy.80) | copy-start | bytes 7864324
  13.9 107.6 %copy-start = (s32[4]{0:T(128)}, s32[4]{0:T(128)S(1)}, u32[]{:S(2)}) copy-start(s32[4]{0:T(128)S(1)} %dynamic_slice.9.lengths_ref) | copy-start | bytes 52
  14.8 68.0 %copy-start.16 = (f32[1024]{0:T(1024)S(1)}, f32[1024]{0:T(1024)}, u32[]{:S(2)}) copy-start(f32[1024]{0:T(1024)} %param.18) | copy-start | bytes 12292
  14.8 68.0 %copy-start.26 = (f32[1024]{0:T(1024)S(1)}, f32[1024]{0:T(1024)}, u32[]{:S(2)}) copy-start(f32[1024]{0:T(1024)} %param.19) | copy-start | bytes 12292
  29.3 67.8 %copy-start.10 = (f32[1280]{0:T(1024)}, f32[1280]{0:T(1024)S(1)}, u32[]{:S(2)}) copy-start(f32[1280]{0:T(1024)S(1)} %broadcast_multiply_fusion.1) | copy-start | bytes 15364
  30.0 0.6 copy-start.14
  30.6 66.5 %copy-start.12 = (f32[1280]{0:T(1024)}, f32[1280]{0:T(1024)S(1)}, u32[]{:S(2)}) copy-start(f32[1280]{0:T(1024)S(1)} %fusion.52) | copy-start | bytes 15364
  150.7 2.8 copy-start.24
  161.9 58.1 %copy-start.18 = (f32[1024]{0:T(1024)S(1)}, f32[1024]{0:T(1024)}, u32[]{:S(2)}) copy-start(f32[1024]{0:T(1024)} %param.24) | copy-start | bytes 12292
  161.9 58.1 %copy-start.28 = (f32[1024]{0:T(1024)S(1)}, f32[1024]{0:T(1024)}, u32[]{:S(2)}) copy-start(f32[1024]{0:T(1024)} %param.25) | copy-start | bytes 12292
  220.0 78.8 %copy-start.8 = (bf16[1280,1024]{0,1:T(8,128)(2,1)S(1)}, bf16[1280,1024]{0,1:T(8,128)(2,1)}, u32[]{:S(2)}) copy-start(bf16[1280,1024]{0,1:T(8,128)(2,1)} %copy.87) | copy-start | bytes 7864324
  220.0 78.8 %copy-start.25 = (f32[1024]{0:T(1024)S(1)}, f32[1024]{0:T(1024)}, u32[]{:S(2)}) copy-start(f32[1024]{0:T(1024)} %param.29) | copy-start | bytes 12292
  390.7 5.5 copy-start.6
  390.7 10.0 %slice-start = ((s8[5242880]{0:T(1024)(128)(4,1)}), s8[4194304]{0:T(1024)(128)(4,1)S(1)}, s32[]{:S(2)}) async-start(s8[5242880]{0:T(1024)(128)(4,1)} %bitcast.100), calls=%async_computation.12 | async-start | bytes 8388608
  396.3 4.5 slice-start.1
  400.7 6.6 copy-start.9
  405.0 2.4 copy-start.7
  413.1 279.3 %reduce-scatter.5.cloned.1.call-start = ((), (), s32[]{:S(2)}) async-start(), calls=%async_computation.8 | async-start | bytes 6488064 | tf_op jit(solution)/shard_map/reduce_scatter | solution.py:158
  420.7 3.4 copy-start.1
  424.1 34.7 %copy-start.3 = (bf16[1280,1024]{0,1:T(8,128)(2,1)S(1)}, bf16[1280,1024]{0,1:T(8,128)(2,1)}, u32[]{:S(2)}) copy-start(bf16[1280,1024]{0,1:T(8,128)(2,1)} %copy-done.2) | copy-start | bytes 7864324
  424.1 34.7 %copy-start.11 = (f32[1280]{0:T(1024)S(1)}, f32[1280]{0:T(1024)}, u32[]{:S(2)}) copy-start(f32[1280]{0:T(1024)} %copy-done.10) | copy-start | bytes 15364
  424.2 34.7 %copy-start.13 = (f32[1280]{0:T(1024)S(1)}, f32[1280]{0:T(1024)}, u32[]{:S(2)}) copy-start(f32[1280]{0:T(1024)} %copy-done.12) | copy-start | bytes 15364
  424.2 34.7 %copy-start.17 = (f32[1024]{0:T(1024)S(1)}, f32[1024]{0:T(1024)}, u32[]{:S(2)}) copy-start(f32[1024]{0:T(1024)} %param.18) | copy-start | bytes 12292
  424.2 34.7 %copy-start.27 = (f32[1024]{0:T(1024)S(1)}, f32[1024]{0:T(1024)}, u32[]{:S(2)}) copy-start(f32[1024]{0:T(1024)} %param.19) | copy-start | bytes 12292
  482.4 0.7 copy-start.29
  482.4 357.4 %reduce-scatter.9.cloned.1.call-start = ((), (), s32[]{:S(2)}) async-start(), calls=%async_computation.10 | async-start | bytes 8650752 | tf_op jit(solution)/shard_map/reduce_scatter | solution.py:158
  500.8 486.9 %reduce-scatter.11.cloned.1.call-start = ((), (), s32[]{:S(2)}) async-start(), calls=%async_computation.11 | async-start | bytes 8650752 | tf_op jit(solution)/shard_map/reduce_scatter | solution.py:158
  534.1 6.1 copy-start.19
  534.1 6.1 copy-start.4
  540.2 3.6 copy-start.15
  540.2 4.1 copy-start.5
  543.8 3.1 copy-start.23
  543.8 3.1 copy-start.22
Sparse Core Ops, SparseCore 0:
  10.9 71.7 all-gather.4
  85.6 55.4 all-gather.6
  143.9 76.0 all-gather.8
  222.7 76.0 all-gather.10
  413.2 135.1 reduce-scatter.6
  550.7 141.6 reduce-scatter.4
  694.8 145.0 reduce-scatter.8
  842.3 145.3 reduce-scatter.10

commit v2 on v1

--- a/solution.py
+++ b/solution.py
@@ -1,4 +1,5 @@
 from functools import partial
+import math
 
 import jax
 import jax.numpy as jnp
@@ -16,6 +17,8 @@
 F32 = jnp.float32
 BF16 = jnp.bfloat16
 EVERY = ("tensor", "dp")
+CORES = 2
+LINE = 4
 
 
 def layer_norm(rows, gain, shift):
@@ -145,17 +148,357 @@
     )(lengths, qkv, mixed_grad, log_total)
 
 
-def whole(weight, axis):
-    full = lax.all_gather(weight, EVERY, axis=axis, tiled=True)
-    halves = lax.axis_size("tensor")
-    shape = full.shape
-    return full.reshape(*shape[:axis], halves, shape[axis] // halves, *shape[axis + 1 :])
-
-
-def scatter(grad, axis):
-    shape = grad.shape
-    flat = grad.reshape(*shape[:axis], shape[axis] * shape[axis + 1], *shape[axis + 2 :])
-    return lax.psum_scatter(flat, EVERY, scatter_dimension=axis, tiled=True).astype(F32)
+AXES = ("tensor", "line", "row", "core")
+MESH = pl.DeviceIdType.MESH
+GATHER_ORDERS = (
+    (("line", "tensor", "row"), ("line", "row", "tensor")),
+    (("tensor", "row", "line"), ("row", "tensor", "line")),
+)
+
+
+def sizes():
+    return {"tensor": lax.axis_size("tensor"), "line": LINE, "row": lax.axis_size("dp") // (LINE * CORES), "core": CORES}
+
+
+class Place:
+    def __init__(self):
+        self.size = sizes()
+        index = lax.axis_index("dp")
+        self.at = {
+            "tensor": lax.axis_index("tensor"),
+            "core": lax.rem(index, CORES),
+            "row": lax.rem(lax.div(index, CORES), self.size["row"]),
+            "line": lax.div(index, CORES * self.size["row"]),
+        }
+
+    def steps(self, axis):
+        return range(1, self.size[axis])
+
+    def peer(self, axis, step):
+        return lax.rem(self.at[axis] + step, self.size[axis])
+
+    def device(self, axis, place):
+        at = {**self.at, axis: place}
+        return {"dp": (at["line"] * self.size["row"] + at["row"]) * CORES + at["core"], "tensor": at["tensor"]}
+
+    def greet(self):
+        barrier = pltpu.get_barrier_semaphore()
+        count = 0
+        for axis in AXES:
+            for step in self.steps(axis):
+                pl.semaphore_signal(barrier, inc=1, device_id=self.device(axis, self.peer(axis, step)), device_id_type=MESH)
+                count += 1
+        pl.semaphore_wait(barrier, count)
+
+
+def pieces_of(shards, width):
+    out = []
+    for a, shard in enumerate(shards):
+        for lead in range(shard.shape[0]) if len(shard.shape) == 3 else (None,):
+            for col in range(shard.shape[-1] // width):
+                out.append((a, lead, col))
+    return out
+
+
+def piece(refs, which, width):
+    a, lead, col = which
+    ref = refs[a] if lead is None else refs[a].at[lead]
+    spare = (slice(None),) * (len(ref.shape) - 1)
+    return ref.at[(*spare, pl.ds(col * width, width))]
+
+
+def gather_kernel(pieces, width, orders, lag, n_weights, n_biases, *refs):
+    n_in = n_weights + n_biases
+    ins, outs = refs[:n_in], refs[n_in : 2 * n_in]
+    send_sem, recv_sem, own_sem, bias_send, bias_recv, bias_own = refs[2 * n_in :]
+    here = Place()
+    here.greet()
+    half = ins[0].shape[-2] // 2
+    count = len(pieces)
+
+    def region(n, h, stage, axis=None, place=None):
+        order = (*orders[n][h], "core")
+        index = [
+            slice(None) if a in order[:stage] else place if a == axis else here.at[a] for a in AXES
+        ]
+        return piece(outs, pieces[n], width).at[(*index, pl.ds(h * half, half))]
+
+    def remote(n, h, stage, step, coming=False):
+        axis = (*orders[n][h], "core")[stage]
+        slot = (n, h, stage, step - 1)
+        to = region(n, h, stage)
+        source = piece(ins, pieces[n], width).at[pl.ds(h * half, half)] if stage == 0 else to
+        if coming:
+            to = region(n, h, stage, axis, here.peer(axis, here.size[axis] - step))
+        return pltpu.make_async_remote_copy(
+            src_ref=source, dst_ref=to, send_sem=send_sem.at[slot], recv_sem=recv_sem.at[slot],
+            device_id=here.device(axis, here.peer(axis, step)), device_id_type=MESH,
+        )
+
+    def every(n, stage, act):
+        for h in range(2):
+            for step in here.steps((*orders[n][h], "core")[stage]):
+                act(n, h, stage, step)
+
+    def own(n):
+        place = tuple(here.at[a] for a in AXES)
+        return pltpu.make_async_copy(
+            piece(ins, pieces[n], width), piece(outs, pieces[n], width).at[place], own_sem.at[n]
+        )
+
+    def bias(b, step, coming=False):
+        ref, out = ins[n_weights + b], outs[n_weights + b]
+        place = here.peer("tensor", here.size["tensor"] - step) if coming else here.at["tensor"]
+        return pltpu.make_async_remote_copy(
+            src_ref=ref, dst_ref=out.at[place], send_sem=bias_send.at[b, step - 1],
+            recv_sem=bias_recv.at[b, step - 1],
+            device_id=here.device("tensor", here.peer("tensor", step)), device_id_type=MESH,
+        )
+
+    def own_bias(b):
+        return pltpu.make_async_copy(
+            ins[n_weights + b], outs[n_weights + b].at[here.at["tensor"]], bias_own.at[b]
+        )
+
+    start = lambda *k: remote(*k).start()
+    arrived = lambda *k: remote(*k, coming=True).wait_recv()
+    sent = lambda *k: remote(*k).wait_send()
+    for n in range(count):
+        every(n, 0, start)
+        own(n).start()
+    for b in range(n_biases):
+        own_bias(b).start()
+        for step in here.steps("tensor"):
+            bias(b, step).start()
+    for tick in range(count + 3 * lag):
+        for stage in range(1, 4):
+            n = tick - lag * (stage - 1)
+            if 0 <= n < count:
+                if stage == 1:
+                    own(n).wait()
+                every(n, stage - 1, arrived)
+                every(n, stage, start)
+    for n in range(count):
+        every(n, 3, arrived)
+        for stage in range(4):
+            every(n, stage, sent)
+    for b in range(n_biases):
+        own_bias(b).wait()
+        for step in here.steps("tensor"):
+            bias(b, step, coming=True).wait_recv()
+            bias(b, step).wait_send()
+
+
+def gather(weights, biases, collective_id, width, third=(), lag=2):
+    size = sizes()
+    lead = tuple(size[a] for a in AXES)
+    outs = [jax.ShapeDtypeStruct((*w.shape[:-2], *lead, *w.shape[-2:]), w.dtype) for w in weights]
+    outs += [jax.ShapeDtypeStruct((size["tensor"], *b.shape), b.dtype) for b in biases]
+    pieces = pieces_of(weights, width)
+    count, most, total = len(pieces), max(size.values()) - 1, len(weights) + len(biases)
+    orders = [GATHER_ORDERS[n in third] for n in range(count)]
+    few = max(len(biases), 1)
+    return pl.pallas_call(
+        partial(gather_kernel, pieces, width, orders, lag, len(weights), len(biases)),
+        out_shape=outs,
+        in_specs=[pl.BlockSpec(memory_space=pl.ANY)] * total,
+        out_specs=[pl.BlockSpec(memory_space=pl.ANY)] * total,
+        scratch_shapes=[
+            pltpu.SemaphoreType.DMA((count, 2, 4, most)),
+            pltpu.SemaphoreType.DMA((count, 2, 4, most)),
+            pltpu.SemaphoreType.DMA((count,)),
+            pltpu.SemaphoreType.DMA((few, size["tensor"])),
+            pltpu.SemaphoreType.DMA((few, size["tensor"])),
+            pltpu.SemaphoreType.DMA((few,)),
+        ],
+        compiler_params=pltpu.CompilerParams(collective_id=collective_id, has_side_effects=True),
+        name="gather",
+    )(*weights, *biases)
+
+
+SCATTER_ORDERS = (
+    (("tensor", "row", "line"), ("row", "tensor", "line")),
+    (("line", "tensor", "row"), ("line", "row", "tensor")),
+)
+SUM_AXES = ("core", "tensor", "row", "line")
+
+
+def scatter_kernel(pieces, width, orders, lag, n_grads, *refs):
+    ins, small = refs[:n_grads], refs[n_grads]
+    outs, small_out = refs[n_grads + 1 : 2 * n_grads + 1], refs[2 * n_grads + 1]
+    own_buf, first_buf, *rest = refs[2 * n_grads + 2 :]
+    count = len(pieces)
+    late = {(n, h, s): rest[(n * 2 + h) * 3 + s - 1] for n in range(count) for h in range(2) for s in (1, 2, 3)}
+    small_bufs = rest[6 * count : 6 * count + 4]
+    send_sem, recv_sem, own_sem, small_send, small_recv = rest[6 * count + 4 :]
+    here = Place()
+    here.greet()
+    half = own_buf.shape[-2] // 2
+    three = AXES[:3]
+
+    def own(n):
+        source = piece(ins, pieces[n], width).at[:, :, :, here.at["core"]]
+        return pltpu.make_async_copy(source, own_buf.at[n], own_sem.at[n])
+
+    def to_core(n):
+        other = here.peer("core", 1)
+        return pltpu.make_async_remote_copy(
+            src_ref=piece(ins, pieces[n], width).at[:, :, :, other], dst_ref=first_buf.at[n],
+            send_sem=send_sem.at[n, 0, 0, 0], recv_sem=recv_sem.at[n, 0, 0, 0],
+            device_id=here.device("core", other), device_id_type=MESH,
+        )
+
+    def remote(n, h, stage, step):
+        order = orders[n][h]
+        axis = order[stage - 1]
+        to = here.peer(axis, step)
+        index = [
+            here.at[a] if a in order[: stage - 1] else to if a == axis else slice(None) for a in three
+        ]
+        slot = (n, h, stage, step - 1)
+        return pltpu.make_async_remote_copy(
+            src_ref=own_buf.at[(n, *index, pl.ds(h * half, half))],
+            dst_ref=late[n, h, stage].at[step - 1],
+            send_sem=send_sem.at[slot], recv_sem=recv_sem.at[slot],
+            device_id=here.device(axis, to), device_id_type=MESH,
+        )
+
+    def every(n, stage, act):
+        for h in range(2):
+            for step in here.steps(orders[n][h][stage - 1]):
+                act(remote(n, h, stage, step))
+
+    def add_core(n):
+        def one(i, _):
+            first, left = lax.div(i, here.size["row"]), lax.rem(i, here.size["row"])
+            at = (n, lax.div(first, LINE), lax.rem(first, LINE), left)
+            own_buf[at] = (own_buf[at].astype(F32) + first_buf[at].astype(F32)).astype(BF16)
+            return 0
+
+        lax.fori_loop(0, math.prod(here.size[a] for a in three), one, 0)
+
+    def add(n, h, stage):
+        order = orders[n][h]
+        buf, steps = late[n, h, stage], here.size[order[stage - 1]] - 1
+        free = [a for a in three if a not in order[:stage]]
+        rows = pl.ds(h * half, half)
+
+        def one(i, _):
+            at, left = dict(here.at), i
+            for a in reversed(free):
+                at[a] = lax.rem(left, here.size[a])
+                left = lax.div(left, here.size[a])
+            mine = (n, *(at[a] for a in three), rows)
+            total = own_buf[mine].astype(F32)
+            for s in range(steps):
+                total += buf[(s, *(at[a] for a in free))].astype(F32)
+            if stage == 3:
+                out = piece(outs, pieces[n], width)
+                out[rows, :] = total
+            else:
+                own_buf[mine] = total.astype(BF16)
+            return 0
+
+        if free:
+            lax.fori_loop(0, math.prod(here.size[a] for a in free), one, 0)
+        else:
+            one(0, 0)
+
+    def small_copy(stage, step, coming=False):
+        axis = SUM_AXES[stage]
+        place = here.peer(axis, here.size[axis] - step) if coming else here.at[axis]
+        buf = small_bufs[stage]
+        return pltpu.make_async_remote_copy(
+            src_ref=buf.at[here.at[axis]], dst_ref=buf.at[place],
+            send_sem=small_send.at[stage, step - 1], recv_sem=small_recv.at[stage, step - 1],
+            device_id=here.device(axis, here.peer(axis, step)), device_id_type=MESH,
+        )
+
+    def small_start(stage, value):
+        axis = SUM_AXES[stage]
+        small_bufs[stage][here.at[axis]] = value
+        for step in here.steps(axis):
+            small_copy(stage, step).start()
+
+    def small_end(stage):
+        axis = SUM_AXES[stage]
+        for step in here.steps(axis):
+            small_copy(stage, step, coming=True).wait_recv()
+            small_copy(stage, step).wait_send()
+        total = small_bufs[stage][0]
+        for place in range(1, here.size[axis]):
+            total += small_bufs[stage][place]
+        return total
+
+    for n in range(count):
+        to_core(n).start()
+        own(n).start()
+    small_start(0, small[...])
+    for tick in range(max(count + 3 * lag, 5)):
+        if 1 <= tick <= 4:
+            total = small_end(tick - 1)
+            if tick < 4:
+                small_start(tick, total)
+            else:
+                small_out[...] = total
+        for stage in range(4):
+            n = tick - lag * stage
+            if not 0 <= n < count:
+                continue
+            if stage == 0:
+                own(n).wait()
+                to_core(n).wait_recv()
+                add_core(n)
+            else:
+                every(n, stage, lambda copy: copy.wait_recv())
+                for h in range(2):
+                    add(n, h, stage)
+            if stage < 3:
+                every(n, stage + 1, lambda copy: copy.start())
+    for n in range(count):
+        to_core(n).wait_send()
+        for stage in (1, 2, 3):
+            every(n, stage, lambda copy: copy.wait_send())
+
+
+def scatter(grads, small, collective_id, width, third=(), lag=2):
+    size = sizes()
+    shards = [jax.ShapeDtypeStruct((*g.shape[:-6], *g.shape[-2:]), F32) for g in grads]
+    pieces = pieces_of(shards, width)
+    count, most = len(pieces), max(size.values()) - 1
+    orders = [SCATTER_ORDERS[n in third] for n in range(count)]
+    rows = grads[0].shape[-2]
+    three = AXES[:3]
+    whole = (count, *(size[a] for a in three), rows, width)
+    late = []
+    for n in range(count):
+        for h in range(2):
+            for s in (1, 2, 3):
+                order = orders[n][h]
+                free = [size[a] for a in three if a not in order[:s]]
+                late.append(pltpu.VMEM((size[order[s - 1]] - 1, *free, rows // 2, width), BF16))
+    vmem = pl.BlockSpec(memory_space=pltpu.VMEM)
+    return pl.pallas_call(
+        partial(scatter_kernel, pieces, width, orders, lag, len(grads)),
+        out_shape=[*shards, jax.ShapeDtypeStruct(small.shape, small.dtype)],
+        in_specs=[*[pl.BlockSpec(memory_space=pl.ANY)] * len(grads), vmem],
+        out_specs=[vmem] * (len(grads) + 1),
+        scratch_shapes=[
+            pltpu.VMEM(whole, BF16),
+            pltpu.VMEM(whole, BF16),
+            *late,
+            *[pltpu.VMEM((size[a], *small.shape), F32) for a in SUM_AXES],
+            pltpu.SemaphoreType.DMA((count, 2, 4, most)),
+            pltpu.SemaphoreType.DMA((count, 2, 4, most)),
+            pltpu.SemaphoreType.DMA((count,)),
+            pltpu.SemaphoreType.DMA((4, most)),
+            pltpu.SemaphoreType.DMA((4, most)),
+        ],
+        compiler_params=pltpu.CompilerParams(
+            collective_id=collective_id, has_side_effects=True, vmem_limit_bytes=60 * 2**20
+        ),
+        name="scatter",
+    )(*grads, small)
 
 
 def body(
@@ -185,12 +528,16 @@
     row_valid = row_valid.astype(F32)
     count = jnp.sum(lengths).astype(F32)
 
-    heads_bias = lax.all_gather(heads_bias, "tensor", axis=1, tiled=True)
-    expand_bias = lax.all_gather(expand_bias, "tensor", axis=0, tiled=True)
-    qkv_full = whole(query_key_value_weight, 1)
-    merge_full = whole(merge_weight, 0)
-    expand_full = whole(expand_weight, 0)
-    reduce_full = whole(reduce_weight, 0)
+    weights = [query_key_value_weight, merge_weight, expand_weight]
+    piece_width = query_key_value_weight.shape[-1]
+    qkv_full, merge_full, expand_full, heads_bias, expand_bias = gather(
+        weights, [heads_bias, expand_bias.reshape(1, -1)], 0, piece_width, (4,), 1
+    )
+    qkv_full = qkv_full.reshape(3, halves, width, -1)
+    merge_full = merge_full.reshape(halves, width, -1)
+    expand_full = expand_full.reshape(halves, width, -1)
+    heads_bias = jnp.moveaxis(heads_bias, 0, 1).reshape(2, width)
+    reduce_full = lax.all_gather(reduce_weight, EVERY, axis=0, tiled=True).reshape(halves, width, -1)
 
     inputs_f = inputs.astype(F32)
     normed, first_back = jax.vjp(layer_norm, inputs_f, first_gain, first_shift)
@@ -216,35 +563,29 @@
     result_grad = 2.0 * error / count
 
     result_grad_b = result_grad.astype(BF16)
-    reduce_grad = scatter(
-        jnp.einsum("rd,rjf->jdf", result_grad_b, activ, preferred_element_type=F32).astype(BF16), 0
-    )
+    reduce_grad = jnp.einsum("rd,rjf->jdf", result_grad_b, activ, preferred_element_type=F32)
+    reduce_grad = lax.psum_scatter(
+        reduce_grad.astype(BF16).reshape(halves * width, -1), EVERY, scatter_dimension=0, tiled=True
+    ).astype(F32)
     activ_grad = jnp.einsum("rd,jdf->rjf", result_grad_b, reduce_full, preferred_element_type=F32)
     pre_grad = gelu_back(activ_grad)[0].astype(BF16)
     expand_bias_grad = jnp.sum(pre_grad, axis=0, dtype=F32).reshape(hidden)
-    expand_grad = scatter(
-        jnp.einsum("rd,rjf->jdf", second, pre_grad, preferred_element_type=F32).astype(BF16), 0
-    )
+    expand_grad = jnp.einsum("rd,rjf->jdf", second, pre_grad, preferred_element_type=F32).astype(BF16)
     second_grad = jnp.einsum("rjf,jdf->rd", pre_grad, expand_full, preferred_element_type=F32)
     hidden_ln_grad, second_gain_grad, second_shift_grad = second_back(second_grad)
     hidden_grad = result_grad + hidden_ln_grad
     reduce_bias_grad = jnp.sum(result_grad, axis=0)
     merge_bias_grad = jnp.sum(hidden_grad, axis=0)
     hidden_grad_b = hidden_grad.astype(BF16)
-    merge_grad = scatter(
-        jnp.einsum(
-            "rd,rjf->jdf", hidden_grad_b, mixed.reshape(rows, halves, -1), preferred_element_type=F32
-        ).astype(BF16),
-        0,
-    )
+    merge_grad = jnp.einsum(
+        "rd,rjf->jdf", hidden_grad_b, mixed.reshape(rows, halves, -1), preferred_element_type=F32
+    ).astype(BF16)
     mixed_grad = jnp.einsum("rd,jdf->rjf", hidden_grad_b, merge_full, preferred_element_type=F32)
     mixed_grad = mixed_grad.astype(BF16).reshape(rows, width)
     qkv_grad, bias_grad = attend_back(mine, qkv, mixed_grad, log_total)
     heads_bias_grad = jnp.moveaxis(bias_grad, 1, 0).reshape(2, width)
     qkv_grad = qkv_grad.reshape(3, rows, halves, -1)
-    heads_grad = scatter(
-        jnp.einsum("rb,mrjx->mjbx", normed, qkv_grad, preferred_element_type=F32).astype(BF16), 1
-    )
+    heads_grad = jnp.einsum("rb,mrjx->mjbx", normed, qkv_grad, preferred_element_type=F32).astype(BF16)
     normed_grad = jnp.einsum("mejx,mjwx->ew", qkv_grad, qkv_full, preferred_element_type=F32)
     inputs_ln_grad, first_gain_grad, first_shift_grad = first_back(normed_grad)
     inputs_grad = hidden_grad + inputs_ln_grad
@@ -262,7 +603,19 @@
             loss_part.reshape(1),
         ]
     )
-    small = lax.psum(small, EVERY)
+    length = small.shape[0]
+    small = jnp.pad(small, (0, -length % 1024)).reshape(-1, 128)
+    size = sizes()
+    places = tuple(size[a] for a in AXES)
+    heads_grad, merge_grad, expand_grad, small = scatter(
+        [
+            heads_grad.reshape(3, *places, -1, piece_width),
+            merge_grad.reshape(*places, -1, piece_width),
+            expand_grad.reshape(*places, -1, hidden // halves),
+        ],
+        small, 1, piece_width, (), 1,
+    )
+    small = small.reshape(-1)
     vectors = small[: 6 * width].reshape(6, width)
     tensor = lax.axis_index("tensor")
     heads_bias_sum = lax.dynamic_slice_in_dim(
@@ -272,7 +625,7 @@
         small, 8 * width + tensor * (hidden // halves), hidden // halves
     )
     return (
-        small[-1] / count,
+        small[length - 1] / count,
         result.astype(BF16),
         inputs_grad,
         vectors[0],

time: 1000 us -> 624 us (0.62)
  waiting for transfers between devices: 542 us -> 0.7 us
  Pallas kernels: 63.7 us -> 285 us
  blocking collectives: 50.8 us -> 0 us
    reduce_scatter x4 -> x1, waiting for transfers between devices: 374 us -> 0.01 us  [body(): lax.psum_scatter(reduce_grad.astype(BF16).reshape(halves * width, -1), EV...]
    pallas_call x0 -> x2, Pallas kernels: none -> 221 us  [the longest x1 125 us: gather(): pl.pallas_call(partial(gather_kernel, pieces, width, orders, lag, len(wei...]
    all_gather x4 -> x1, waiting for transfers between devices: 166 us -> 0.01 us  [body(): lax.all_gather(reduce_weight, EVERY, axis=0, tiled=True)]
    psum x1 -> x0, blocking collectives: 41.2 us -> none  [body(): small = lax.psum(small, EVERY)]
    unnamed x79 -> x101, local copies, waits for them, and re-layouts: 22.4 us -> 28.2 us
  transfers between devices with their start and end apart: 8 -> 2, of which waited for: 6 -> 0; matrix products, arithmetic and copies ran while one was open for 21% -> 35% of each run, Pallas kernels for 6% -> 46%
where the time goes in v2:
time: 624 us; the launch traced here: 618 us
  Pallas kernels  285 us (46%)
  matrix products  197 us (32%)
  local copies, waits for them, and re-layouts  80.5 us (13%)
  other arithmetic  38.2 us (6%)
  between operations  17.3 us (3%)
    pallas_call x1, Pallas kernels, gather(): pl.pallas_call(partial(gather_kernel, pieces, width, orders, lag, len(wei...  125 us
    pallas_call x1, Pallas kernels, scatter(): pl.pallas_call(partial(scatter_kernel, pieces, width, orders, lag, len(gr...  96.2 us
    dot_general x1, matrix products, body(): jnp.einsum('rd,jdf->rjf', result_grad_b, reduce_full, preferred_element_t...  43.6 us
    pallas_call x1, Pallas kernels, attend_back(): pl.pallas_call(attend_back_kernel, grid_spec=pltpu.PrefetchScalarGridSpec...  34.6 us
    pallas_call x1, Pallas kernels, attend(): pl.pallas_call(attend_kernel, grid_spec=pltpu.PrefetchScalarGridSpec(num_...  29.1 us
    unnamed x101, local copies, waits for them, and re-layouts  28.2 us
    dot_general x1, matrix products, body(): jnp.einsum('rjf,jdf->rd', activ, reduce_full, preferred_element_type=F32)  24.1 us
    dot_general x1, matrix products, body(): jnp.einsum('rd,rjf->jdf', result_grad_b, activ, preferred_element_type=F32)  19.1 us
  transfers between devices with their start and end apart: 2, of which 0 were waited for; matrix products, arithmetic and copies ran while one was open for 35% of the time, Pallas kernels for 46%

profile of v2, /device:TPU:0, one launch (start us, length us, event | category | flops | bytes accessed | tf_op | source)
XLA Modules:
  0.0 618.4 jit_solution(3706232649946603486)
XLA Ops:
  7.2 0.0 all-gather.2.cloned.1.call-start
  7.2 0.7 all-gather.2.cloned.1.call-update
  7.9 0.0 reduce-scatter.2.cloned.1.call-start
  8.0 1.3 reduce_sum.155
  9.9 0.7 dynamic_slice.9.lengths_ref
  10.7 0.1 fusion.54
  10.7 0.1 reshape.210
  10.8 3.0 copy.56
  13.8 5.0 copy.63
  18.8 124.7 %gather.1 = (bf16[3,2,4,2,2,64,512]{6,5,4,3,2,1,0:T(8,128)(2,1)}, bf16[2,4,2,2,64,512]{5,4,3,2,1,0:T(8,128)(2,1)}, bf16[2,4,2,2,64,2048]{5,4,3,2,1,0:T(8,128)(2,1)}, f32[2,2,512]{2,1,0:T(2,128)}, f32[2,1,2048]{2,1,0:T(1,128)}) custom-call(bf16[3,64,512]{2,1,0:T(8,128)(2,1)} %refs_0_.1, bf16[64,512]{1,0:T(8,128)(2,1)} %refs_1_.1, bf16[64,2048]{1,0:T(8,128)(2,1)} %refs_2_.1, ...), custom_call_target="tpu_custom_call" | custom-call | tf_op jit(solution)/shard_map/gather/pallas_call | solution.py:301
  143.5 0.7 copy.129
  144.2 0.4 convert_reduce_fusion.1
  144.7 0.7 fusion.23
  145.4 0.6 copy-done.18
  146.0 14.1 %fusion.50 = f32[3,2,512,1280]{3,2,1,0:T(8,128)} fusion(bf16[3,2,1024,512]{3,2,1,0:T(8,128)(2,1)} %bitcast.146, bf16[1280,1024]{0,1:T(8,128)(2,1)S(1)} %copy.56, f32[1024]{0:T(1024)S(1)} %copy-done.32, f32[1024]{0:T(1024)S(1)} %copy-done.24, f32[1280]{0:T(1024)S(1)} %fusion.52, f32[1280]{0:T(1024)S(1)} %broadcast_multiply_fusion.1), kind=kOutput, calls=%fused_computation.67 | convolution fusion | flops 8060928000 | bytes 24659968 | tf_op jit(solution)/shard_map/xz,ejzi->exji/dot_general | solution.py:546
  160.2 15.6 %copy.94 = f32[3,1280,1024]{2,1,0:T(8,128)} copy(f32[3,1280,1024]{1,2,0:T(8,128)} %bitcast.122) | data formatting | bytes 31457280 | tf_op jit(solution)/shard_map/reshape | solution.py:547
  175.8 0.1 pad.6.clone
  175.9 0.1 pad_maximum_fusion
  176.0 8.8 %add_convert_fusion.qkv_ref = bf16[3,1280,1024]{2,1,0:T(8,128)(2,1)} fusion(f32[3,1280,1024]{2,1,0:T(8,128)} %copy.94, f32[3,1024]{1,0:T(4,128)S(1)} %pad_maximum_fusion), kind=kLoop, calls=%fused_computation.11 | loop fusion | flops 7864320 | bytes 23605248 | tf_op jit(solution)/shard_map/convert_element_type | solution.py:547
  184.8 29.1 %attend.1 = (bf16[1280,1024]{1,0:T(8,128)(2,1)S(1)}, f32[32,1,640]{2,1,0:T(1,128)S(1)}) custom-call(s32[4]{0:T(128)S(1)} %dynamic_slice.9.lengths_ref, bf16[3,1280,1024]{2,1,0:T(8,128)(2,1)} %add_convert_fusion.qkv_ref), custom_call_target="tpu_custom_call" | custom-call | flops 6710886400 | bytes 10485760 | tf_op jit(solution)/shard_map/attend/pallas_call | solution.py:96
  213.9 3.0 copy.103
  216.9 6.2 %fusion.62 = (f32[1280]{0:T(1024)S(1)}, f32[1280,1024]{0,1:T(8,128)S(1)}) fusion(f32[1024]{0:T(1024)S(1)} %copy-done.30, bf16[2,1024,512]{2,1,0:T(8,128)(2,1)} %bitcast.148, bf16[1280,2,512]{0,2,1:T(8,128)(2,1)} %bitcast.126, bf16[1280,1024]{0,1:T(8,128)(2,1)} %copy-done.2), kind=kOutput, calls=%fused_computation.104 | convolution fusion | flops 2689596160 | bytes 12592128 | tf_op jit(solution)/shard_map/rjf,jdf->rd/dot_general | solution.py:549
  223.2 0.6 multiply_reduce_fusion.3
  223.8 0.6 copy-done.20
  224.4 1.1 copy-done.5
  225.5 15.1 %fusion.57 = f32[1280,2,2048]{2,0,1:T(8,128)} fusion(bf16[2,1024,2048]{2,1,0:T(8,128)(2,1)S(1)} %bitcast.145, f32[1280,1024]{0,1:T(8,128)S(1)} %get-tuple-element.90, f32[1024]{0:T(1024)S(1)} %copy-done.34, f32[1024]{0:T(1024)S(1)} %copy-done.26, f32[1280]{0:T(1024)S(1)} %fusion.53, f32[1280]{0:T(1024)S(1)} %broadcast_multiply_fusion), kind=kOutput, calls=%fused_computation.100 | convolution fusion | flops 10743971840 | bytes 34621440 | tf_op jit(solution)/shard_map/rd,jdf->rjf/dot_general | solution.py:555
  240.7 24.1 %fusion.59 = (f32[1024]{0:T(1024)}, f32[1280,1024]{0,1:T(8,128)}, f32[]{:T(128)}, bf16[1280,1024]{0,1:T(8,128)(2,1)}) fusion(f32[]{:T(128)S(6)} %convert_element_type.87, f32[1280]{0:T(1024)S(1)} %reshape.210, bf16[1280,1024]{0,1:T(8,128)(2,1)S(1)} %copy-done.10, f32[1024]{0:T(1024)S(1)} %copy-done.31, f32[1280,1024]{0,1:T(8,128)} %copy-done.5, ...), kind=kOutput, calls=%fused_computation.101 | convolution fusion | flops 10805574656 | bytes 45118472 | tf_op jit(solution)/shard_map/rjf,jdf->rd/dot_general | solution.py:559
  264.8 43.6 %convert_reduce_fusion = (f32[2,2048]{1,0:T(2,128)S(1)}, bf16[1280,2,2048]{2,0,1:T(8,128)(2,1)}) fusion(f32[1280,2,2048]{2,0,1:T(8,128)} %fusion.57, f32[2,2048]{1,0:T(2,128)S(1)} %bitcast.133, bf16[2,1024,2048]{2,1,0:T(8,128)(2,1)} %bitcast.141, f32[1280,1024]{0,1:T(8,128)} %get-tuple-element.76), kind=kOutput, calls=%fused_computation.9 | convolution fusion | flops 10859311104 | bytes 45121536 | tf_op jit(solution)/shard_map/rd,jdf->rjf/dot_general | solution.py:570
  308.3 19.1 %convolution_convert_fusion = bf16[2,2048,1024]{1,2,0:T(8,128)(2,1)} fusion(f32[1280,1024]{0,1:T(8,128)} %get-tuple-element.76, f32[1280,2,2048]{2,0,1:T(8,128)} %fusion.57, f32[2,2048]{1,0:T(2,128)S(1)} %bitcast.134), kind=kOutput, calls=%fused_computation.31 | convolution fusion | flops 10795352064 | bytes 34619392 | tf_op jit(solution)/shard_map/rd,rjf->jdf/dot_general | solution.py:566
  327.4 17.4 %fusion.64 = (f32[1024]{0:T(1024)S(1)}, f32[1280,1024]{1,0:T(8,128)}) fusion(bf16[1280,2,2048]{2,0,1:T(8,128)(2,1)} %get-tuple-element.97, bf16[2,1024,2048]{2,1,0:T(8,128)(2,1)} %bitcast.142), kind=kOutput, calls=%fused_computation.106 | convolution fusion | flops 10738727936 | bytes 24121344 | tf_op jit(solution)/shard_map/rjf,jdf->rd/dot_general | solution.py:574
  344.9 2.6 copy.81
  347.5 5.9 copy.65
  353.5 5.1 multiply_reduce_fusion.2
  358.6 0.6 copy-done.7
  359.2 5.1 multiply_reduce_fusion.1
  364.3 4.4 fusion.60
  368.7 2.3 copy-done.8
  371.1 3.1 convert_bitcast_fusion.1
  374.2 2.6 copy.74
  376.8 7.6 %convolution_convert_fusion.2 = bf16[1280,2,512]{0,2,1:T(8,128)(2,1)} fusion(bf16[2,1024,512]{2,1,0:T(8,128)(2,1)} %bitcast.149, f32[1280,1024]{0,1:T(8,128)} %copy-done.8), kind=kOutput, calls=%fused_computation.53 | convolution fusion | flops 2686976000 | bytes 9961472 | tf_op jit(solution)/shard_map/rd,jdf->rjf/dot_general | solution.py:583
  384.4 3.0 copy.99.mixed_grad_ref
  387.5 34.6 %attend_back.1 = (bf16[3,1280,1024]{2,1,0:T(8,128)(2,1)}, f32[8,2,128]{2,1,0:T(2,128)S(1)}) custom-call(s32[4]{0:T(128)S(1)} %copy-done.1, bf16[3,1280,1024]{2,1,0:T(8,128)(2,1)} %add_convert_fusion.qkv_ref, bf16[1280,1024]{1,0:T(8,128)(2,1)S(1)} %copy.99.mixed_grad_ref, f32[32,1,640]{2,1,0:T(1,128)S(1)} %get-tuple-element.34.log_ref), custom_call_target="tpu_custom_call" | custom-call | flops 16777216000 | bytes 18350080 | tf_op jit(solution)/shard_map/attend_back/pallas_call | solution.py:123
  422.2 14.6 %convert_bitcast_fusion = bf16[3,2,1024,512]{2,3,1,0:T(8,128)(2,1)} fusion(bf16[3,160,2,8,512]{4,3,2,1,0:T(8,128)(2,1)} %bitcast.150, bf16[1280,1024]{0,1:T(8,128)(2,1)S(1)} %copy-done.3, f32[1024]{0:T(1024)S(1)} %copy-done.33, f32[1024]{0:T(1024)S(1)} %copy-done.25, f32[1280]{0:T(1024)S(1)} %copy-done.17, f32[1280]{0:T(1024)S(1)} %copy-done.13), kind=kOutput, calls=%fused_computation.28 | convolution fusion | flops 8064073728 | bytes 16795648 | tf_op jit(solution)/shard_map/rb,mrjx->mjbx/dot_general | solution.py:588
  436.8 8.8 %copy.71 = bf16[3,2,1024,512]{3,2,1,0:T(8,128)(2,1)} copy(bf16[3,2,1024,512]{2,3,1,0:T(8,128)(2,1)} %convert_bitcast_fusion) | data formatting | bytes 12582912 | tf_op jit(solution)/shard_map/convert_element_type | solution.py:588
  445.6 14.3 %fusion.63 = (f32[1024]{0:T(1024)S(1)}, f32[1280,1024]{1,0:T(8,128)}) fusion(bf16[3,2,1024,512]{3,2,1,0:T(8,128)(2,1)} %bitcast.147, bf16[3,160,2,8,512]{4,3,2,1,0:T(8,128)(2,1)} %bitcast.151), kind=kOutput, calls=%fused_computation.105 | convolution fusion | flops 8054373376 | bytes 19402752 | tf_op jit(solution)/shard_map/mejx,mjwx->ew/dot_general | solution.py:589
  459.9 6.0 copy.77
  466.0 3.6 fusion.24
  469.6 0.5 copy-done.6
  470.0 2.6 fusion.48
  472.7 3.7 add_add_fusion.2
  476.3 5.9 copy.82
  482.3 0.6 constant_dynamic-update-slice_fusion
  483.0 0.6 pad_bitcast_fusion.refs_3_
  483.6 17.6 %convolution_convert_fusion.1 = bf16[2,2048,1024]{1,2,0:T(8,128)(2,1)} fusion(bf16[1280,2,2048]{2,0,1:T(8,128)(2,1)} %get-tuple-element.97, f32[1280,1024]{0,1:T(8,128)} %copy-done.5, f32[1024]{0:T(1024)S(1)} %copy-done.35, f32[1024]{0:T(1024)S(1)} %copy-done.27, f32[1280]{0:T(1024)S(1)} %copy-done.23, f32[1280]{0:T(1024)S(1)} %copy-done.15), kind=kOutput, calls=%fused_computation.32 | convolution fusion | flops 10748166144 | bytes 24135680 | tf_op jit(solution)/shard_map/rd,rjf->jdf/dot_general | solution.py:573
  501.3 96.2 %scatter.1 = (f32[3,64,512]{2,1,0:T(8,128)}, f32[64,512]{1,0:T(8,128)}, f32[64,2048]{1,0:T(8,128)}, f32[104,128]{1,0:T(8,128)}) custom-call(bf16[3,2,4,2,2,64,512]{6,5,4,3,2,1,0:T(8,128)(2,1)} %bitcast.119, bf16[2,4,2,2,64,512]{5,4,3,2,1,0:T(8,128)(2,1)} %bitcast.125, bf16[2,4,2,2,64,2048]{5,4,3,2,1,0:T(8,128)(2,1)} %bitcast.124, ...), custom_call_target="tpu_custom_call" | custom-call | tf_op jit(solution)/shard_map/scatter/pallas_call | solution.py:481
  597.4 0.7 slice.58
  598.1 1.2 slice.65
  600.0 1.3 dynamic_slice.11
  601.3 0.6 constant_dynamic-slice_fusion
  601.9 1.3 slice_bitcast_fusion
  603.2 1.8 convert_element_type.102
  605.0 1.8 copy.141
  606.8 1.6 copy.142
  608.4 1.9 copy.143
  (103 shorter events, 0.3 us)
Async XLA Ops:
  7.2 233.5 %all-gather.2.cloned.1.call-start = ((), (), s32[]{:S(2)}) async-start(), calls=%async_computation.1 | async-start | bytes 8650752 | tf_op jit(solution)/shard_map/all_gather | solution.py:540
  7.9 595.3 %reduce-scatter.2.cloned.1.call-start = ((), (), s32[]{:S(2)}) async-start(), calls=%async_computation.2 | async-start | bytes 8650752 | tf_op jit(solution)/shard_map/reduce_scatter | solution.py:567
  10.7 174.2 %copy-start = (s32[4]{0:T(128)}, s32[4]{0:T(128)S(1)}, u32[]{:S(2)}) copy-start(s32[4]{0:T(128)S(1)} %dynamic_slice.9.lengths_ref) | copy-start | bytes 52
  13.8 132.2 %copy-start.2 = (bf16[1280,1024]{0,1:T(8,128)(2,1)}, bf16[1280,1024]{0,1:T(8,128)(2,1)S(1)}, u32[]{:S(2)}) copy-start(bf16[1280,1024]{0,1:T(8,128)(2,1)S(1)} %copy.56) | copy-start | bytes 7864324
  13.8 132.2 %copy-start.24 = (f32[1024]{0:T(1024)S(1)}, f32[1024]{0:T(1024)}, u32[]{:S(2)}) copy-start(f32[1024]{0:T(1024)} %param.18) | copy-start | bytes 12292
  13.8 132.2 %copy-start.32 = (f32[1024]{0:T(1024)S(1)}, f32[1024]{0:T(1024)}, u32[]{:S(2)}) copy-start(f32[1024]{0:T(1024)} %param.19) | copy-start | bytes 12292
  144.7 15.5 %copy-start.12 = (f32[1280]{0:T(1024)}, f32[1280]{0:T(1024)S(1)}, u32[]{:S(2)}) copy-start(f32[1280]{0:T(1024)S(1)} %broadcast_multiply_fusion.1) | copy-start | bytes 15364
  145.4 0.6 copy-start.18
  146.0 14.2 %copy-start.16 = (f32[1280]{0:T(1024)}, f32[1280]{0:T(1024)S(1)}, u32[]{:S(2)}) copy-start(f32[1280]{0:T(1024)S(1)} %fusion.52) | copy-start | bytes 15364
  160.2 15.7 %copy-start.28 = (f32[2,2,512]{2,1,0:T(2,128)S(1)}, f32[2,2,512]{2,1,0:T(2,128)}, u32[]{:S(2)}) copy-start(f32[2,2,512]{2,1,0:T(2,128)} %get-tuple-element.29) | copy-start | bytes 24580
  213.9 3.0 copy-start.30
  216.9 8.6 %slice-start.4 = ((s8[8388608]{0:T(1024)(128)(4,1)}), s8[4194304]{0:T(1024)(128)(4,1)S(1)}, s32[]{:S(2)}) async-start(s8[8388608]{0:T(1024)(128)(4,1)} %bitcast.143), calls=%async_computation.7 | async-start | bytes 8388608
  216.9 8.6 %slice-start.5 = ((s8[8388608]{0:T(1024)(128)(4,1)}), s8[4194304]{0:T(1024)(128)(4,1)S(1)}, s32[]{:S(2)}) async-start(s8[8388608]{0:T(1024)(128)(4,1)} %bitcast.143), calls=%async_computation.8 | async-start | bytes 8388608
  223.2 2.3 copy-start.5
  223.2 2.3 copy-start.26
  223.2 2.3 copy-start.34
  223.2 2.3 copy-start.14
  223.8 0.6 copy-start.20
  223.8 1.7 copy-start.22
  225.5 15.2 %copy-start.10 = (bf16[1280,1024]{0,1:T(8,128)(2,1)S(1)}, bf16[1280,1024]{0,1:T(8,128)(2,1)}, u32[]{:S(2)}) copy-start(bf16[1280,1024]{0,1:T(8,128)(2,1)} %copy.63) | copy-start | bytes 7864324
  225.5 15.1 %copy-start.31 = (f32[1024]{0:T(1024)S(1)}, f32[1024]{0:T(1024)}, u32[]{:S(2)}) copy-start(f32[1024]{0:T(1024)} %param.29) | copy-start | bytes 12292
  327.4 17.4 %copy-start.11 = (bf16[1280,1024]{0,1:T(8,128)(2,1)S(1)}, bf16[1280,1024]{0,1:T(8,128)(2,1)}, u32[]{:S(2)}) copy-start(bf16[1280,1024]{0,1:T(8,128)(2,1)} %get-tuple-element.80) | copy-start | bytes 7864324
  347.5 5.9 copy-start.15
  347.5 5.9 copy-start.27
  353.4 5.2 copy-start.21
  353.4 5.8 copy-start.7
  353.4 5.8 copy-start.23
  353.4 10.9 %slice-start = ((s8[5242880]{0:T(1024)(128)(4,1)}), s8[1048576]{0:T(1024)(128)(4,1)S(1)}, s32[]{:S(2)}) async-start(s8[5242880]{0:T(1024)(128)(4,1)} %bitcast.117), calls=%async_computation.3 | async-start | bytes 2097152
  359.2 5.1 slice-start.1
  364.3 6.8 %copy-start.9 = (bf16[1280,1024]{0,1:T(8,128)(2,1)S(1)}, bf16[1280,1024]{0,1:T(8,128)(2,1)}, u32[]{:S(2)}) copy-start(bf16[1280,1024]{0,1:T(8,128)(2,1)} %copy.103) | copy-start | bytes 7864324
  368.7 2.4 copy-start.8
  384.4 3.0 copy-start.1
  387.4 34.7 %copy-start.3 = (bf16[1280,1024]{0,1:T(8,128)(2,1)S(1)}, bf16[1280,1024]{0,1:T(8,128)(2,1)}, u32[]{:S(2)}) copy-start(bf16[1280,1024]{0,1:T(8,128)(2,1)} %copy-done.2) | copy-start | bytes 7864324
  387.4 34.7 %copy-start.13 = (f32[1280]{0:T(1024)S(1)}, f32[1280]{0:T(1024)}, u32[]{:S(2)}) copy-start(f32[1280]{0:T(1024)} %copy-done.12) | copy-start | bytes 15364
  387.4 34.7 %copy-start.17 = (f32[1280]{0:T(1024)S(1)}, f32[1280]{0:T(1024)}, u32[]{:S(2)}) copy-start(f32[1280]{0:T(1024)} %copy-done.16) | copy-start | bytes 15364
  387.5 34.7 %copy-start.25 = (f32[1024]{0:T(1024)S(1)}, f32[1024]{0:T(1024)}, u32[]{:S(2)}) copy-start(f32[1024]{0:T(1024)} %param.18) | copy-start | bytes 12292
  387.5 34.7 %copy-start.33 = (f32[1024]{0:T(1024)S(1)}, f32[1024]{0:T(1024)}, u32[]{:S(2)}) copy-start(f32[1024]{0:T(1024)} %param.19) | copy-start | bytes 12292
  459.9 6.0 copy-start.4
  459.9 9.6 %copy-start.19 = (f32[1280]{0:T(1024)S(1)}, f32[1280]{0:T(1024)}, u32[]{:S(2)}) copy-start(f32[1280]{0:T(1024)} %copy-done.18) | copy-start | bytes 15364
  466.0 4.0 copy-start.6
  466.0 6.7 %slice-start.2 = ((s8[5242880]{0:T(1024)(128)(4,1)}), s8[4194304]{0:T(1024)(128)(4,1)S(1)}, s32[]{:S(2)}) async-start(s8[5242880]{0:T(1024)(128)(4,1)} %bitcast.120), calls=%async_computation.5 | async-start | bytes 8388608
  470.0 2.6 slice-start.3
  476.3 6.0 copy-start.29
  476.3 7.3 %copy-start.35 = (f32[1024]{0:T(1024)S(1)}, f32[1024]{0:T(1024)}, u32[]{:S(2)}) copy-start(f32[1024]{0:T(1024)} %param.25) | copy-start | bytes 12292
Sparse Core Ops, SparseCore 0:
  10.8 118.0 all-gather.1
  327.5 153.1 reduce-scatter.1

commit v3 on v2

v3 whole, which is shorter than its diff:
```python
from functools import partial
import math

import jax
import jax.numpy as jnp
from jax import lax
from jax.experimental import pallas as pl
from jax.experimental.pallas import tpu as pltpu
from jax.sharding import PartitionSpec as P

HD = 64
SLOTS = 320
PAIR = 2 * HD

EPSILON = 1e-05
MASKED_SCORE = -1e30
F32 = jnp.float32
BF16 = jnp.bfloat16
EVERY = ("tensor", "dp")
CORES = 2
LINE = 4


AXES = ("tensor", "line", "row", "core")
MESH = pl.DeviceIdType.MESH
GATHER_ORDERS = (("line", "tensor", "row", "core"), ("line", "row", "tensor", "core"))


def sizes():
    dp = lax.axis_size("dp")
    return {"tensor": lax.axis_size("tensor"), "line": LINE, "row": dp // (LINE * CORES), "core": CORES}


class Place:
    def __init__(self):
        self.size = sizes()
        index = lax.axis_index("dp")
        self.at = {
            "tensor": lax.axis_index("tensor"),
            "core": lax.rem(index, CORES),
            "row": lax.rem(lax.div(index, CORES), self.size["row"]),
            "line": lax.div(index, CORES * self.size["row"]),
        }

    def steps(self, axis):
        return range(1, self.size[axis])

    def peer(self, axis, step):
        return lax.rem(self.at[axis] + step, self.size[axis])

    def device(self, axis, place):
        at = {**self.at, axis: place}
        return {"dp": (at["line"] * self.size["row"] + at["row"]) * CORES + at["core"], "tensor": at["tensor"]}

    def greet(self):
        barrier = pltpu.get_barrier_semaphore()
        count = 0
        for axis in AXES:
            for step in self.steps(axis):
                pl.semaphore_signal(
                    barrier, inc=1, device_id=self.device(axis, self.peer(axis, step)), device_id_type=MESH
                )
                count += 1
        pl.semaphore_wait(barrier, count)


def pieces_of(shards, width):
    out = []
    for a, shard in enumerate(shards):
        for lead in range(shard.shape[0]) if len(shard.shape) == 3 else (None,):
            for col in range(shard.shape[-1] // width):
                out.append((a, lead, col))
    return out


def piece(refs, which, width):
    a, lead, col = which
    ref = refs[a] if lead is None else refs[a].at[lead]
    spare = (slice(None),) * (len(ref.shape) - 1)
    return ref.at[(*spare, pl.ds(col * width, width))]


def whole_shape(weight):
    size = sizes()
    return (*weight.shape[:-2], *(size[a] for a in AXES), *weight.shape[-2:])


class Gather:
    def __init__(self, pieces, width, offsets, ins, outs, sems):
        self.here = Place()
        self.pieces, self.width, self.offsets, self.ins, self.outs = pieces, width, offsets, ins, outs
        self.send_sem, self.recv_sem, self.own_sem = sems
        self.half = ins[0].shape[-2] // 2
        self.count = len(pieces)

    def region(self, n, h, stage, axis=None, place=None):
        order = GATHER_ORDERS[h]
        index = [
            slice(None) if a in order[:stage] else place if a == axis else self.here.at[a] for a in AXES
        ]
        return piece(self.outs, self.pieces[n], self.width).at[(*index, pl.ds(h * self.half, self.half))]

    def remote(self, n, h, stage, step, coming=False):
        here, axis = self.here, GATHER_ORDERS[h][stage]
        slot = (n, h, stage, step - 1)
        to = source = self.region(n, h, stage)
        if stage == 0:
            source = piece(self.ins, self.pieces[n], self.width).at[pl.ds(h * self.half, self.half)]
        if coming:
            to = self.region(n, h, stage, axis, here.peer(axis, here.size[axis] - step))
        return pltpu.make_async_remote_copy(
            src_ref=source, dst_ref=to, send_sem=self.send_sem.at[slot], recv_sem=self.recv_sem.at[slot],
            device_id=here.device(axis, here.peer(axis, step)), device_id_type=MESH,
        )

    def every(self, n, stage):
        return [(n, h, stage, step) for h in range(2) for step in self.here.steps(GATHER_ORDERS[h][stage])]

    def start(self, n, stage):
        for slot in self.every(n, stage):
            self.remote(*slot).start()

    def arrived(self, n, stage=3):
        for slot in self.every(n, stage):
            self.remote(*slot, coming=True).wait_recv()

    def own(self, n):
        place = tuple(self.here.at[a] for a in AXES)
        return pltpu.make_async_copy(
            piece(self.ins, self.pieces[n], self.width),
            piece(self.outs, self.pieces[n], self.width).at[place], self.own_sem.at[n],
        )

    def begin(self):
        self.here.greet()
        for n in range(self.count):
            self.start(n, 0)
            self.own(n).start()

    def ticks(self):
        return self.count + self.offsets[-1]

    def tick(self, k):
        for stage, offset in enumerate(self.offsets, 1):
            n = k - offset
            if 0 <= n < self.count:
                if stage == 1:
                    self.own(n).wait()
                self.arrived(n, stage - 1)
                self.start(n, stage)

    def end(self):
        for n in range(self.count):
            for stage in range(4):
                for slot in self.every(n, stage):
                    self.remote(*slot).wait_send()


class Share:
    def __init__(self, here, source, target, sems):
        self.here, self.source, self.target = here, source, target
        self.send_sem, self.recv_sem, self.own_sem = sems

    def remote(self, step, coming=False):
        here = self.here
        place = here.peer("tensor", here.size["tensor"] - step) if coming else here.at["tensor"]
        return pltpu.make_async_remote_copy(
            src_ref=self.source, dst_ref=self.target.at[place],
            send_sem=self.send_sem.at[step - 1], recv_sem=self.recv_sem.at[step - 1],
            device_id=here.device("tensor", here.peer("tensor", step)), device_id_type=MESH,
        )

    def own(self):
        return pltpu.make_async_copy(self.source, self.target.at[self.here.at["tensor"]], self.own_sem)

    def begin(self):
        self.own().start()
        for step in self.here.steps("tensor"):
            self.remote(step).start()

    def arrived(self):
        self.own().wait()
        for step in self.here.steps("tensor"):
            self.remote(step, coming=True).wait_recv()

    def end(self):
        for step in self.here.steps("tensor"):
            self.remote(step).wait_send()


SCATTER_ORDERS = (
    (("tensor", "row", "line"), ("row", "tensor", "line")),
    (("line", "tensor", "row"), ("line", "row", "tensor")),
)
SUM_AXES = ("core", "tensor", "row", "line")


def scatter_kernel(pieces, width, orders, lag, n_grads, *refs):
    ins, small = refs[:n_grads], refs[n_grads]
    outs, small_out = refs[n_grads + 1 : 2 * n_grads + 1], refs[2 * n_grads + 1]
    own_buf, first_buf, *rest = refs[2 * n_grads + 2 :]
    count = len(pieces)
    late = {(n, h, s): rest[(n * 2 + h) * 3 + s - 1] for n in range(count) for h in range(2) for s in (1, 2, 3)}
    small_bufs = rest[6 * count : 6 * count + 4]
    send_sem, recv_sem, own_sem, small_send, small_recv = rest[6 * count + 4 :]
    here = Place()
    here.greet()
    half = own_buf.shape[-2] // 2
    three = AXES[:3]

    def own(n):
        source = piece(ins, pieces[n], width).at[:, :, :, here.at["core"]]
        return pltpu.make_async_copy(source, own_buf.at[n], own_sem.at[n])

    def to_core(n):
        other = here.peer("core", 1)
        return pltpu.make_async_remote_copy(
            src_ref=piece(ins, pieces[n], width).at[:, :, :, other], dst_ref=first_buf.at[n],
            send_sem=send_sem.at[n, 0, 0, 0], recv_sem=recv_sem.at[n, 0, 0, 0],
            device_id=here.device("core", other), device_id_type=MESH,
        )

    def remote(n, h, stage, step):
        order = orders[n][h]
        axis = order[stage - 1]
        to = here.peer(axis, step)
        index = [
            here.at[a] if a in order[: stage - 1] else to if a == axis else slice(None) for a in three
        ]
        slot = (n, h, stage, step - 1)
        return pltpu.make_async_remote_copy(
            src_ref=own_buf.at[(n, *index, pl.ds(h * half, half))],
            dst_ref=late[n, h, stage].at[step - 1],
            send_sem=send_sem.at[slot], recv_sem=recv_sem.at[slot],
            device_id=here.device(axis, to), device_id_type=MESH,
        )

    def every(n, stage, act):
        for h in range(2):
            for step in here.steps(orders[n][h][stage - 1]):
                act(remote(n, h, stage, step))

    def add_core(n):
        def one(i, _):
            first, left = lax.div(i, here.size["row"]), lax.rem(i, here.size["row"])
            at = (n, lax.div(first, LINE), lax.rem(first, LINE), left)
            own_buf[at] = (own_buf[at].astype(F32) + first_buf[at].astype(F32)).astype(BF16)
            return 0

        lax.fori_loop(0, math.prod(here.size[a] for a in three), one, 0)

    def add(n, h, stage):
        order = orders[n][h]
        buf, steps = late[n, h, stage], here.size[order[stage - 1]] - 1
        free = [a for a in three if a not in order[:stage]]
        rows = pl.ds(h * half, half)

        def one(i, _):
            at, left = dict(here.at), i
            for a in reversed(free):
                at[a] = lax.rem(left, here.size[a])
                left = lax.div(left, here.size[a])
            mine = (n, *(at[a] for a in three), rows)
            total = own_buf[mine].astype(F32)
            for s in range(steps):
                total += buf[(s, *(at[a] for a in free))].astype(F32)
            if stage == 3:
                out = piece(outs, pieces[n], width)
                out[rows, :] = total
            else:
                own_buf[mine] = total.astype(BF16)
            return 0

        if free:
            lax.fori_loop(0, math.prod(here.size[a] for a in free), one, 0)
        else:
            one(0, 0)

    def small_copy(stage, step, coming=False):
        axis = SUM_AXES[stage]
        place = here.peer(axis, here.size[axis] - step) if coming else here.at[axis]
        buf = small_bufs[stage]
        return pltpu.make_async_remote_copy(
            src_ref=buf.at[here.at[axis]], dst_ref=buf.at[place],
            send_sem=small_send.at[stage, step - 1], recv_sem=small_recv.at[stage, step - 1],
            device_id=here.device(axis, here.peer(axis, step)), device_id_type=MESH,
        )

    def small_start(stage, value):
        axis = SUM_AXES[stage]
        small_bufs[stage][here.at[axis]] = value
        for step in here.steps(axis):
            small_copy(stage, step).start()

    def small_end(stage):
        axis = SUM_AXES[stage]
        for step in here.steps(axis):
            small_copy(stage, step, coming=True).wait_recv()
            small_copy(stage, step).wait_send()
        total = small_bufs[stage][0]
        for place in range(1, here.size[axis]):
            total += small_bufs[stage][place]
        return total

    for n in range(count):
        to_core(n).start()
        own(n).start()
    small_start(0, small[...])
    for tick in range(max(count + 3 * lag, 5)):
        if 1 <= tick <= 4:
            total = small_end(tick - 1)
            if tick < 4:
                small_start(tick, total)
            else:
                small_out[...] = total
        for stage in range(4):
            n = tick - lag * stage
            if not 0 <= n < count:
                continue
            if stage == 0:
                own(n).wait()
                to_core(n).wait_recv()
                add_core(n)
            else:
                every(n, stage, lambda copy: copy.wait_recv())
                for h in range(2):
                    add(n, h, stage)
            if stage < 3:
                every(n, stage + 1, lambda copy: copy.start())
    for n in range(count):
        to_core(n).wait_send()
        for stage in (1, 2, 3):
            every(n, stage, lambda copy: copy.wait_send())


def scatter(grads, small, collective_id, width, third=(), lag=2):
    size = sizes()
    shards = [jax.ShapeDtypeStruct((*g.shape[:-6], *g.shape[-2:]), F32) for g in grads]
    pieces = pieces_of(shards, width)
    count, most = len(pieces), max(size.values()) - 1
    orders = [SCATTER_ORDERS[n in third] for n in range(count)]
    rows = grads[0].shape[-2]
    three = AXES[:3]
    whole = (count, *(size[a] for a in three), rows, width)
    late = []
    for n in range(count):
        for h in range(2):
            for s in (1, 2, 3):
                order = orders[n][h]
                free = [size[a] for a in three if a not in order[:s]]
                late.append(pltpu.VMEM((size[order[s - 1]] - 1, *free, rows // 2, width), BF16))
    vmem = pl.BlockSpec(memory_space=pltpu.VMEM)
    return pl.pallas_call(
        partial(scatter_kernel, pieces, width, orders, lag, len(grads)),
        out_shape=[*shards, jax.ShapeDtypeStruct(small.shape, small.dtype)],
        in_specs=[*[pl.BlockSpec(memory_space=pl.ANY)] * len(grads), vmem],
        out_specs=[vmem] * (len(grads) + 1),
        scratch_shapes=[
            pltpu.VMEM(whole, BF16),
            pltpu.VMEM(whole, BF16),
            *late,
            *[pltpu.VMEM((size[a], *small.shape), F32) for a in SUM_AXES],
            pltpu.SemaphoreType.DMA((count, 2, 4, most)),
            pltpu.SemaphoreType.DMA((count, 2, 4, most)),
            pltpu.SemaphoreType.DMA((count,)),
            pltpu.SemaphoreType.DMA((4, most)),
            pltpu.SemaphoreType.DMA((4, most)),
        ],
        compiler_params=pltpu.CompilerParams(
            collective_id=collective_id, has_side_effects=True, vmem_limit_bytes=60 * 2**20
        ),
        name="scatter",
    )(*grads, small)


def dot(left, right, left_dim=1, right_dim=0):
    return lax.dot_general(
        left, right, (((left_dim,), (right_dim,)), ((), ())), preferred_element_type=F32
    )


def side_by_side(ref, *lead):
    return jnp.concatenate([ref[(*lead, t)] for t in range(ref.shape[-3])], axis=-1)


def centred(rows):
    off = rows - jnp.mean(rows, axis=-1, keepdims=True)
    inverse = lax.rsqrt(jnp.mean(off * off, axis=-1, keepdims=True) + EPSILON)
    return off * inverse, inverse


def norm_back(grad, hat, inverse, gain):
    scaled = grad * gain
    along = jnp.mean(scaled * hat, axis=-1, keepdims=True)
    return inverse * (scaled - jnp.mean(scaled, axis=-1, keepdims=True) - hat * along)


def fold(rows):
    return jnp.sum(rows.reshape(-1, 8, rows.shape[-1]), axis=0)


def row_blocks(rows, size, one):
    def step(i, _):
        one(i, pl.ds(pl.multiple_of(i * size, size), size))
        return 0

    lax.fori_loop(0, rows // size, step, 0)


def transpose_into(source, target):
    rows = source.shape[0]
    for first in range(0, rows, 128):
        size = min(128, rows - first)
        target[:, first : first + size] = source[first : first + size, :].astype(F32).T.astype(BF16)


def two_heads(pair):
    first = lax.broadcasted_iota(jnp.int32, pair.shape, 1) < HD
    zero = jnp.zeros_like(pair)
    return jnp.concatenate([jnp.where(first, pair, zero), jnp.where(first, zero, pair)], axis=0)


def one_pair(stacked):
    first = lax.broadcasted_iota(jnp.int32, (SLOTS, PAIR), 1) < HD
    return jnp.where(first, stacked[:SLOTS], stacked[SLOTS:])


def masked_scores(query_stack, keys, length):
    scores = dot(keys, query_stack, 1, 1)
    slot = lax.broadcasted_iota(jnp.int32, scores.shape, 0)
    return jnp.where(slot < length, scores, MASKED_SCORE)


def group_weight(qkv_held, columns):
    parts = [qkv_held[e, t, ..., columns] for t in range(qkv_held.shape[1]) for e in range(3)]
    return jnp.concatenate([part.reshape(-1, PAIR) for part in parts], axis=-1)


def merge_tile(merge_held, columns):
    parts = [merge_held[t, ..., columns] for t in range(merge_held.shape[0])]
    return jnp.concatenate([part.reshape(-1, PAIR) for part in parts], axis=-1)


def schedule(ticks, last_piece, needed, steps):
    at = []
    first = needed.index(next(s for s in needed if s > 0), 0) if any(needed) else len(needed)
    early = first + last_piece
    for k in range(ticks):
        piece_done = k - last_piece
        even = 0 if k < early else 1 + (k - early) * (steps - 1) // (ticks - early)
        at.append(min(even, needed[max(piece_done, 0)]))
    for k in range(ticks - 2, -1, -1):
        at[k] = min(at[k], at[k + 1])
    return at


def forward_kernel(
    width_of_piece, offsets, feed_columns,
    lengths, x_ref, gain, shift, merge_bias, gain_2, shift_2, heads_bias, expand_bias,
    qkv_part, merge_part, expand_part, reduce_part,
    a_turned, qkv_ref, mixed_ref, log_ref, hidden_ref, second_ref, second_turned, activ, slope,
    qkv_full, merge_full, expand_full, reduce_full,
    a_ref, qkv_held, merge_held, tiles, heads_bias_all, expand_bias_all,
    send_sem, recv_sem, own_sem, share_send, share_recv, share_own, held_sem, tile_sem,
):
    now = pl.program_id(0)
    rows = x_ref.shape[0]
    images = rows // SLOTS
    halves = qkv_held.shape[1]
    groups = width_of_piece // PAIR
    attention_steps = groups * images
    feed_steps = expand_part.shape[1] // feed_columns
    steps = attention_steps + feed_steps
    parts = [qkv_part, merge_part, expand_part, reduce_part]
    pieces = pieces_of(parts, width_of_piece)
    gather = Gather(
        pieces, width_of_piece, offsets, parts, [qkv_full, merge_full, expand_full, reduce_full],
        (send_sem, recv_sem, own_sem),
    )
    shares = [
        Share(gather.here, source, target, (share_send.at[n], share_recv.at[n], share_own.at[n]))
        for n, (source, target) in enumerate([(heads_bias, heads_bias_all), (expand_bias, expand_bias_all)])
    ]
    tiles_of_piece = width_of_piece // feed_columns
    needed = [
        0 if a == 0 else images - 1 if a == 1
        else max(attention_steps + col * tiles_of_piece - 1, 0) if a == 2 else steps - 1
        for a, _, col in pieces
    ]
    when = schedule(gather.ticks(), offsets[-1], needed, steps)
    image = lax.rem(now, images)
    group = lax.min(lax.div(now, images), groups - 1)
    columns = pl.ds(pl.multiple_of(group * PAIR, PAIR), PAIR)

    def hold(n):
        a, lead, _ = pieces[n]
        source, target = (qkv_full.at[lead], qkv_held.at[lead]) if a == 0 else (merge_full, merge_held)
        return pltpu.make_async_copy(source, target, held_sem.at[n])

    def tile_copy(j):
        block = pl.ds(j * feed_columns, feed_columns)
        return pltpu.make_async_copy(
            expand_full.at[:, :, :, :, :, block], tiles.at[j % 2], tile_sem.at[j % 2]
        )

    def fetch_tile(j):
        if j % tiles_of_piece == 0:
            gather.arrived(4 + j // tiles_of_piece)
        tile_copy(j).start()

    @pl.when(now == 0)
    def _():
        gather.begin()
        for share in shares:
            share.begin()
        early = [k for k in range(gather.ticks()) if when[k] == 0]
        blocks = rows // 32
        per = -(-blocks // max(len(early), 1))

        def norm(i, _):
            at = pl.ds(pl.multiple_of(i * 32, 32), 32)
            x = x_ref[at, :].astype(F32)
            hidden_ref[at, :] = x + merge_bias[...]
            a_ref[at, :] = (centred(x)[0] * gain[...] + shift[...]).astype(BF16)
            return 0

        done = 0
        for k in early:
            lax.fori_loop(done, min(done + per, blocks), norm, 0)
            done = min(done + per, blocks)
            gather.tick(k)
            n = k - offsets[-1] - 1
            if 0 <= n < 3:
                gather.arrived(n)
                hold(n).start()
        lax.fori_loop(done, blocks, norm, 0)
        transpose_into(a_ref, a_turned)
        for n in range(max(len(early) - offsets[-1] - 1, 0), 3):
            gather.arrived(n)
            hold(n).start()
        for share in shares:
            share.arrived()
        for n in range(3):
            hold(n).wait()

    for k in range(gather.ticks()):
        if when[k] > 0:
            pl.when(now == when[k])(partial(gather.tick, k))

    @pl.when((now < attention_steps) & (image == 0))
    def _():
        weight = group_weight(qkv_held, columns)
        bias = []
        for t in range(halves):
            query = heads_bias_all[t, 0:1, columns]
            bias += [query, jnp.zeros_like(query), heads_bias_all[t, 1:2, columns]]
        bias = jnp.concatenate(bias, axis=-1)
        for i in range(images):
            at = slice(i * SLOTS, (i + 1) * SLOTS)
            out = (dot(a_ref[at, :], weight) + bias).astype(BF16)
            for t in range(halves):
                query = slice(t * 3 * PAIR, (t * 3 + 1) * PAIR)
                qkv_ref[0, at, query] = out[:, query] * 0.125
                rest = slice((t * 3 + 1) * PAIR, (t * 3 + 3) * PAIR)
                qkv_ref[0, at, rest] = out[:, rest]

    @pl.when(now < attention_steps)
    def _():
        length = lengths[image]
        at = pl.ds(pl.multiple_of(image * SLOTS, SLOTS), SLOTS)
        for t in range(halves):
            first = t * 3 * PAIR
            query_stack = two_heads(qkv_ref[0, at, first : first + PAIR])
            scores = masked_scores(query_stack, qkv_ref[0, at, first + PAIR : first + 2 * PAIR], length)
            highest = jnp.max(scores, axis=0, keepdims=True)
            expo = jnp.exp(scores - highest)
            totals = jnp.sum(expo, axis=0, keepdims=True)
            values = qkv_ref[0, at, first + 2 * PAIR : first + 3 * PAIR]
            mixed = dot(values, expo.astype(BF16), 0, 0) * (1.0 / totals)
            mixed_ref[0, at, t * PAIR : (t + 1) * PAIR] = one_pair(mixed.T).astype(BF16)
            log_ref[0, 0, t : t + 1] = highest + jnp.log(totals)

    @pl.when(now == images - 1)
    def _():
        gather.arrived(3)
        hold(3).start()
        hold(3).wait()

    @pl.when((now < attention_steps) & (image == images - 1))
    def _():
        weight = merge_tile(merge_held, columns)
        for i in range(images):
            part = slice(i * SLOTS, (i + 1) * SLOTS)
            hidden_ref[part, :] += dot(mixed_ref[0, part, :], weight, 1, 1)

    @pl.when(now == attention_steps - 1)
    def _():
        fetch_tile(0)

        def norm(_, at):
            hat, _ = centred(hidden_ref[at, :])
            second_ref[at, :] = (hat * gain_2[...] + shift_2[...]).astype(BF16)

        row_blocks(rows, 32, norm)
        transpose_into(second_ref, second_turned)

    for j in range(feed_steps):

        @pl.when(now == attention_steps + j)
        def _(j=j):
            tile_copy(j).wait()
            if j + 1 < feed_steps:
                fetch_tile(j + 1)

    @pl.when(now >= attention_steps)
    def _():
        j = now - attention_steps
        block = pl.ds(pl.multiple_of(j * feed_columns, feed_columns), feed_columns)
        slot = lax.rem(j, 2)
        weight = jnp.concatenate(
            [tiles[slot, t].reshape(-1, feed_columns) for t in range(halves)], axis=-1
        )
        bias = jnp.concatenate([expand_bias_all[t, :, block] for t in range(halves)], axis=-1)
        for i in range(images):
            at = slice(i * SLOTS, (i + 1) * SLOTS)
            z = dot(second_ref[at, :], weight) + bias
            square = z * z
            bend = jnp.tanh(0.7978845608 * z * (1.0 + 0.044715 * square))
            half = 0.5 + 0.5 * bend
            activ[0, at, :] = (z * half).astype(BF16)
            inner = 0.7978845608 * z * (1.0 + (3 * 0.044715) * square)
            slope[0, at, :] = (half + 0.5 * inner * (1.0 - bend * bend)).astype(BF16)

    @pl.when(now == steps - 1)
    def _():
        for n in range(8, gather.count):
            gather.arrived(n)
        gather.end()
        for share in shares:
            share.end()


def feed_kernel(
    lengths, count, activ, hidden, reduce, reduce_bias, teacher,
    out, grad, grad_b, grad_turned, bias_grad, loss, total,
):
    step = pl.program_id(0)
    rows = hidden.shape[0]
    reduce_tile = side_by_side(reduce)

    @pl.when(step == 0)
    def _():
        total[...] = jnp.zeros_like(total)

    for i in range(rows // SLOTS):
        at = slice(i * SLOTS, (i + 1) * SLOTS)
        total[at, :] += dot(activ[0, at, :], reduce_tile, 1, 1)

    @pl.when(step == pl.num_programs(0) - 1)
    def _():
        bias_grad[...] = jnp.zeros_like(bias_grad)
        loss[...] = jnp.zeros_like(loss)

        def end(i, at):
            image, block = lax.div(i, SLOTS // 32), lax.rem(i, SLOTS // 32)
            slot = block * 32 + lax.broadcasted_iota(jnp.int32, (32, 1), 0)
            valid = slot < lengths[image]
            result = jnp.where(valid, hidden[at, :] + total[at, :] + reduce_bias[...], 0.0)
            out[at, :] = result.astype(BF16)
            error = jnp.where(valid, result - teacher[at, :].astype(F32), 0.0)
            loss[...] += fold(error * error)
            back = 2.0 * error / count[0]
            bias_grad[...] += fold(back)
            grad[at, :] = back
            grad_b[at, :] = back.astype(BF16)

        row_blocks(rows, 32, end)
        transpose_into(grad_b, grad_turned)


def feed_back_kernel(
    result_b, result_turned, second_turned, expand, reduce, activ, slope, hidden, result_grad, gain,
    reduce_grad, expand_grad, expand_bias_grad, hidden_grad, hidden_b, hidden_turned, sums, total,
):
    step = pl.program_id(0)
    rows = result_b.shape[0]
    halves, width, columns = expand.shape
    expand_tile, reduce_tile = side_by_side(expand), side_by_side(reduce)

    @pl.when(step == 0)
    def _():
        total[...] = jnp.zeros_like(total)

    reduce_part = dot(result_turned[...], activ[0])
    for t in range(halves):
        reduce_grad[t] = reduce_part[:, t * columns : (t + 1) * columns].astype(BF16)
    bias = jnp.zeros((8, halves * columns), F32)
    parts = []
    for i in range(rows // SLOTS):
        at = slice(i * SLOTS, (i + 1) * SLOTS)
        z_grad = (dot(result_b[at, :], reduce_tile) * slope[0, at, :].astype(F32)).astype(BF16)
        bias += fold(z_grad.astype(F32))
        parts.append(z_grad)
        total[at, :] += dot(z_grad, expand_tile, 1, 1)
    expand_bias_grad[0] = jnp.sum(bias, axis=0, keepdims=True)
    expand_part = dot(second_turned[...], jnp.concatenate(parts, axis=0))
    for t in range(halves):
        expand_grad[t] = expand_part[:, t * columns : (t + 1) * columns].astype(BF16)

    @pl.when(step == pl.num_programs(0) - 1)
    def _():
        sums[...] = jnp.zeros_like(sums)

        def end(_, at):
            hat, inverse = centred(hidden[at, :])
            second_grad = total[at, :]
            back = result_grad[at, :] + norm_back(second_grad, hat, inverse, gain[...])
            sums[0] += fold(second_grad * hat)
            sums[1] += fold(second_grad)
            sums[2] += fold(back)
            hidden_grad[at, :] = back
            hidden_b[at, :] = back.astype(BF16)

        row_blocks(rows, 32, end)
        transpose_into(hidden_b, hidden_turned)


def attend_back_kernel(
    lengths, a_turned, hidden_b, hidden_turned, qkv_ref, mixed_ref, log_ref, x_ref, hidden_grad, gain,
    qkv_weight, merge_weight,
    merge_grad, qkv_grad, bias_grad, inputs_grad, sums,
    mixed_grad, heads_grad, total, qkv_held, merge_held, sem,
):
    group, image = pl.program_id(0), pl.program_id(1)
    rows = x_ref.shape[0]
    halves = qkv_held.shape[1]
    columns = pl.ds(pl.multiple_of(group * PAIR, PAIR), PAIR)

    @pl.when((group == 0) & (image == 0))
    def _():
        copies = [
            pltpu.make_async_copy(merge_weight, merge_held, sem.at[1]),
            pltpu.make_async_copy(qkv_weight, qkv_held, sem.at[0]),
        ]
        for copy in copies:
            copy.start()
        total[...] = jnp.zeros_like(total)
        for copy in copies:
            copy.wait()

    @pl.when(image == 0)
    def _():
        weight = merge_tile(merge_held, columns)
        for i in range(rows // SLOTS):
            part = slice(i * SLOTS, (i + 1) * SLOTS)
            mixed_grad[part, :] = dot(hidden_b[part, :], weight).astype(BF16)
        part = dot(hidden_turned[...], mixed_ref[0]).astype(BF16)
        for t in range(halves):
            merge_grad[t] = part[:, t * PAIR : (t + 1) * PAIR]

    length = lengths[image]
    at = pl.ds(pl.multiple_of(image * SLOTS, SLOTS), SLOTS)
    for t in range(halves):
        first = t * 3 * PAIR
        query_stack = two_heads(qkv_ref[0, at, first : first + PAIR])
        keys = qkv_ref[0, at, first + PAIR : first + 2 * PAIR]
        values = qkv_ref[0, at, first + 2 * PAIR : first + 3 * PAIR]
        scores = masked_scores(query_stack, keys, length)
        attend = jnp.exp(scores - log_ref[0, 0, t : t + 1])
        grad_stack = two_heads(mixed_grad[at, t * PAIR : (t + 1) * PAIR])
        attend_grad = dot(values, grad_stack, 1, 1)
        value_grad = dot(attend.astype(BF16), grad_stack).astype(BF16)
        centre = jnp.sum(attend * attend_grad, axis=0, keepdims=True)
        score_grad = (attend * (attend_grad - centre)).astype(BF16)
        key_grad = dot(score_grad, query_stack).astype(BF16)
        query_grad = dot(keys, score_grad, 0, 0)
        query_grad = (one_pair(query_grad.T) * 0.125).astype(BF16)
        heads_grad[at, first : first + PAIR] = query_grad
        heads_grad[at, first + PAIR : first + 2 * PAIR] = key_grad
        heads_grad[at, first + 2 * PAIR : first + 3 * PAIR] = value_grad

    @pl.when(image == pl.num_programs(1) - 1)
    def _():
        weight = group_weight(qkv_held, columns)
        bias = jnp.zeros((8, halves * 3 * PAIR), F32)
        for i in range(rows // SLOTS):
            part = slice(i * SLOTS, (i + 1) * SLOTS)
            total[part, :] += dot(heads_grad[part, :], weight, 1, 1)
            bias += fold(heads_grad[part, :].astype(F32))
        bias_grad[0] = jnp.sum(bias, axis=0, keepdims=True)
        part = dot(a_turned[...], heads_grad[...]).astype(BF16)
        for t in range(halves):
            for e in range(3):
                first = (t * 3 + e) * PAIR
                qkv_grad[e, t] = part[:, first : first + PAIR]

    @pl.when((image == pl.num_programs(1) - 1) & (group == pl.num_programs(0) - 1))
    def _():
        sums[...] = jnp.zeros_like(sums)

        def end(_, at):
            hat, inverse = centred(x_ref[at, :].astype(F32))
            grad = total[at, :]
            sums[0] += fold(grad * hat)
            sums[1] += fold(grad)
            inputs_grad[at, :] = hidden_grad[at, :] + norm_back(grad, hat, inverse, gain[...])

        row_blocks(rows, 32, end)


def shape(dims, kind=BF16):
    return jax.ShapeDtypeStruct(dims, kind)


def once(dims):
    return pl.BlockSpec(dims, lambda *_: (0,) * len(dims), pipeline_mode=pl.Buffered(1))


ELSEWHERE = pl.BlockSpec(memory_space=pl.ANY)
SCALARS = pl.BlockSpec(memory_space=pltpu.SMEM)
LIMIT = 63 * 2**20


OFFSETS = (0, 1, 2)


def feed_width(halves):
    return max(PAIR, 512 // halves)


def forward(lengths, x, gain, shift, merge_bias, gain_2, shift_2, heads_bias, expand_bias, parts):
    rows, width = x.shape
    halves, columns = lax.axis_size("tensor"), parts[0].shape[2]
    groups, images = columns // PAIR, rows // SLOTS
    attention_steps = groups * images
    feed_columns = feed_width(halves)
    feed_steps = parts[2].shape[1] // feed_columns
    pieces = len(pieces_of(parts, columns))
    most = max(sizes().values()) - 1
    line = once((1, width))
    group_at = lambda s: lax.min(lax.div(s, images), groups - 1)
    feed_at = lambda s: lax.max(s - attention_steps, 0)
    wholes = [whole_shape(part) for part in parts]
    saved = pl.BlockSpec((1, rows, halves * feed_columns), lambda s: (feed_at(s), 0, 0))
    return pl.pallas_call(
        partial(forward_kernel, columns, OFFSETS, feed_columns),
        grid=(attention_steps + feed_steps,),
        in_specs=[SCALARS, once((rows, width)), *[line] * 5, *[ELSEWHERE] * 6],
        out_specs=[
            once((width, rows)),
            pl.BlockSpec((1, rows, halves * 3 * PAIR), lambda s: (group_at(s), 0, 0)),
            pl.BlockSpec((1, rows, halves * PAIR), lambda s: (group_at(s), 0, 0)),
            pl.BlockSpec(
                (1, 1, halves, 2 * SLOTS),
                lambda s: (group_at(s), jnp.where(s < attention_steps, lax.rem(s, images), images - 1), 0, 0),
            ),
            once((rows, width)), once((rows, width)), once((width, rows)), saved, saved,
            *[ELSEWHERE] * 4,
        ],
        out_shape=[
            shape((width, rows)),
            shape((groups, rows, halves * 3 * PAIR)),
            shape((groups, rows, halves * PAIR)),
            shape((groups, images, halves, 2 * SLOTS), F32),
            shape((rows, width), F32), shape((rows, width)), shape((width, rows)),
            *[shape((feed_steps, rows, halves * feed_columns))] * 2,
            *[shape(dims) for dims in wholes],
        ],
        scratch_shapes=[
            pltpu.VMEM((rows, width), BF16),
            pltpu.VMEM(wholes[0], BF16),
            pltpu.VMEM(wholes[1], BF16),
            pltpu.VMEM((2, *wholes[2][:-1], feed_columns), BF16),
            pltpu.VMEM((halves, *heads_bias.shape), F32),
            pltpu.VMEM((halves, *expand_bias.shape), F32),
            pltpu.SemaphoreType.DMA((pieces, 2, 4, most)),
            pltpu.SemaphoreType.DMA((pieces, 2, 4, most)),
            pltpu.SemaphoreType.DMA((pieces,)),
            pltpu.SemaphoreType.DMA((2, halves)),
            pltpu.SemaphoreType.DMA((2, halves)),
            pltpu.SemaphoreType.DMA((2,)),
            pltpu.SemaphoreType.DMA((4,)),
            pltpu.SemaphoreType.DMA((2,)),
        ],
        compiler_params=pltpu.CompilerParams(
            vmem_limit_bytes=LIMIT, collective_id=0, has_side_effects=True
        ),
        name="forward",
    )(lengths, x, gain, shift, merge_bias, gain_2, shift_2, heads_bias, expand_bias, *parts)


def feed(lengths, count, activ, hidden, reduce, reduce_bias, teacher):
    rows, width = hidden.shape
    halves, _, wide = reduce.shape
    steps, columns = activ.shape[0], activ.shape[2] // halves
    whole = once((rows, width))
    return pl.pallas_call(
        feed_kernel,
        grid=(steps,),
        in_specs=[
            SCALARS, SCALARS, pl.BlockSpec((1, rows, halves * columns), lambda j: (j, 0, 0)), whole,
            pl.BlockSpec((halves, width, columns), lambda j: (0, 0, j)), once((1, width)), whole,
        ],
        out_specs=[whole, whole, whole, once((width, rows)), once((8, width)), once((8, width))],
        out_shape=[
            shape((rows, width)), shape((rows, width), F32), shape((rows, width)), shape((width, rows)),
            shape((8, width), F32), shape((8, width), F32),
        ],
        scratch_shapes=[pltpu.VMEM((rows, width), F32)],
        compiler_params=pltpu.CompilerParams(vmem_limit_bytes=LIMIT),
        cost_estimate=pl.CostEstimate(
            flops=2 * rows * width * halves * wide,
            bytes_accessed=2 * rows * halves * wide + 2 * width * halves * wide + 20 * rows * width,
            transcendentals=0,
        ),
        name="feed",
    )(lengths, count, activ, hidden, reduce, reduce_bias, teacher)


def feed_back(result_b, result_turned, second_turned, expand, reduce, activ, slope, hidden, result_grad, gain):
    rows, width = result_b.shape
    halves, _, wide = expand.shape
    steps, columns = activ.shape[0], activ.shape[2] // halves
    tile = pl.BlockSpec((halves, width, columns), lambda j: (0, 0, j))
    saved = pl.BlockSpec((1, rows, halves * columns), lambda j: (j, 0, 0))
    whole, turned = once((rows, width)), once((width, rows))
    return pl.pallas_call(
        feed_back_kernel,
        grid=(steps,),
        in_specs=[whole, turned, turned, tile, tile, saved, saved, whole, whole, once((1, width))],
        out_specs=[
            tile, tile, pl.BlockSpec((1, 1, halves * columns), lambda j: (j, 0, 0)),
            whole, whole, turned, once((3, 8, width)),
        ],
        out_shape=[
            shape(expand.shape), shape(expand.shape), shape((steps, 1, halves * columns), F32),
            shape((rows, width), F32), shape((rows, width)), shape((width, rows)), shape((3, 8, width), F32),
        ],
        scratch_shapes=[pltpu.VMEM((rows, width), F32)],
        compiler_params=pltpu.CompilerParams(vmem_limit_bytes=LIMIT),
        cost_estimate=pl.CostEstimate(
            flops=8 * rows * width * halves * wide,
            bytes_accessed=4 * rows * halves * wide + 8 * width * halves * wide, transcendentals=0,
        ),
        name="feed_back",
    )(result_b, result_turned, second_turned, expand, reduce, activ, slope, hidden, result_grad, gain)


def attend_back(
    lengths, a_turned, hidden_b, hidden_turned, qkv, mixed, log_total, x, hidden_grad, gain,
    qkv_weight, merge_weight,
):
    rows, width = x.shape
    halves, columns = qkv_weight.shape[1], qkv_weight.shape[3]
    groups, images = columns // PAIR, rows // SLOTS
    whole, turned = once((rows, width)), once((width, rows))
    return pl.pallas_call(
        attend_back_kernel,
        grid=(groups, images),
        in_specs=[
            SCALARS, turned, whole, turned,
            pl.BlockSpec((1, rows, halves * 3 * PAIR), lambda c, i: (c, 0, 0)),
            pl.BlockSpec((1, rows, halves * PAIR), lambda c, i: (c, 0, 0)),
            pl.BlockSpec((1, 1, halves, 2 * SLOTS), lambda c, i: (c, i, 0, 0)),
            whole, whole, once((1, width)), ELSEWHERE, ELSEWHERE,
        ],
        out_specs=[
            pl.BlockSpec((halves, width, PAIR), lambda c, i: (0, 0, c)),
            pl.BlockSpec((3, halves, width, PAIR), lambda c, i: (0, 0, 0, c)),
            pl.BlockSpec((1, 1, halves * 3 * PAIR), lambda c, i: (c, 0, 0)),
            whole, once((2, 8, width)),
        ],
        out_shape=[
            shape(merge_weight.shape), shape(qkv_weight.shape),
            shape((groups, 1, halves * 3 * PAIR), F32), shape((rows, width), F32), shape((2, 8, width), F32),
        ],
        scratch_shapes=[
            pltpu.VMEM((rows, halves * PAIR), BF16),
            pltpu.VMEM((rows, halves * 3 * PAIR), BF16),
            pltpu.VMEM((rows, width), F32),
            pltpu.VMEM(qkv_weight.shape, BF16),
            pltpu.VMEM(merge_weight.shape, BF16),
            pltpu.SemaphoreType.DMA((2,)),
        ],
        compiler_params=pltpu.CompilerParams(vmem_limit_bytes=LIMIT),
        cost_estimate=pl.CostEstimate(
            flops=16 * rows * width * width + 40 * rows * SLOTS * width,
            bytes_accessed=40 * rows * width, transcendentals=rows * SLOTS * width // HD,
        ),
        name="attend_back",
    )(lengths, a_turned, hidden_b, hidden_turned, qkv, mixed, log_total, x, hidden_grad, gain,
      qkv_weight, merge_weight)


def body(
    inputs,
    teacher,
    lengths,
    first_gain,
    first_shift,
    query_key_value_weight,
    heads_bias,
    merge_weight,
    merge_bias,
    second_gain,
    second_shift,
    expand_weight,
    expand_bias,
    reduce_weight,
    reduce_bias,
):
    rows, width = inputs.shape
    images = rows // SLOTS
    halves = lax.axis_size("tensor")
    tensor = lax.axis_index("tensor")
    hidden = expand_weight.shape[1] * halves
    piece_width = query_key_value_weight.shape[-1]
    groups = piece_width // PAIR
    place = lax.axis_index("dp") * halves + tensor
    mine = lax.dynamic_slice_in_dim(lengths, place * images, images)
    count = jnp.sum(lengths).astype(F32)
    line = lambda vector: vector.reshape(1, width)

    a_turned, qkv, mixed, log_total, hidden_state, _, second_turned, activ, slope, *wholes = forward(
        mine, inputs, line(first_gain), line(first_shift), line(merge_bias), line(second_gain),
        line(second_shift), heads_bias, expand_bias.reshape(1, -1),
        [query_key_value_weight, merge_weight, expand_weight, reduce_weight],
    )
    qkv_full = wholes[0].reshape(3, halves, width, -1)
    merge_full, expand_full, reduce_full = (whole.reshape(halves, width, -1) for whole in wholes[1:])
    columns = feed_width(halves)
    steps = hidden // halves // columns
    outputs, result_grad, result_b, result_turned, reduce_bias_grad, loss = feed(
        mine, count.reshape(1), activ, hidden_state, reduce_full, line(reduce_bias), teacher
    )
    reduce_grad, expand_grad, expand_bias_grad, hidden_grad, hidden_b, hidden_turned, second_sums = feed_back(
        result_b, result_turned, second_turned, expand_full, reduce_full, activ, slope, hidden_state,
        result_grad, line(second_gain),
    )
    reduce_grad = lax.psum_scatter(
        reduce_grad.reshape(halves * width, -1), EVERY, scatter_dimension=0, tiled=True
    ).astype(F32)
    merge_grad, heads_grad, bias_grad, inputs_grad, first_sums = attend_back(
        mine, a_turned, hidden_b, hidden_turned, qkv, mixed, log_total, inputs, hidden_grad,
        line(first_gain), qkv_full, merge_full,
    )
    bias_grad = jnp.moveaxis(bias_grad.reshape(groups, halves, 3, PAIR), 0, 2).reshape(halves, 3, -1)
    expand_bias_grad = jnp.moveaxis(expand_bias_grad.reshape(steps, halves, columns), 0, 1)
    sums = jnp.sum(jnp.concatenate([first_sums, second_sums, reduce_bias_grad[None]]), axis=1)
    small = jnp.concatenate(
        [
            sums.reshape(-1),
            bias_grad[:, 0].reshape(-1),
            bias_grad[:, 2].reshape(-1),
            expand_bias_grad.reshape(-1),
            jnp.sum(loss).reshape(1),
        ]
    )
    length = small.shape[0]
    small = jnp.pad(small, (0, -length % 1024)).reshape(-1, 128)
    size = sizes()
    places = tuple(size[a] for a in AXES)
    heads_grad, merge_grad, expand_grad, small = scatter(
        [
            heads_grad.reshape(3, *places, -1, piece_width),
            merge_grad.reshape(*places, -1, piece_width),
            expand_grad.reshape(*places, -1, hidden // halves),
        ],
        small, 1, piece_width, (), 1,
    )
    small = small.reshape(-1)
    vectors = small[: 6 * width].reshape(6, width)
    heads_bias_sum = lax.dynamic_slice_in_dim(
        small[6 * width : 8 * width].reshape(2, width), tensor * piece_width, piece_width, 1
    )
    expand_bias_sum = lax.dynamic_slice_in_dim(
        small, 8 * width + tensor * (hidden // halves), hidden // halves
    )
    return (
        small[length - 1] / count,
        outputs,
        inputs_grad,
        vectors[0],
        vectors[1],
        heads_grad,
        heads_bias_sum,
        merge_grad,
        vectors[4],
        vectors[2],
        vectors[3],
        expand_grad,
        expand_bias_sum,
        reduce_grad,
        vectors[5],
    )


def solution(mesh):
    return jax.shard_map(
        body,
        mesh=mesh,
        in_specs=(
            P(("dp", "tensor"), None),
            P(("dp", "tensor"), None),
            P(),
            P(),
            P(),
            P(None, "dp", "tensor"),
            P(None, "tensor"),
            P("dp", "tensor"),
            P(),
            P(),
            P(),
            P("dp", "tensor"),
            P("tensor"),
            P("dp", "tensor"),
            P(),
        ),
        out_specs=(
            P(),
            P(("dp", "tensor"), None),
            P(("dp", "tensor"), None),
            P(),
            P(),
            P(None, "dp", "tensor"),
            P(None, "tensor"),
            P("dp", "tensor"),
            P(),
            P(),
            P(),
            P("dp", "tensor"),
            P("tensor"),
            P("dp", "tensor"),
            P(),
        ),
        check_vma=False,
    )
```

time: 624 us -> 497 us (0.80)
  matrix products: 197 us -> 0 us
  Pallas kernels: 285 us -> 461 us
  local copies, waits for them, and re-layouts: 80.5 us -> 13.6 us
  other arithmetic: 38.2 us -> 4.61 us
    dot_general x12 -> x0, matrix products: 197 us -> none  [the longest x1 43.6 us: body(): jnp.einsum('rd,jdf->rjf', result_grad_b, reduce_full, preferred_element_t...]
    pallas_call x3 -> x4, Pallas kernels: 188 us -> 337 us  [the longest x1 162 us: forward(): pl.pallas_call(partial(forward_kernel, columns, OFFSETS, feed_columns), g...]
    pallas_call x1, Pallas kernels: 96.2 us -> 123 us  [scatter(): pl.pallas_call(partial(scatter_kernel, pieces, width, orders, lag, len(gr...]
    unnamed x101 -> x19, local copies, waits for them, and re-layouts: 28.2 us -> 5.26 us
    reshape x3 -> x2, local copies, waits for them, and re-layouts: 21.7 us -> 0.03 us  [the longest x1 0.02 us: body(): jnp.moveaxis(bias_grad.reshape(groups, halves, 3, PAIR), 0, 2)]
    reduce_sum x8 -> x2, other arithmetic: 22.5 us -> 1.5 us  [the longest x1 0.89 us: body(): jnp.sum(jnp.concatenate([first_sums, second_sums, reduce_bias_grad[None]]...]
    dot_general x2 -> x0, local copies, waits for them, and re-layouts: 12 us -> none  [the longest x1 6.03 us: body(): jnp.einsum('mejx,mjwx->ew', qkv_grad, qkv_full, preferred_element_type=F32)]
    convert_element_type x3 -> x0, local copies, waits for them, and re-layouts: 11.5 us -> none  [the longest x1 8.82 us: body(): jnp.einsum('rb,mrjx->mjbx', normed, qkv_grad, preferred_element_type=F32)]
  transfers between devices with their start and end apart: 2 -> 1, of which waited for: 0 -> 0; matrix products, arithmetic and copies ran while one was open for 35% -> 2% of each run, Pallas kernels for 46% -> 40%
where the time goes in v3:
time: 497 us; the launch traced here: 496 us
  Pallas kernels  461 us (93%)
  between operations  16.7 us (3%)
  local copies, waits for them, and re-layouts  13.6 us (3%)
    pallas_call x1, Pallas kernels, forward(): pl.pallas_call(partial(forward_kernel, columns, OFFSETS, feed_columns), g...  162 us
    pallas_call x1, Pallas kernels, scatter(): pl.pallas_call(partial(scatter_kernel, pieces, width, orders, lag, len(gr...  123 us
    pallas_call x1, Pallas kernels, attend_back(): pl.pallas_call(attend_back_kernel, grid=(groups, images), in_specs=[SCALA...  75.2 us
    pallas_call x1, Pallas kernels, feed_back(): pl.pallas_call(feed_back_kernel, grid=(steps,), in_specs=[whole, turned,...  74 us
    pallas_call x1, Pallas kernels, feed(): pl.pallas_call(feed_kernel, grid=(steps,), in_specs=[SCALARS, SCALARS, pl...  26 us
  transfers between devices with their start and end apart: 1, of which 0 were waited for; matrix products, arithmetic and copies ran while one was open for 2% of the time, Pallas kernels for 40%

profile of v3, /device:TPU:0, one launch (start us, length us, event | category | flops | bytes accessed | tf_op | source)
XLA Modules:
  0.0 495.8 jit_solution(15570824557709488422)
XLA Ops:
  7.2 0.0 reduce-scatter.2.cloned.1.call-start
  7.2 1.3 reduce_sum.27
  9.2 1.2 dynamic_slice.9.lengths
  10.4 162.4 %forward.1 = (bf16[1024,1280]{1,0:T(8,128)(2,1)}, bf16[4,1280,768]{2,1,0:T(8,128)(2,1)}, bf16[4,1280,256]{2,1,0:T(8,128)(2,1)}, f32[4,4,2,640]{3,2,1,0:T(2,128)}...) custom-call(s32[4]{0:T(128)} %dynamic_slice.9.lengths, ...), custom_call_target="tpu_custom_call" | custom-call | tf_op jit(solution)/shard_map/forward/pallas_call | solution.py:845
  172.8 26.0 %feed.1 = (bf16[1280,1024]{1,0:T(8,128)(2,1)}, f32[1280,1024]{1,0:T(8,128)}, bf16[1280,1024]{1,0:T(8,128)(2,1)}, bf16[1024,1280]{1,0:T(8,128)(2,1)}, f32[8,1024]{1,0:T(8,128)}, /*index=5*/f32[8,1024]{1,0:T(8,128)}) custom-call(s32[4]{0:T(128)} %dynamic_slice.9.lengths, f32[1]{0:T(128)} %bitcast.6.count, bf16[8,1280,512]{2,1,0:T(8,128)(2,1)} %get-tuple-element.50.activ, ...), custom_call_target="tpu_custom_call" | custom-call | flops 10737418240 | bytes 45088768 | tf_op jit(solution)/shard_map/feed/pallas_call | solution.py:897
  198.8 74.0 %feed_back.1 = (bf16[2,1024,2048]{2,1,0:T(8,128)(2,1)}, bf16[2,1024,2048]{2,1,0:T(8,128)(2,1)}, f32[8,1,512]{2,1,0:T(1,128)}, f32[1280,1024]{1,0:T(8,128)}, bf16...) custom-call(bf16[1280,1024]{1,0:T(8,128)(2,1)} %get-tuple-element.53.result_b, ...), custom_call_target="tpu_custom_call" | custom-call | flops 42949672960 | bytes 54525952 | tf_op jit(solution)/shard_map/feed_back/pallas_call | solution.py:927
  272.7 0.0 reduce-scatter.2.cloned.1.call-update
  272.8 0.0 copy-start
  272.8 0.0 copy-start.1
  272.8 0.0 copy-start.3
  272.8 0.0 copy-start.2
  272.8 75.2 %attend_back.1 = (bf16[2,1024,512]{2,1,0:T(8,128)(2,1)}, bf16[3,2,1024,512]{3,2,1,0:T(8,128)(2,1)}, f32[4,1,768]{2,1,0:T(1,128)}, f32[1280,1024]{1,0:T(8,128)}, f32[2,8,1024]{2,1,0:T(8,128)}) custom-call(s32[4]{0:T(128)} %dynamic_slice.9.lengths, bf16[1024,1280]{1,0:T(8,128)(2,1)} %get-tuple-element.49.a_turned, ...), custom_call_target="tpu_custom_call" | custom-call | flops 38252052480 | bytes 52428800 | tf_op jit(solution)/shard_map/attend_back/pallas_call | solution.py:957
  348.0 0.0 copy-done
  348.0 0.0 copy-done.1
  348.0 0.9 maximum_reduce_fusion
  348.9 0.7 copy.30
  349.7 0.0 copy-done.3
  349.8 0.0 copy-done.2
  349.8 0.6 reduce_sum.29
  350.4 0.6 constant_dynamic-update-slice_fusion
  351.1 0.6 pad_bitcast_fusion.refs_3_
  351.7 123.3 %scatter.1 = (f32[3,64,512]{2,1,0:T(8,128)}, f32[64,512]{1,0:T(8,128)}, f32[64,2048]{1,0:T(8,128)}, f32[104,128]{1,0:T(8,128)}) custom-call(bf16[3,2,4,2,2,64,512]{6,5,4,3,2,1,0:T(8,128)(2,1)} %bitcast.54, bf16[2,4,2,2,64,512]{5,4,3,2,1,0:T(8,128)(2,1)} %bitcast.55, bf16[2,4,2,2,64,2048]{5,4,3,2,1,0:T(8,128)(2,1)} %bitcast.53, ...), custom_call_target="tpu_custom_call" | custom-call | tf_op jit(solution)/shard_map/scatter/pallas_call | solution.py:353
  475.1 0.7 slice.50
  475.8 1.2 slice.57
  477.6 1.3 dynamic_slice.11
  478.9 0.6 constant_dynamic-slice_fusion
  479.5 1.3 slice_bitcast_fusion.2
  480.8 0.0 reduce-scatter.2.cloned.1.call-done
  480.8 1.8 convert_element_type.9
  482.6 1.8 copy.43
  484.4 1.6 copy.44
  486.0 1.9 copy.45
  (13 shorter events, 0.1 us)
Async XLA Ops:
  7.2 473.7 %reduce-scatter.2.cloned.1.call-start = ((), (), s32[]{:S(2)}) async-start(), calls=%async_computation.1 | async-start | bytes 8650752 | tf_op jit(solution)/shard_map/reduce_scatter | solution.py:1040
  272.8 75.2 %copy-start = (f32[3,8,1024]{2,1,0:T(8,128)S(1)}, f32[3,8,1024]{2,1,0:T(8,128)}, u32[]{:S(2)}) copy-start(f32[3,8,1024]{2,1,0:T(8,128)} %get-tuple-element.71) | copy-start | bytes 294916
  272.8 75.2 %copy-start.1 = (f32[8,1024]{1,0:T(8,128)S(1)}, f32[8,1024]{1,0:T(8,128)}, u32[]{:S(2)}) copy-start(f32[8,1024]{1,0:T(8,128)} %get-tuple-element.72) | copy-start | bytes 98308
  272.8 76.9 %copy-start.3 = (f32[8,1,512]{2,1,0:T(1,128)S(1)}, f32[8,1,512]{2,1,0:T(1,128)}, u32[]{:S(2)}) copy-start(f32[8,1,512]{2,1,0:T(1,128)} %get-tuple-element.74) | copy-start | bytes 49156
  272.8 77.0 %copy-start.2 = (f32[8,1024]{1,0:T(8,128)S(1)}, f32[8,1024]{1,0:T(8,128)}, u32[]{:S(2)}) copy-start(f32[8,1024]{1,0:T(8,128)} %get-tuple-element.75) | copy-start | bytes 98308
Sparse Core Ops, SparseCore 0:
  272.9 157.8 reduce-scatter.1

commit v4 on v3

--- a/solution.py
+++ b/solution.py
@@ -3,6 +3,7 @@
 
 import jax
 import jax.numpy as jnp
+import numpy as np
 from jax import lax
 from jax.experimental import pallas as pl
 from jax.experimental.pallas import tpu as pltpu
@@ -16,7 +17,6 @@
 MASKED_SCORE = -1e30
 F32 = jnp.float32
 BF16 = jnp.bfloat16
-EVERY = ("tensor", "dp")
 CORES = 2
 LINE = 4
 
@@ -188,189 +188,180 @@
             self.remote(step).wait_send()
 
 
-SCATTER_ORDERS = (
-    (("tensor", "row", "line"), ("row", "tensor", "line")),
-    (("line", "tensor", "row"), ("line", "row", "tensor")),
-)
-SUM_AXES = ("core", "tensor", "row", "line")
-
-
-def scatter_kernel(pieces, width, orders, lag, n_grads, *refs):
-    ins, small = refs[:n_grads], refs[n_grads]
-    outs, small_out = refs[n_grads + 1 : 2 * n_grads + 1], refs[2 * n_grads + 1]
-    own_buf, first_buf, *rest = refs[2 * n_grads + 2 :]
-    count = len(pieces)
-    late = {(n, h, s): rest[(n * 2 + h) * 3 + s - 1] for n in range(count) for h in range(2) for s in (1, 2, 3)}
-    small_bufs = rest[6 * count : 6 * count + 4]
-    send_sem, recv_sem, own_sem, small_send, small_recv = rest[6 * count + 4 :]
-    here = Place()
-    here.greet()
-    half = own_buf.shape[-2] // 2
-    three = AXES[:3]
-
-    def own(n):
-        source = piece(ins, pieces[n], width).at[:, :, :, here.at["core"]]
-        return pltpu.make_async_copy(source, own_buf.at[n], own_sem.at[n])
-
-    def to_core(n):
+SCATTER_ORDERS = (("tensor", "row", "line"), ("row", "tensor", "line"))
+THREE = AXES[:3]
+
+
+def late_shapes(count, rows, columns):
+    size, out = sizes(), []
+    for order in SCATTER_ORDERS:
+        for stage in (1, 2, 3):
+            free = [size[a] for a in THREE if a not in order[:stage]]
+            out.append((count, size[order[stage - 1]] - 1, *free, rows // 2, columns))
+    return out
+
+
+def scatter_scratch(count, rows, columns):
+    size = sizes()
+    most = max(size.values()) - 1
+    half_piece = (count, *(size[a] for a in THREE), rows, columns)
+    return [
+        pltpu.VMEM(half_piece, BF16),
+        pltpu.VMEM(half_piece, BF16),
+        *[pltpu.VMEM(dims, BF16) for dims in late_shapes(count, rows, columns)],
+        pltpu.SemaphoreType.DMA((count, 2, 4, most)),
+        pltpu.SemaphoreType.DMA((count, 2, 4, most)),
+    ]
+
+
+SCATTER_REFS = 10
+
+
+def plus(terms):
+    if len(terms) == 2:
+        return terms[0] + terms[1]
+    return sum(term.astype(F32) for term in terms).astype(BF16)
+
+
+class Scatter:
+    def __init__(self, here, staging, out, refs):
+        self.here, self.staging, self.out = here, staging, out
+        self.own, self.first, *late, self.send_sem, self.recv_sem = refs
+        self.late = {(h, s): late[h * 3 + s - 1] for h in range(2) for s in (1, 2, 3)}
+        self.half = self.own.shape[-2] // 2
+
+    def to_core(self, n):
+        here = self.here
         other = here.peer("core", 1)
         return pltpu.make_async_remote_copy(
-            src_ref=piece(ins, pieces[n], width).at[:, :, :, other], dst_ref=first_buf.at[n],
-            send_sem=send_sem.at[n, 0, 0, 0], recv_sem=recv_sem.at[n, 0, 0, 0],
+            src_ref=self.staging(n).at[:, :, :, other], dst_ref=self.first.at[n],
+            send_sem=self.send_sem.at[n, 0, 0, 0], recv_sem=self.recv_sem.at[n, 0, 0, 0],
             device_id=here.device("core", other), device_id_type=MESH,
         )
 
-    def remote(n, h, stage, step):
-        order = orders[n][h]
+    def remote(self, n, h, stage, step):
+        here, order = self.here, SCATTER_ORDERS[h]
         axis = order[stage - 1]
         to = here.peer(axis, step)
         index = [
-            here.at[a] if a in order[: stage - 1] else to if a == axis else slice(None) for a in three
+            here.at[a] if a in order[: stage - 1] else to if a == axis else slice(None) for a in THREE
         ]
         slot = (n, h, stage, step - 1)
         return pltpu.make_async_remote_copy(
-            src_ref=own_buf.at[(n, *index, pl.ds(h * half, half))],
-            dst_ref=late[n, h, stage].at[step - 1],
-            send_sem=send_sem.at[slot], recv_sem=recv_sem.at[slot],
+            src_ref=self.own.at[(n, *index, pl.ds(h * self.half, self.half))],
+            dst_ref=self.late[h, stage].at[n, step - 1],
+            send_sem=self.send_sem.at[slot], recv_sem=self.recv_sem.at[slot],
             device_id=here.device(axis, to), device_id_type=MESH,
         )
 
-    def every(n, stage, act):
-        for h in range(2):
-            for step in here.steps(orders[n][h][stage - 1]):
-                act(remote(n, h, stage, step))
-
-    def add_core(n):
-        def one(i, _):
-            first, left = lax.div(i, here.size["row"]), lax.rem(i, here.size["row"])
-            at = (n, lax.div(first, LINE), lax.rem(first, LINE), left)
-            own_buf[at] = (own_buf[at].astype(F32) + first_buf[at].astype(F32)).astype(BF16)
+    def every(self, n, stage):
+        return [
+            self.remote(n, h, stage, step)
+            for h in range(2)
+            for step in self.here.steps(SCATTER_ORDERS[h][stage - 1])
+        ]
+
+    def add_core(self, n):
+        source, core = self.staging(n), self.here.at["core"]
+        for at in np.ndindex(self.own.shape[1:3]):
+            self.own[(n, *at)] = plus([source[(*at, slice(None), core)], self.first[(n, *at)]])
+
+    def add(self, n, h, stage):
+        here, order = self.here, SCATTER_ORDERS[h]
+        buf, steps = self.late[h, stage], here.size[order[stage - 1]] - 1
+        free = [a for a in THREE if a not in order[:stage]]
+        rows = pl.ds(h * self.half, self.half)
+        for free_at in np.ndindex(*(here.size[a] for a in free)):
+            at = {**here.at, **dict(zip(free, free_at, strict=True))}
+            mine = (n, *(at[a] for a in THREE), rows)
+            terms = [self.own[mine]] + [buf[(n, s, *free_at)] for s in range(steps)]
+            if stage == 3:
+                self.out(n)[rows, :] = sum(term.astype(F32) for term in terms)
+            else:
+                self.own[mine] = plus(terms)
+
+    def begin(self, n):
+        self.to_core(n).start()
+
+    def tick(self, n, stage):
+        if stage == 0:
+            copy = self.to_core(n)
+            copy.wait_recv()
+            copy.wait_send()
+            self.add_core(n)
+        else:
+            for copy in self.every(n, stage):
+                copy.wait_recv()
+            for h in range(2):
+                self.add(n, h, stage)
+        if stage < 3:
+            for copy in self.every(n, stage + 1):
+                copy.start()
+
+    def end(self, count):
+        def one(n, _):
+            for stage in (1, 2, 3):
+                for copy in self.every(n, stage):
+                    copy.wait_send()
             return 0
 
-        lax.fori_loop(0, math.prod(here.size[a] for a in three), one, 0)
-
-    def add(n, h, stage):
-        order = orders[n][h]
-        buf, steps = late[n, h, stage], here.size[order[stage - 1]] - 1
-        free = [a for a in three if a not in order[:stage]]
-        rows = pl.ds(h * half, half)
-
-        def one(i, _):
-            at, left = dict(here.at), i
-            for a in reversed(free):
-                at[a] = lax.rem(left, here.size[a])
-                left = lax.div(left, here.size[a])
-            mine = (n, *(at[a] for a in three), rows)
-            total = own_buf[mine].astype(F32)
-            for s in range(steps):
-                total += buf[(s, *(at[a] for a in free))].astype(F32)
-            if stage == 3:
-                out = piece(outs, pieces[n], width)
-                out[rows, :] = total
-            else:
-                own_buf[mine] = total.astype(BF16)
-            return 0
-
-        if free:
-            lax.fori_loop(0, math.prod(here.size[a] for a in free), one, 0)
-        else:
-            one(0, 0)
-
-    def small_copy(stage, step, coming=False):
-        axis = SUM_AXES[stage]
+        lax.fori_loop(0, count, one, 0)
+
+
+SUM_AXES = ("core", "tensor", "row", "line")
+
+
+class SmallSum:
+    def __init__(self, here, refs):
+        self.here = here
+        *self.bufs, self.send_sem, self.recv_sem = refs
+
+    @staticmethod
+    def scratch(dims):
+        size = sizes()
+        most = max(size.values()) - 1
+        return [
+            *[pltpu.VMEM((size[a], *dims), F32) for a in SUM_AXES],
+            pltpu.SemaphoreType.DMA((4, most)),
+            pltpu.SemaphoreType.DMA((4, most)),
+        ]
+
+    def remote(self, stage, step, coming=False):
+        here, axis, buf = self.here, SUM_AXES[stage], self.bufs[stage]
         place = here.peer(axis, here.size[axis] - step) if coming else here.at[axis]
-        buf = small_bufs[stage]
         return pltpu.make_async_remote_copy(
             src_ref=buf.at[here.at[axis]], dst_ref=buf.at[place],
-            send_sem=small_send.at[stage, step - 1], recv_sem=small_recv.at[stage, step - 1],
+            send_sem=self.send_sem.at[stage, step - 1], recv_sem=self.recv_sem.at[stage, step - 1],
             device_id=here.device(axis, here.peer(axis, step)), device_id_type=MESH,
         )
 
-    def small_start(stage, value):
+    def start(self, stage, value):
+        self.bufs[stage][self.here.at[SUM_AXES[stage]]] = value
+        self.send(stage)
+
+    def send(self, stage):
+        for step in self.here.steps(SUM_AXES[stage]):
+            self.remote(stage, step).start()
+
+    def finish(self, stage):
         axis = SUM_AXES[stage]
-        small_bufs[stage][here.at[axis]] = value
-        for step in here.steps(axis):
-            small_copy(stage, step).start()
-
-    def small_end(stage):
-        axis = SUM_AXES[stage]
-        for step in here.steps(axis):
-            small_copy(stage, step, coming=True).wait_recv()
-            small_copy(stage, step).wait_send()
-        total = small_bufs[stage][0]
-        for place in range(1, here.size[axis]):
-            total += small_bufs[stage][place]
+        for step in self.here.steps(axis):
+            self.remote(stage, step, coming=True).wait_recv()
+            self.remote(stage, step).wait_send()
+        total = self.bufs[stage][0]
+        for place in range(1, self.here.size[axis]):
+            total += self.bufs[stage][place]
         return total
 
-    for n in range(count):
-        to_core(n).start()
-        own(n).start()
-    small_start(0, small[...])
-    for tick in range(max(count + 3 * lag, 5)):
-        if 1 <= tick <= 4:
-            total = small_end(tick - 1)
-            if tick < 4:
-                small_start(tick, total)
-            else:
-                small_out[...] = total
-        for stage in range(4):
-            n = tick - lag * stage
-            if not 0 <= n < count:
-                continue
-            if stage == 0:
-                own(n).wait()
-                to_core(n).wait_recv()
-                add_core(n)
-            else:
-                every(n, stage, lambda copy: copy.wait_recv())
-                for h in range(2):
-                    add(n, h, stage)
-            if stage < 3:
-                every(n, stage + 1, lambda copy: copy.start())
-    for n in range(count):
-        to_core(n).wait_send()
-        for stage in (1, 2, 3):
-            every(n, stage, lambda copy: copy.wait_send())
-
-
-def scatter(grads, small, collective_id, width, third=(), lag=2):
-    size = sizes()
-    shards = [jax.ShapeDtypeStruct((*g.shape[:-6], *g.shape[-2:]), F32) for g in grads]
-    pieces = pieces_of(shards, width)
-    count, most = len(pieces), max(size.values()) - 1
-    orders = [SCATTER_ORDERS[n in third] for n in range(count)]
-    rows = grads[0].shape[-2]
-    three = AXES[:3]
-    whole = (count, *(size[a] for a in three), rows, width)
-    late = []
-    for n in range(count):
-        for h in range(2):
-            for s in (1, 2, 3):
-                order = orders[n][h]
-                free = [size[a] for a in three if a not in order[:s]]
-                late.append(pltpu.VMEM((size[order[s - 1]] - 1, *free, rows // 2, width), BF16))
-    vmem = pl.BlockSpec(memory_space=pltpu.VMEM)
-    return pl.pallas_call(
-        partial(scatter_kernel, pieces, width, orders, lag, len(grads)),
-        out_shape=[*shards, jax.ShapeDtypeStruct(small.shape, small.dtype)],
-        in_specs=[*[pl.BlockSpec(memory_space=pl.ANY)] * len(grads), vmem],
-        out_specs=[vmem] * (len(grads) + 1),
-        scratch_shapes=[
-            pltpu.VMEM(whole, BF16),
-            pltpu.VMEM(whole, BF16),
-            *late,
-            *[pltpu.VMEM((size[a], *small.shape), F32) for a in SUM_AXES],
-            pltpu.SemaphoreType.DMA((count, 2, 4, most)),
-            pltpu.SemaphoreType.DMA((count, 2, 4, most)),
-            pltpu.SemaphoreType.DMA((count,)),
-            pltpu.SemaphoreType.DMA((4, most)),
-            pltpu.SemaphoreType.DMA((4, most)),
-        ],
-        compiler_params=pltpu.CompilerParams(
-            collective_id=collective_id, has_side_effects=True, vmem_limit_bytes=60 * 2**20
-        ),
-        name="scatter",
-    )(*grads, small)
+    def tick(self, stage, target):
+        total = self.finish(stage)
+        if stage < 3:
+            self.start(stage + 1, total)
+        else:
+            target[...] = total
+
+
+SMALL_REFS = 6
 
 
 def dot(left, right, left_dim=1, right_dim=0):
@@ -668,9 +659,9 @@
             result = jnp.where(valid, hidden[at, :] + total[at, :] + reduce_bias[...], 0.0)
             out[at, :] = result.astype(BF16)
             error = jnp.where(valid, result - teacher[at, :].astype(F32), 0.0)
-            loss[...] += fold(error * error)
+            loss[0] += fold(error * error)
             back = 2.0 * error / count[0]
-            bias_grad[...] += fold(back)
+            bias_grad[0] += fold(back)
             grad[at, :] = back
             grad_b[at, :] = back.astype(BF16)
 
@@ -680,20 +671,40 @@
 
 def feed_back_kernel(
     result_b, result_turned, second_turned, expand, reduce, activ, slope, hidden, result_grad, gain,
-    reduce_grad, expand_grad, expand_bias_grad, hidden_grad, hidden_b, hidden_turned, sums, total,
+    reduce_grad, expand_grad, expand_bias_grad, hidden_grad, hidden_b, hidden_turned, sums,
+    total, staging, *scatter_refs,
 ):
-    step = pl.program_id(0)
-    rows = result_b.shape[0]
-    halves, width, columns = expand.shape
+    step, steps = pl.program_id(0), reduce_grad.shape[1] // expand.shape[-1]
+    rows, width = result_b.shape
+    halves, _, columns = expand.shape
     expand_tile, reduce_tile = side_by_side(expand), side_by_side(reduce)
 
+    scatters = []
+    here = Place()
+    for p, target in enumerate((reduce_grad, expand_grad)):
+        slot = lambda j, p=p: staging.at[lax.rem(j, 2), p]
+        part = lambda j, target=target: target.at[:, pl.ds(pl.multiple_of(j * columns, columns), columns)]
+        scatters.append(Scatter(here, slot, part, scatter_refs[p * SCATTER_REFS : (p + 1) * SCATTER_REFS]))
+
     @pl.when(step == 0)
     def _():
+        here.greet()
         total[...] = jnp.zeros_like(total)
 
-    reduce_part = dot(result_turned[...], activ[0])
-    for t in range(halves):
-        reduce_grad[t] = reduce_part[:, t * columns : (t + 1) * columns].astype(BF16)
+    for stage in range(3, -1, -1):
+
+        @pl.when(step >= stage + 1)
+        def _(stage=stage):
+            for scatter in scatters:
+                scatter.tick(step - 1 - stage, stage)
+
+    def stage_out(p, part):
+        for t in range(halves):
+            block = part[:, t * columns : (t + 1) * columns].astype(BF16)
+            staging[lax.rem(step, 2), p, t] = block.reshape(staging.shape[3:])
+        scatters[p].begin(step)
+
+    stage_out(0, dot(result_turned[...], activ[0]))
     bias = jnp.zeros((8, halves * columns), F32)
     parts = []
     for i in range(rows // SLOTS):
@@ -703,40 +714,83 @@
         parts.append(z_grad)
         total[at, :] += dot(z_grad, expand_tile, 1, 1)
     expand_bias_grad[0] = jnp.sum(bias, axis=0, keepdims=True)
-    expand_part = dot(second_turned[...], jnp.concatenate(parts, axis=0))
-    for t in range(halves):
-        expand_grad[t] = expand_part[:, t * columns : (t + 1) * columns].astype(BF16)
-
-    @pl.when(step == pl.num_programs(0) - 1)
+    stage_out(1, dot(second_turned[...], jnp.concatenate(parts, axis=0)))
+
+    @pl.when(step == steps - 1)
     def _():
         sums[...] = jnp.zeros_like(sums)
-
-        def end(_, at):
-            hat, inverse = centred(hidden[at, :])
-            second_grad = total[at, :]
-            back = result_grad[at, :] + norm_back(second_grad, hat, inverse, gain[...])
-            sums[0] += fold(second_grad * hat)
-            sums[1] += fold(second_grad)
-            sums[2] += fold(back)
-            hidden_grad[at, :] = back
-            hidden_b[at, :] = back.astype(BF16)
-
-        row_blocks(rows, 32, end)
-        transpose_into(hidden_b, hidden_turned)
+        size = 128 if rows % 128 == 0 else rows
+        blocks = rows // size
+
+        def end(first, h_ref, g_ref, back_ref, back_b_ref, turned_ref):
+            block = pl.program_id(0) + first
+            for k in range(0, size, 32):
+                at = slice(k, k + 32)
+                hat, inverse = centred(h_ref[at, :])
+                second_grad = total[pl.ds(pl.multiple_of(block * size + k, 32), 32), :]
+                back = g_ref[at, :] + norm_back(second_grad, hat, inverse, gain[...])
+                sums[0] += fold(second_grad * hat)
+                sums[1] += fold(second_grad)
+                sums[2] += fold(back)
+                back_ref[at, :] = back
+                back_b_ref[at, :] = back.astype(BF16)
+            turned_ref[...] = back_ref[...].T.astype(BF16)
+
+        def some(first, last):
+            row_block = pl.BlockSpec((size, width), lambda i: (i + first, 0))
+            pltpu.emit_pipeline(
+                partial(end, first),
+                grid=(last - first,),
+                in_specs=[row_block, row_block],
+                out_specs=[row_block, row_block, pl.BlockSpec((width, size), lambda i: (0, i + first))],
+            )(hidden, result_grad, hidden_grad, hidden_b, hidden_turned)
+
+        bounds = [blocks * k // 3 for k in range(4)]
+        for drain in range(4):
+            for stage in range(3, -1, -1):
+                for scatter in scatters:
+                    if stage >= drain and steps + drain - 1 - stage >= 0:
+                        scatter.tick(steps + drain - 1 - stage, stage)
+            if drain < 3 and bounds[drain + 1] > bounds[drain]:
+                some(bounds[drain], bounds[drain + 1])
+        for scatter in scatters:
+            scatter.end(steps)
 
 
 def attend_back_kernel(
     lengths, a_turned, hidden_b, hidden_turned, qkv_ref, mixed_ref, log_ref, x_ref, hidden_grad, gain,
-    qkv_weight, merge_weight,
-    merge_grad, qkv_grad, bias_grad, inputs_grad, sums,
-    mixed_grad, heads_grad, total, qkv_held, merge_held, sem,
+    qkv_weight, merge_weight, second_sums, reduce_bias_grad, loss, expand_bias_grad,
+    merge_grad, qkv_grad, inputs_grad, early_out, expand_out, late_out, heads_out,
+    mixed_grad, heads_grad, total, qkv_held, merge_held, sem, merge_staging, qkv_staging, sums, bias_grad,
+    *comm,
 ):
-    group, image = pl.program_id(0), pl.program_id(1)
+    now = pl.program_id(0)
     rows = x_ref.shape[0]
+    images = rows // SLOTS
     halves = qkv_held.shape[1]
+    groups = merge_grad.shape[1] // PAIR
+    steps = groups * images
+    group, image = lax.div(now, images), lax.rem(now, images)
+    here = Place()
+    block = lambda c: pl.ds(pl.multiple_of(c * PAIR, PAIR), PAIR)
+    merge_scatter = Scatter(here, lambda n: merge_staging, lambda n: merge_grad.at[:, block(n)], comm[:SCATTER_REFS])
+    qkv_scatter = Scatter(
+        here, lambda n: qkv_staging.at[lax.rem(n, 3)],
+        lambda n: qkv_grad.at[lax.rem(n, 3), :, block(lax.div(n, 3))], comm[SCATTER_REFS : 2 * SCATTER_REFS],
+    )
+    early, expand_sum, late, heads_sum = (
+        SmallSum(here, comm[2 * SCATTER_REFS + k * SMALL_REFS :][:SMALL_REFS]) for k in range(4)
+    )
+
+    def merge_tick(c, stage):
+        merge_scatter.tick(c, stage)
+
+    def qkv_tick(c, stage):
+        for e in range(3):
+            qkv_scatter.tick(3 * c + e, stage)
     columns = pl.ds(pl.multiple_of(group * PAIR, PAIR), PAIR)
 
-    @pl.when((group == 0) & (image == 0))
+    @pl.when(now == 0)
     def _():
         copies = [
             pltpu.make_async_copy(merge_weight, merge_held, sem.at[1]),
@@ -744,9 +798,31 @@
         ]
         for copy in copies:
             copy.start()
+        here.greet()
         total[...] = jnp.zeros_like(total)
+        rowsum = lambda ref, k: jnp.sum(ref[k], axis=0, keepdims=True)
+        vectors = [rowsum(second_sums, k) for k in range(3)] + [rowsum(reduce_bias_grad, 0)]
+        lost = jnp.sum(rowsum(loss, 0), axis=1, keepdims=True)
+        vectors.append(jnp.broadcast_to(lost, vectors[0].shape))
+        early.start(0, jnp.concatenate(vectors, axis=0))
+        expand_sum.start(0, expand_bias_grad[:, 0])
         for copy in copies:
             copy.wait()
+
+    for stage in range(4):
+
+        @pl.when(now == min(stage + 1, steps - 1))
+        def _(stage=stage):
+            early.tick(stage, early_out)
+            expand_sum.tick(stage, expand_out)
+
+    for stage in range(3, -1, -1):
+        for ready, tick in ((0, merge_tick), (images - 1, qkv_tick)):
+            since = now - 1 - stage - ready
+
+            @pl.when((since >= 0) & (lax.rem(since, images) == 0))
+            def _(stage=stage, tick=tick, since=since):
+                tick(lax.div(since, images), stage)
 
     @pl.when(image == 0)
     def _():
@@ -756,7 +832,8 @@
             mixed_grad[part, :] = dot(hidden_b[part, :], weight).astype(BF16)
         part = dot(hidden_turned[...], mixed_ref[0]).astype(BF16)
         for t in range(halves):
-            merge_grad[t] = part[:, t * PAIR : (t + 1) * PAIR]
+            merge_staging[t] = part[:, t * PAIR : (t + 1) * PAIR].reshape(merge_staging.shape[1:])
+        merge_scatter.begin(group)
 
     length = lengths[image]
     at = pl.ds(pl.multiple_of(image * SLOTS, SLOTS), SLOTS)
@@ -779,33 +856,64 @@
         heads_grad[at, first + PAIR : first + 2 * PAIR] = key_grad
         heads_grad[at, first + 2 * PAIR : first + 3 * PAIR] = value_grad
 
-    @pl.when(image == pl.num_programs(1) - 1)
+    @pl.when(image == images - 1)
     def _():
         weight = group_weight(qkv_held, columns)
         bias = jnp.zeros((8, halves * 3 * PAIR), F32)
         for i in range(rows // SLOTS):
             part = slice(i * SLOTS, (i + 1) * SLOTS)
-            total[part, :] += dot(heads_grad[part, :], weight, 1, 1)
             bias += fold(heads_grad[part, :].astype(F32))
-        bias_grad[0] = jnp.sum(bias, axis=0, keepdims=True)
+        bias_grad[pl.ds(group, 1), :] = jnp.sum(bias, axis=0, keepdims=True)
         part = dot(a_turned[...], heads_grad[...]).astype(BF16)
         for t in range(halves):
             for e in range(3):
                 first = (t * 3 + e) * PAIR
-                qkv_grad[e, t] = part[:, first : first + PAIR]
-
-    @pl.when((image == pl.num_programs(1) - 1) & (group == pl.num_programs(0) - 1))
-    def _():
+                qkv_staging[e, t] = part[:, first : first + PAIR].reshape(qkv_staging.shape[2:])
+        for e in range(3):
+            qkv_scatter.begin(3 * group + e)
+        for i in range(rows // SLOTS):
+            part = slice(i * SLOTS, (i + 1) * SLOTS)
+            total[part, :] += dot(heads_grad[part, :], weight, 1, 1)
+
+    @pl.when(now == steps - 1)
+    def _():
+        heads_sum.start(0, bias_grad[...])
         sums[...] = jnp.zeros_like(sums)
 
-        def end(_, at):
+        def end(i, _):
+            at = pl.ds(pl.multiple_of(i * 32, 32), 32)
             hat, inverse = centred(x_ref[at, :].astype(F32))
             grad = total[at, :]
             sums[0] += fold(grad * hat)
             sums[1] += fold(grad)
             inputs_grad[at, :] = hidden_grad[at, :] + norm_back(grad, hat, inverse, gain[...])
-
-        row_blocks(rows, 32, end)
+            return 0
+
+        blocks = rows // 32
+
+        def drain(d):
+            for stage in range(3, -1, -1):
+                for ready, tick in ((0, merge_tick), (images - 1, qkv_tick)):
+                    since = steps + d - 1 - stage - ready
+                    if stage >= d and since >= 0 and since % images == 0 and since // images < groups:
+                        tick(since // images, stage)
+
+        drain(0)
+        heads_sum.tick(0, heads_out)
+        lax.fori_loop(0, blocks // 2, end, 0)
+        drain(1)
+        heads_sum.tick(1, heads_out)
+        lax.fori_loop(blocks // 2, blocks, end, 0)
+        late.start(0, jnp.sum(sums[...], axis=1))
+        drain(2)
+        heads_sum.tick(2, heads_out)
+        late.tick(0, late_out)
+        drain(3)
+        heads_sum.tick(3, heads_out)
+        for stage in range(1, 4):
+            late.tick(stage, late_out)
+        merge_scatter.end(groups)
+        qkv_scatter.end(3 * groups)
 
 
 def shape(dims, kind=BF16):
@@ -901,10 +1009,10 @@
             SCALARS, SCALARS, pl.BlockSpec((1, rows, halves * columns), lambda j: (j, 0, 0)), whole,
             pl.BlockSpec((halves, width, columns), lambda j: (0, 0, j)), once((1, width)), whole,
         ],
-        out_specs=[whole, whole, whole, once((width, rows)), once((8, width)), once((8, width))],
+        out_specs=[whole, whole, whole, once((width, rows)), once((1, 8, width)), once((1, 8, width))],
         out_shape=[
             shape((rows, width)), shape((rows, width), F32), shape((rows, width)), shape((width, rows)),
-            shape((8, width), F32), shape((8, width), F32),
+            shape((1, 8, width), F32), shape((1, 8, width), F32),
         ],
         scratch_shapes=[pltpu.VMEM((rows, width), F32)],
         compiler_params=pltpu.CompilerParams(vmem_limit_bytes=LIMIT),
@@ -921,26 +1029,32 @@
     rows, width = result_b.shape
     halves, _, wide = expand.shape
     steps, columns = activ.shape[0], activ.shape[2] // halves
+    size = sizes()
+    part_rows = width // math.prod(size[a] for a in ("line", "row", "core"))
     tile = pl.BlockSpec((halves, width, columns), lambda j: (0, 0, j))
     saved = pl.BlockSpec((1, rows, halves * columns), lambda j: (j, 0, 0))
-    whole, turned = once((rows, width)), once((width, rows))
+    whole, turned, part = once((rows, width)), once((width, rows)), once((part_rows, wide))
     return pl.pallas_call(
         feed_back_kernel,
         grid=(steps,),
-        in_specs=[whole, turned, turned, tile, tile, saved, saved, whole, whole, once((1, width))],
+        in_specs=[whole, turned, turned, tile, tile, saved, saved, ELSEWHERE, ELSEWHERE, once((1, width))],
         out_specs=[
-            tile, tile, pl.BlockSpec((1, 1, halves * columns), lambda j: (j, 0, 0)),
-            whole, whole, turned, once((3, 8, width)),
+            part, part, pl.BlockSpec((1, 1, halves * columns), lambda j: (j, 0, 0)),
+            ELSEWHERE, ELSEWHERE, ELSEWHERE, once((3, 8, width)),
         ],
         out_shape=[
-            shape(expand.shape), shape(expand.shape), shape((steps, 1, halves * columns), F32),
+            shape((part_rows, wide), F32), shape((part_rows, wide), F32),
+            shape((steps, 1, halves * columns), F32),
             shape((rows, width), F32), shape((rows, width)), shape((width, rows)), shape((3, 8, width), F32),
         ],
-        scratch_shapes=[pltpu.VMEM((rows, width), F32)],
-        compiler_params=pltpu.CompilerParams(vmem_limit_bytes=LIMIT),
-        cost_estimate=pl.CostEstimate(
-            flops=8 * rows * width * halves * wide,
-            bytes_accessed=4 * rows * halves * wide + 8 * width * halves * wide, transcendentals=0,
+        scratch_shapes=[
+            pltpu.VMEM((rows, width), F32),
+            pltpu.VMEM((2, 2, *(size[a] for a in AXES), part_rows, columns), BF16),
+            *scatter_scratch(steps, part_rows, columns),
+            *scatter_scratch(steps, part_rows, columns),
+        ],
+        compiler_params=pltpu.CompilerParams(
+            vmem_limit_bytes=LIMIT, collective_id=1, has_side_effects=True
         ),
         name="feed_back",
     )(result_b, result_turned, second_turned, expand, reduce, activ, slope, hidden, result_grad, gain)
@@ -948,48 +1062,58 @@
 
 def attend_back(
     lengths, a_turned, hidden_b, hidden_turned, qkv, mixed, log_total, x, hidden_grad, gain,
-    qkv_weight, merge_weight,
+    qkv_whole, merge_whole, second_sums, reduce_bias_grad, loss, expand_bias_grad,
 ):
     rows, width = x.shape
-    halves, columns = qkv_weight.shape[1], qkv_weight.shape[3]
+    halves, (part_rows, columns) = qkv_whole.shape[1], qkv_whole.shape[-2:]
     groups, images = columns // PAIR, rows // SLOTS
     whole, turned = once((rows, width)), once((width, rows))
+    group_at = lambda s: lax.div(s, images)
+    size = sizes()
+    staging = (*(size[a] for a in AXES), part_rows, PAIR)
+    small = [(5, width), (expand_bias_grad.shape[0], expand_bias_grad.shape[2]), (2, width), (groups, halves * 3 * PAIR)]
+    vmem = lambda array: once(array.shape)
     return pl.pallas_call(
         attend_back_kernel,
-        grid=(groups, images),
+        grid=(groups * images,),
         in_specs=[
             SCALARS, turned, whole, turned,
-            pl.BlockSpec((1, rows, halves * 3 * PAIR), lambda c, i: (c, 0, 0)),
-            pl.BlockSpec((1, rows, halves * PAIR), lambda c, i: (c, 0, 0)),
-            pl.BlockSpec((1, 1, halves, 2 * SLOTS), lambda c, i: (c, i, 0, 0)),
+            pl.BlockSpec((1, rows, halves * 3 * PAIR), lambda s: (group_at(s), 0, 0)),
+            pl.BlockSpec((1, rows, halves * PAIR), lambda s: (group_at(s), 0, 0)),
+            pl.BlockSpec((1, 1, halves, 2 * SLOTS), lambda s: (group_at(s), lax.rem(s, images), 0, 0)),
             whole, whole, once((1, width)), ELSEWHERE, ELSEWHERE,
+            vmem(second_sums), vmem(reduce_bias_grad), vmem(loss), vmem(expand_bias_grad),
         ],
         out_specs=[
-            pl.BlockSpec((halves, width, PAIR), lambda c, i: (0, 0, c)),
-            pl.BlockSpec((3, halves, width, PAIR), lambda c, i: (0, 0, 0, c)),
-            pl.BlockSpec((1, 1, halves * 3 * PAIR), lambda c, i: (c, 0, 0)),
-            whole, once((2, 8, width)),
+            once((part_rows, columns)), once((3, part_rows, columns)), whole, *[once(dims) for dims in small]
         ],
         out_shape=[
-            shape(merge_weight.shape), shape(qkv_weight.shape),
-            shape((groups, 1, halves * 3 * PAIR), F32), shape((rows, width), F32), shape((2, 8, width), F32),
+            shape((part_rows, columns), F32), shape((3, part_rows, columns), F32), shape((rows, width), F32),
+            *[shape(dims, F32) for dims in small],
         ],
         scratch_shapes=[
             pltpu.VMEM((rows, halves * PAIR), BF16),
             pltpu.VMEM((rows, halves * 3 * PAIR), BF16),
             pltpu.VMEM((rows, width), F32),
-            pltpu.VMEM(qkv_weight.shape, BF16),
-            pltpu.VMEM(merge_weight.shape, BF16),
+            pltpu.VMEM(qkv_whole.shape, BF16),
+            pltpu.VMEM(merge_whole.shape, BF16),
             pltpu.SemaphoreType.DMA((2,)),
+            pltpu.VMEM(staging, BF16),
+            pltpu.VMEM((3, *staging), BF16),
+            pltpu.VMEM((2, 8, width), F32),
+            pltpu.VMEM((groups, halves * 3 * PAIR), F32),
+            *scatter_scratch(groups, part_rows, PAIR),
+            *scatter_scratch(3 * groups, part_rows, PAIR),
+            *[ref for dims in small for ref in SmallSum.scratch(dims)],
         ],
-        compiler_params=pltpu.CompilerParams(vmem_limit_bytes=LIMIT),
-        cost_estimate=pl.CostEstimate(
-            flops=16 * rows * width * width + 40 * rows * SLOTS * width,
-            bytes_accessed=40 * rows * width, transcendentals=rows * SLOTS * width // HD,
+        compiler_params=pltpu.CompilerParams(
+            vmem_limit_bytes=LIMIT, collective_id=2, has_side_effects=True
         ),
         name="attend_back",
-    )(lengths, a_turned, hidden_b, hidden_turned, qkv, mixed, log_total, x, hidden_grad, gain,
-      qkv_weight, merge_weight)
+    )(
+        lengths, a_turned, hidden_b, hidden_turned, qkv, mixed, log_total, x, hidden_grad, gain,
+        qkv_whole, merge_whole, second_sums, reduce_bias_grad, loss, expand_bias_grad,
+    )
 
 
 def body(
@@ -1026,8 +1150,7 @@
         line(second_shift), heads_bias, expand_bias.reshape(1, -1),
         [query_key_value_weight, merge_weight, expand_weight, reduce_weight],
     )
-    qkv_full = wholes[0].reshape(3, halves, width, -1)
-    merge_full, expand_full, reduce_full = (whole.reshape(halves, width, -1) for whole in wholes[1:])
+    expand_full, reduce_full = (whole.reshape(halves, width, -1) for whole in wholes[2:])
     columns = feed_width(halves)
     steps = hidden // halves // columns
     outputs, result_grad, result_b, result_turned, reduce_bias_grad, loss = feed(
@@ -1037,61 +1160,30 @@
         result_b, result_turned, second_turned, expand_full, reduce_full, activ, slope, hidden_state,
         result_grad, line(second_gain),
     )
-    reduce_grad = lax.psum_scatter(
-        reduce_grad.reshape(halves * width, -1), EVERY, scatter_dimension=0, tiled=True
-    ).astype(F32)
-    merge_grad, heads_grad, bias_grad, inputs_grad, first_sums = attend_back(
+    merge_grad, heads_grad, inputs_grad, early, expand_sum, late, heads_sum = attend_back(
         mine, a_turned, hidden_b, hidden_turned, qkv, mixed, log_total, inputs, hidden_grad,
-        line(first_gain), qkv_full, merge_full,
+        line(first_gain), wholes[0], wholes[1], second_sums, reduce_bias_grad, loss, expand_bias_grad,
     )
-    bias_grad = jnp.moveaxis(bias_grad.reshape(groups, halves, 3, PAIR), 0, 2).reshape(halves, 3, -1)
-    expand_bias_grad = jnp.moveaxis(expand_bias_grad.reshape(steps, halves, columns), 0, 1)
-    sums = jnp.sum(jnp.concatenate([first_sums, second_sums, reduce_bias_grad[None]]), axis=1)
-    small = jnp.concatenate(
-        [
-            sums.reshape(-1),
-            bias_grad[:, 0].reshape(-1),
-            bias_grad[:, 2].reshape(-1),
-            expand_bias_grad.reshape(-1),
-            jnp.sum(loss).reshape(1),
-        ]
-    )
-    length = small.shape[0]
-    small = jnp.pad(small, (0, -length % 1024)).reshape(-1, 128)
-    size = sizes()
-    places = tuple(size[a] for a in AXES)
-    heads_grad, merge_grad, expand_grad, small = scatter(
-        [
-            heads_grad.reshape(3, *places, -1, piece_width),
-            merge_grad.reshape(*places, -1, piece_width),
-            expand_grad.reshape(*places, -1, hidden // halves),
-        ],
-        small, 1, piece_width, (), 1,
-    )
-    small = small.reshape(-1)
-    vectors = small[: 6 * width].reshape(6, width)
-    heads_bias_sum = lax.dynamic_slice_in_dim(
-        small[6 * width : 8 * width].reshape(2, width), tensor * piece_width, piece_width, 1
-    )
-    expand_bias_sum = lax.dynamic_slice_in_dim(
-        small, 8 * width + tensor * (hidden // halves), hidden // halves
-    )
+    heads_sum = jnp.moveaxis(heads_sum.reshape(groups, halves, 3, PAIR), 0, 2)
+    heads_sum = lax.dynamic_index_in_dim(heads_sum, tensor, 0, False).reshape(3, piece_width)
+    expand_sum = jnp.moveaxis(expand_sum.reshape(steps, halves, columns), 0, 1)
+    expand_sum = lax.dynamic_index_in_dim(expand_sum, tensor, 0, False).reshape(-1)
     return (
-        small[length - 1] / count,
+        early[4, 0] / count,
         outputs,
         inputs_grad,
-        vectors[0],
-        vectors[1],
+        late[0],
+        late[1],
         heads_grad,
-        heads_bias_sum,
+        heads_sum[::2],
         merge_grad,
-        vectors[4],
-        vectors[2],
-        vectors[3],
+        early[2],
+        early[0],
+        early[1],
         expand_grad,
-        expand_bias_sum,
+        expand_sum,
         reduce_grad,
-        vectors[5],
+        early[3],
     )
 
 

time: 497 us -> 438 us (0.88)
  Pallas kernels: 461 us -> 418 us
  between operations: 16.7 us -> 3.15 us
    pallas_call x2 -> x1, Pallas kernels: 199 us -> 126 us  [attend_back(): pl.pallas_call(attend_back_kernel, grid=(groups * images,), in_specs=[SCA...]
    pallas_call x1, Pallas kernels: 74 us -> 104 us  [feed_back(): pl.pallas_call(feed_back_kernel, grid=(steps,), in_specs=[whole, turned,...]
    unnamed x19 -> x17, local copies, waits for them, and re-layouts: 5.26 us -> 10.8 us
  transfers between devices with their start and end apart: 1 -> 0, of which waited for: 0 -> 0; matrix products, arithmetic and copies ran while one was open for 2% -> 0% of each run, Pallas kernels for 40% -> 0%
where the time goes in v4:
time: 438 us
  Pallas kernels  418 us (95%)
  local copies, waits for them, and re-layouts  15.4 us (4%)
    pallas_call x1, Pallas kernels, forward(): pl.pallas_call(partial(forward_kernel, columns, OFFSETS, feed_columns), g...  162 us
    pallas_call x1, Pallas kernels, attend_back(): pl.pallas_call(attend_back_kernel, grid=(groups * images,), in_specs=[SCA...  126 us
    pallas_call x1, Pallas kernels, feed_back(): pl.pallas_call(feed_back_kernel, grid=(steps,), in_specs=[whole, turned,...  104 us
    pallas_call x1, Pallas kernels, feed(): pl.pallas_call(feed_kernel, grid=(steps,), in_specs=[SCALARS, SCALARS, pl...  26 us
    unnamed x17, local copies, waits for them, and re-layouts  10.8 us

profile of v4, /device:TPU:0, one launch (start us, length us, event | category | flops | bytes accessed | tf_op | source)
XLA Modules:
  0.0 437.7 jit_solution(17370968022466203395)
XLA Ops:
  0.7 1.3 reduce_sum.9
  2.6 1.2 dynamic_slice.9.lengths
  3.8 162.3 %forward.1 = (bf16[1024,1280]{1,0:T(8,128)(2,1)}, bf16[4,1280,768]{2,1,0:T(8,128)(2,1)}, bf16[4,1280,256]{2,1,0:T(8,128)(2,1)}, f32[4,4,2,640]{3,2,1,0:T(2,128)}...) custom-call(s32[4]{0:T(128)} %dynamic_slice.9.lengths, ...), custom_call_target="tpu_custom_call" | custom-call | tf_op jit(solution)/shard_map/forward/pallas_call | solution.py:953
  166.2 26.0 %feed.1 = (bf16[1280,1024]{1,0:T(8,128)(2,1)}, f32[1280,1024]{1,0:T(8,128)}, bf16[1280,1024]{1,0:T(8,128)(2,1)}, bf16[1024,1280]{1,0:T(8,128)(2,1)}, f32[1,8,1024]{2,1,0:T(8,128)}, /*index=5*/f32[1,8,1024]{2,1,0:T(8,128)}) custom-call(s32[4]{0:T(128)} %dynamic_slice.9.lengths, f32[1]{0:T(128)} %bitcast.6.count, ...), custom_call_target="tpu_custom_call" | custom-call | flops 10737418240 | bytes 45088768 | tf_op jit(solution)/shard_map/feed/pallas_call | solution.py:1005
  192.2 103.7 %feed_back.1 = (f32[64,2048]{1,0:T(8,128)}, f32[64,2048]{1,0:T(8,128)}, f32[8,1,512]{2,1,0:T(1,128)}, f32[1280,1024]{1,0:T(8,128)}, bf16[1280,1024]{1,0:T(8,128)...) custom-call(bf16[1280,1024]{1,0:T(8,128)(2,1)} %get-tuple-element.51.result_b, ...), custom_call_target="tpu_custom_call" | custom-call | tf_op jit(solution)/shard_map/feed_back/pallas_call | solution.py:1037
  295.8 125.9 %attend_back.1 = (f32[64,512]{1,0:T(8,128)}, f32[3,64,512]{2,1,0:T(8,128)}, f32[1280,1024]{1,0:T(8,128)}, f32[5,1024]{1,0:T(8,128)}, f32[8,512]{1,0:T(8,128)}, /*index=5*/f32[2,1024]{1,0:T(2,128)}, f32[4,768]{1,0:T(4,128)}) custom-call(s32[4]{0:T(128)} %dynamic_slice.9.lengths, bf16[1024,1280]{1,0:T(8,128)(2,1)} %get-tuple-element.47.a_turned, ...), custom_call_target="tpu_custom_call" | custom-call | tf_op jit(solution)/shard_map/attend_back/pallas_call | solution.py:1076
  421.7 1.2 slice.24
  423.5 0.7 dynamic-slice_bitcast_fusion.1
  424.2 0.7 dynamic-slice_bitcast_fusion
  424.9 0.6 copy.32
  425.6 0.6 slice.27
  426.2 1.6 fusion
  427.7 0.0 copy-start.2
  427.7 0.0 copy-start.3
  427.7 0.0 copy-start.1
  427.8 0.0 copy-start
  427.8 5.8 %copy.40 = f32[1280,1024]{1,0:T(8,128)} copy(f32[1280,1024]{1,0:T(8,128)} %get-tuple-element.104) | data formatting | bytes 10485760
  433.6 0.0 copy-done.2
  433.6 0.7 copy.41
  434.3 0.0 copy-done.3
  434.3 0.7 copy.42
  435.0 0.0 copy-done.1
  435.0 0.8 copy.43
  435.8 0.0 copy-done
  435.8 0.8 copy.44
  (1 shorter events, 0.0 us)
Async XLA Ops:
  427.7 5.8 %copy-start.2 = (f32[3,64,512]{2,1,0:T(8,128)S(1)}, f32[3,64,512]{2,1,0:T(8,128)}, u32[]{:S(2)}) copy-start(f32[3,64,512]{2,1,0:T(8,128)} %get-tuple-element.107) | copy-start | bytes 1179652
  427.7 6.6 %copy-start.3 = (f32[64,512]{1,0:T(8,128)S(1)}, f32[64,512]{1,0:T(8,128)}, u32[]{:S(2)}) copy-start(f32[64,512]{1,0:T(8,128)} %get-tuple-element.109) | copy-start | bytes 393220
  427.7 7.2 %copy-start.1 = (f32[64,2048]{1,0:T(8,128)S(1)}, f32[64,2048]{1,0:T(8,128)}, u32[]{:S(2)}) copy-start(f32[64,2048]{1,0:T(8,128)} %get-tuple-element.113) | copy-start | bytes 1572868
  427.8 8.0 %copy-start = (f32[64,2048]{1,0:T(8,128)S(1)}, f32[64,2048]{1,0:T(8,128)}, u32[]{:S(2)}) copy-start(f32[64,2048]{1,0:T(8,128)} %get-tuple-element.115) | copy-start | bytes 1572868

commit v5 on v4

--- a/solution.py
+++ b/solution.py
@@ -12,6 +12,7 @@
 HD = 64
 SLOTS = 320
 PAIR = 2 * HD
+BLOCK = SLOTS // 2
 
 EPSILON = 1e-05
 MASKED_SCORE = -1e30
@@ -445,14 +446,20 @@
     return at
 
 
+def forward_pieces(parts, width):
+    pieces = pieces_of(parts, width)
+    return sorted(pieces, key=lambda which: (max(which[0], 0) if which[0] < 2 else 2, which[2], which[0]))
+
+
 def forward_kernel(
     width_of_piece, offsets, feed_columns,
-    lengths, x_ref, gain, shift, merge_bias, gain_2, shift_2, heads_bias, expand_bias,
-    qkv_part, merge_part, expand_part, reduce_part,
-    a_turned, qkv_ref, mixed_ref, log_ref, hidden_ref, second_ref, second_turned, activ, slope,
-    qkv_full, merge_full, expand_full, reduce_full,
-    a_ref, qkv_held, merge_held, tiles, heads_bias_all, expand_bias_all,
-    send_sem, recv_sem, own_sem, share_send, share_recv, share_own, held_sem, tile_sem,
+    lengths, count, x_ref, teacher, gain, shift, merge_bias, gain_2, shift_2, reduce_bias,
+    heads_bias, expand_bias, qkv_part, merge_part, expand_part, reduce_part,
+    a_turned, qkv_ref, mixed_ref, log_ref, second_turned, activ, slope,
+    out, grad_b, grad_turned, bias_grad, loss,
+    hidden, grad, qkv_full, merge_full, expand_full, reduce_full,
+    hidden_ref, second_ref, a_ref, qkv_held, merge_held, tiles, heads_bias_all, expand_bias_all,
+    send_sem, recv_sem, own_sem, share_send, share_recv, share_own, held_sem, tile_sem, keep_sem,
 ):
     now = pl.program_id(0)
     rows = x_ref.shape[0]
@@ -463,7 +470,7 @@
     feed_steps = expand_part.shape[1] // feed_columns
     steps = attention_steps + feed_steps
     parts = [qkv_part, merge_part, expand_part, reduce_part]
-    pieces = pieces_of(parts, width_of_piece)
+    pieces = forward_pieces(parts, width_of_piece)
     gather = Gather(
         pieces, width_of_piece, offsets, parts, [qkv_full, merge_full, expand_full, reduce_full],
         (send_sem, recv_sem, own_sem),
@@ -474,8 +481,7 @@
     ]
     tiles_of_piece = width_of_piece // feed_columns
     needed = [
-        0 if a == 0 else images - 1 if a == 1
-        else max(attention_steps + col * tiles_of_piece - 1, 0) if a == 2 else steps - 1
+        0 if a == 0 else images - 1 if a == 1 else max(attention_steps + col * tiles_of_piece - 1, 0)
         for a, _, col in pieces
     ]
     when = schedule(gather.ticks(), offsets[-1], needed, steps)
@@ -488,16 +494,23 @@
         source, target = (qkv_full.at[lead], qkv_held.at[lead]) if a == 0 else (merge_full, merge_held)
         return pltpu.make_async_copy(source, target, held_sem.at[n])
 
-    def tile_copy(j):
+    def tile_copies(j):
         block = pl.ds(j * feed_columns, feed_columns)
-        return pltpu.make_async_copy(
-            expand_full.at[:, :, :, :, :, block], tiles.at[j % 2], tile_sem.at[j % 2]
-        )
-
-    def fetch_tile(j):
-        if j % tiles_of_piece == 0:
-            gather.arrived(4 + j // tiles_of_piece)
-        tile_copy(j).start()
+        return [
+            pltpu.make_async_copy(
+                full.at[:, :, :, :, :, block], tiles.at[j % 2, kind], tile_sem.at[j % 2, kind]
+            )
+            for kind, full in enumerate((expand_full, reduce_full))
+        ]
+
+    def fetch_tiles(j):
+        for kind, copy in enumerate(tile_copies(j)):
+            if j % tiles_of_piece == 0:
+                gather.arrived(4 + 2 * (j // tiles_of_piece) + kind)
+            copy.start()
+
+    def keep_hidden():
+        return pltpu.make_async_copy(hidden_ref, hidden, keep_sem)
 
     @pl.when(now == 0)
     def _():
@@ -505,11 +518,11 @@
         for share in shares:
             share.begin()
         early = [k for k in range(gather.ticks()) if when[k] == 0]
-        blocks = rows // 32
+        blocks = rows // BLOCK
         per = -(-blocks // max(len(early), 1))
 
         def norm(i, _):
-            at = pl.ds(pl.multiple_of(i * 32, 32), 32)
+            at = pl.ds(pl.multiple_of(i * BLOCK, BLOCK), BLOCK)
             x = x_ref[at, :].astype(F32)
             hidden_ref[at, :] = x + merge_bias[...]
             a_ref[at, :] = (centred(x)[0] * gain[...] + shift[...]).astype(BF16)
@@ -586,30 +599,35 @@
 
     @pl.when(now == attention_steps - 1)
     def _():
-        fetch_tile(0)
+        keep_hidden().start()
+        fetch_tiles(0)
 
         def norm(_, at):
             hat, _ = centred(hidden_ref[at, :])
             second_ref[at, :] = (hat * gain_2[...] + shift_2[...]).astype(BF16)
 
-        row_blocks(rows, 32, norm)
+        row_blocks(rows, BLOCK, norm)
         transpose_into(second_ref, second_turned)
 
     for j in range(feed_steps):
 
         @pl.when(now == attention_steps + j)
         def _(j=j):
-            tile_copy(j).wait()
+            if j == 0:
+                keep_hidden().wait()
+            for copy in tile_copies(j):
+                copy.wait()
             if j + 1 < feed_steps:
-                fetch_tile(j + 1)
+                fetch_tiles(j + 1)
 
     @pl.when(now >= attention_steps)
     def _():
         j = now - attention_steps
         block = pl.ds(pl.multiple_of(j * feed_columns, feed_columns), feed_columns)
         slot = lax.rem(j, 2)
-        weight = jnp.concatenate(
-            [tiles[slot, t].reshape(-1, feed_columns) for t in range(halves)], axis=-1
+        weight, reduce_tile = (
+            jnp.concatenate([tiles[slot, kind, t].reshape(-1, feed_columns) for t in range(halves)], axis=-1)
+            for kind in range(2)
         )
         bias = jnp.concatenate([expand_bias_all[t, :, block] for t in range(halves)], axis=-1)
         for i in range(images):
@@ -618,55 +636,38 @@
             square = z * z
             bend = jnp.tanh(0.7978845608 * z * (1.0 + 0.044715 * square))
             half = 0.5 + 0.5 * bend
-            activ[0, at, :] = (z * half).astype(BF16)
+            act = (z * half).astype(BF16)
+            activ[0, at, :] = act
             inner = 0.7978845608 * z * (1.0 + (3 * 0.044715) * square)
             slope[0, at, :] = (half + 0.5 * inner * (1.0 - bend * bend)).astype(BF16)
+            hidden_ref[at, :] += dot(act, reduce_tile, 1, 1)
 
     @pl.when(now == steps - 1)
-    def _():
-        for n in range(8, gather.count):
-            gather.arrived(n)
-        gather.end()
-        for share in shares:
-            share.end()
-
-
-def feed_kernel(
-    lengths, count, activ, hidden, reduce, reduce_bias, teacher,
-    out, grad, grad_b, grad_turned, bias_grad, loss, total,
-):
-    step = pl.program_id(0)
-    rows = hidden.shape[0]
-    reduce_tile = side_by_side(reduce)
-
-    @pl.when(step == 0)
-    def _():
-        total[...] = jnp.zeros_like(total)
-
-    for i in range(rows // SLOTS):
-        at = slice(i * SLOTS, (i + 1) * SLOTS)
-        total[at, :] += dot(activ[0, at, :], reduce_tile, 1, 1)
-
-    @pl.when(step == pl.num_programs(0) - 1)
     def _():
         bias_grad[...] = jnp.zeros_like(bias_grad)
         loss[...] = jnp.zeros_like(loss)
 
         def end(i, at):
-            image, block = lax.div(i, SLOTS // 32), lax.rem(i, SLOTS // 32)
-            slot = block * 32 + lax.broadcasted_iota(jnp.int32, (32, 1), 0)
+            image, block = lax.div(i, SLOTS // BLOCK), lax.rem(i, SLOTS // BLOCK)
+            slot = block * BLOCK + lax.broadcasted_iota(jnp.int32, (BLOCK, 1), 0)
             valid = slot < lengths[image]
-            result = jnp.where(valid, hidden[at, :] + total[at, :] + reduce_bias[...], 0.0)
+            result = jnp.where(valid, hidden_ref[at, :] + reduce_bias[...], 0.0)
             out[at, :] = result.astype(BF16)
             error = jnp.where(valid, result - teacher[at, :].astype(F32), 0.0)
             loss[0] += fold(error * error)
             back = 2.0 * error / count[0]
             bias_grad[0] += fold(back)
-            grad[at, :] = back
+            hidden_ref[at, :] = back
             grad_b[at, :] = back.astype(BF16)
 
-        row_blocks(rows, 32, end)
+        row_blocks(rows, BLOCK, end)
+        keep = pltpu.make_async_copy(hidden_ref, grad, keep_sem)
+        keep.start()
         transpose_into(grad_b, grad_turned)
+        keep.wait()
+        gather.end()
+        for share in shares:
+            share.end()
 
 
 def feed_back_kernel(
@@ -691,12 +692,12 @@
         here.greet()
         total[...] = jnp.zeros_like(total)
 
-    for stage in range(3, -1, -1):
-
-        @pl.when(step >= stage + 1)
-        def _(stage=stage):
-            for scatter in scatters:
-                scatter.tick(step - 1 - stage, stage)
+    def ticks(p, back):
+        for stage in range(3, -1, -1):
+
+            @pl.when(step >= stage + back)
+            def _(stage=stage):
+                scatters[p].tick(step - back - stage, stage)
 
     def stage_out(p, part):
         for t in range(halves):
@@ -705,6 +706,7 @@
         scatters[p].begin(step)
 
     stage_out(0, dot(result_turned[...], activ[0]))
+    ticks(1, 1)
     bias = jnp.zeros((8, halves * columns), F32)
     parts = []
     for i in range(rows // SLOTS):
@@ -714,6 +716,7 @@
         parts.append(z_grad)
         total[at, :] += dot(z_grad, expand_tile, 1, 1)
     expand_bias_grad[0] = jnp.sum(bias, axis=0, keepdims=True)
+    ticks(0, 0)
     stage_out(1, dot(second_turned[...], jnp.concatenate(parts, axis=0)))
 
     @pl.when(step == steps - 1)
@@ -748,9 +751,10 @@
         bounds = [blocks * k // 3 for k in range(4)]
         for drain in range(4):
             for stage in range(3, -1, -1):
-                for scatter in scatters:
-                    if stage >= drain and steps + drain - 1 - stage >= 0:
-                        scatter.tick(steps + drain - 1 - stage, stage)
+                for p, first in ((0, drain + 1), (1, drain)):
+                    n = steps + first - 1 - stage
+                    if stage >= first and n >= 0:
+                        scatters[p].tick(n, stage)
             if drain < 3 and bounds[drain + 1] > bounds[drain]:
                 some(bounds[drain], bounds[drain + 1])
         for scatter in scatters:
@@ -782,9 +786,6 @@
         SmallSum(here, comm[2 * SCATTER_REFS + k * SMALL_REFS :][:SMALL_REFS]) for k in range(4)
     )
 
-    def merge_tick(c, stage):
-        merge_scatter.tick(c, stage)
-
     def qkv_tick(c, stage):
         for e in range(3):
             qkv_scatter.tick(3 * c + e, stage)
@@ -809,21 +810,6 @@
         for copy in copies:
             copy.wait()
 
-    for stage in range(4):
-
-        @pl.when(now == min(stage + 1, steps - 1))
-        def _(stage=stage):
-            early.tick(stage, early_out)
-            expand_sum.tick(stage, expand_out)
-
-    for stage in range(3, -1, -1):
-        for ready, tick in ((0, merge_tick), (images - 1, qkv_tick)):
-            since = now - 1 - stage - ready
-
-            @pl.when((since >= 0) & (lax.rem(since, images) == 0))
-            def _(stage=stage, tick=tick, since=since):
-                tick(lax.div(since, images), stage)
-
     @pl.when(image == 0)
     def _():
         weight = merge_tile(merge_held, columns)
@@ -834,6 +820,16 @@
         for t in range(halves):
             merge_staging[t] = part[:, t * PAIR : (t + 1) * PAIR].reshape(merge_staging.shape[1:])
         merge_scatter.begin(group)
+
+        @pl.when(group == 0)
+        def _():
+            early.tick(0, early_out)
+            expand_sum.tick(0, expand_out)
+
+        @pl.when(group > 0)
+        def _():
+            merge_scatter.tick(group - 1, 2)
+            qkv_tick(group - 1, 1)
 
     length = lengths[image]
     at = pl.ds(pl.multiple_of(image * SLOTS, SLOTS), SLOTS)
@@ -858,6 +854,17 @@
 
     @pl.when(image == images - 1)
     def _():
+        @pl.when(group == 0)
+        def _():
+            early.tick(1, early_out)
+            expand_sum.tick(1, expand_out)
+
+        @pl.when(group > 0)
+        def _():
+            merge_scatter.tick(group - 1, 3)
+            qkv_tick(group - 1, 2)
+
+        merge_scatter.tick(group, 0)
         weight = group_weight(qkv_held, columns)
         bias = jnp.zeros((8, halves * 3 * PAIR), F32)
         for i in range(rows // SLOTS):
@@ -875,13 +882,25 @@
             part = slice(i * SLOTS, (i + 1) * SLOTS)
             total[part, :] += dot(heads_grad[part, :], weight, 1, 1)
 
+        @pl.when(group == 0)
+        def _():
+            early.tick(2, early_out)
+            expand_sum.tick(2, expand_out)
+
+        @pl.when(group > 0)
+        def _():
+            qkv_tick(group - 1, 3)
+
+        merge_scatter.tick(group, 1)
+        qkv_tick(group, 0)
+
     @pl.when(now == steps - 1)
     def _():
         heads_sum.start(0, bias_grad[...])
         sums[...] = jnp.zeros_like(sums)
 
         def end(i, _):
-            at = pl.ds(pl.multiple_of(i * 32, 32), 32)
+            at = pl.ds(pl.multiple_of(i * BLOCK, BLOCK), BLOCK)
             hat, inverse = centred(x_ref[at, :].astype(F32))
             grad = total[at, :]
             sums[0] += fold(grad * hat)
@@ -889,29 +908,26 @@
             inputs_grad[at, :] = hidden_grad[at, :] + norm_back(grad, hat, inverse, gain[...])
             return 0
 
-        blocks = rows // 32
-
-        def drain(d):
-            for stage in range(3, -1, -1):
-                for ready, tick in ((0, merge_tick), (images - 1, qkv_tick)):
-                    since = steps + d - 1 - stage - ready
-                    if stage >= d and since >= 0 and since % images == 0 and since // images < groups:
-                        tick(since // images, stage)
-
-        drain(0)
+        blocks = rows // BLOCK
+        last = groups - 1
+        lax.fori_loop(0, blocks // 2, end, 0)
+        merge_scatter.tick(last, 2)
+        qkv_tick(last, 1)
+        early.tick(3, early_out)
+        expand_sum.tick(3, expand_out)
         heads_sum.tick(0, heads_out)
-        lax.fori_loop(0, blocks // 2, end, 0)
-        drain(1)
-        heads_sum.tick(1, heads_out)
         lax.fori_loop(blocks // 2, blocks, end, 0)
         late.start(0, jnp.sum(sums[...], axis=1))
-        drain(2)
+        merge_scatter.tick(last, 3)
+        qkv_tick(last, 2)
+        heads_sum.tick(1, heads_out)
+        late.tick(0, late_out)
+        qkv_tick(last, 3)
         heads_sum.tick(2, heads_out)
-        late.tick(0, late_out)
-        drain(3)
+        late.tick(1, late_out)
         heads_sum.tick(3, heads_out)
-        for stage in range(1, 4):
-            late.tick(stage, late_out)
+        late.tick(2, late_out)
+        late.tick(3, late_out)
         merge_scatter.end(groups)
         qkv_scatter.end(3 * groups)
 
@@ -936,7 +952,9 @@
     return max(PAIR, 512 // halves)
 
 
-def forward(lengths, x, gain, shift, merge_bias, gain_2, shift_2, heads_bias, expand_bias, parts):
+def forward(
+    lengths, count, x, teacher, gain, shift, merge_bias, gain_2, shift_2, reduce_bias, heads_bias, expand_bias, parts
+):
     rows, width = x.shape
     halves, columns = lax.axis_size("tensor"), parts[0].shape[2]
     groups, images = columns // PAIR, rows // SLOTS
@@ -945,7 +963,7 @@
     feed_steps = parts[2].shape[1] // feed_columns
     pieces = len(pieces_of(parts, columns))
     most = max(sizes().values()) - 1
-    line = once((1, width))
+    line, whole, turned = once((1, width)), once((rows, width)), once((width, rows))
     group_at = lambda s: lax.min(lax.div(s, images), groups - 1)
     feed_at = lambda s: lax.max(s - attention_steps, 0)
     wholes = [whole_shape(part) for part in parts]
@@ -953,32 +971,37 @@
     return pl.pallas_call(
         partial(forward_kernel, columns, OFFSETS, feed_columns),
         grid=(attention_steps + feed_steps,),
-        in_specs=[SCALARS, once((rows, width)), *[line] * 5, *[ELSEWHERE] * 6],
+        in_specs=[SCALARS, SCALARS, whole, whole, *[line] * 6, *[ELSEWHERE] * 6],
         out_specs=[
-            once((width, rows)),
+            turned,
             pl.BlockSpec((1, rows, halves * 3 * PAIR), lambda s: (group_at(s), 0, 0)),
             pl.BlockSpec((1, rows, halves * PAIR), lambda s: (group_at(s), 0, 0)),
             pl.BlockSpec(
                 (1, 1, halves, 2 * SLOTS),
                 lambda s: (group_at(s), jnp.where(s < attention_steps, lax.rem(s, images), images - 1), 0, 0),
             ),
-            once((rows, width)), once((rows, width)), once((width, rows)), saved, saved,
-            *[ELSEWHERE] * 4,
+            turned, saved, saved, whole, whole, turned, once((1, 8, width)), once((1, 8, width)),
+            *[ELSEWHERE] * 6,
         ],
         out_shape=[
             shape((width, rows)),
             shape((groups, rows, halves * 3 * PAIR)),
             shape((groups, rows, halves * PAIR)),
             shape((groups, images, halves, 2 * SLOTS), F32),
-            shape((rows, width), F32), shape((rows, width)), shape((width, rows)),
+            shape((width, rows)),
             *[shape((feed_steps, rows, halves * feed_columns))] * 2,
+            shape((rows, width)), shape((rows, width)), shape((width, rows)),
+            shape((1, 8, width), F32), shape((1, 8, width), F32),
+            shape((rows, width), F32), shape((rows, width), F32),
             *[shape(dims) for dims in wholes],
         ],
         scratch_shapes=[
+            pltpu.VMEM((rows, width), F32),
+            pltpu.VMEM((rows, width), BF16),
             pltpu.VMEM((rows, width), BF16),
             pltpu.VMEM(wholes[0], BF16),
             pltpu.VMEM(wholes[1], BF16),
-            pltpu.VMEM((2, *wholes[2][:-1], feed_columns), BF16),
+            pltpu.VMEM((2, 2, *wholes[2][:-1], feed_columns), BF16),
             pltpu.VMEM((halves, *heads_bias.shape), F32),
             pltpu.VMEM((halves, *expand_bias.shape), F32),
             pltpu.SemaphoreType.DMA((pieces, 2, 4, most)),
@@ -988,41 +1011,17 @@
             pltpu.SemaphoreType.DMA((2, halves)),
             pltpu.SemaphoreType.DMA((2,)),
             pltpu.SemaphoreType.DMA((4,)),
-            pltpu.SemaphoreType.DMA((2,)),
+            pltpu.SemaphoreType.DMA((2, 2)),
+            pltpu.SemaphoreType.DMA(()),
         ],
         compiler_params=pltpu.CompilerParams(
             vmem_limit_bytes=LIMIT, collective_id=0, has_side_effects=True
         ),
         name="forward",
-    )(lengths, x, gain, shift, merge_bias, gain_2, shift_2, heads_bias, expand_bias, *parts)
-
-
-def feed(lengths, count, activ, hidden, reduce, reduce_bias, teacher):
-    rows, width = hidden.shape
-    halves, _, wide = reduce.shape
-    steps, columns = activ.shape[0], activ.shape[2] // halves
-    whole = once((rows, width))
-    return pl.pallas_call(
-        feed_kernel,
-        grid=(steps,),
-        in_specs=[
-            SCALARS, SCALARS, pl.BlockSpec((1, rows, halves * columns), lambda j: (j, 0, 0)), whole,
-            pl.BlockSpec((halves, width, columns), lambda j: (0, 0, j)), once((1, width)), whole,
-        ],
-        out_specs=[whole, whole, whole, once((width, rows)), once((1, 8, width)), once((1, 8, width))],
-        out_shape=[
-            shape((rows, width)), shape((rows, width), F32), shape((rows, width)), shape((width, rows)),
-            shape((1, 8, width), F32), shape((1, 8, width), F32),
-        ],
-        scratch_shapes=[pltpu.VMEM((rows, width), F32)],
-        compiler_params=pltpu.CompilerParams(vmem_limit_bytes=LIMIT),
-        cost_estimate=pl.CostEstimate(
-            flops=2 * rows * width * halves * wide,
-            bytes_accessed=2 * rows * halves * wide + 2 * width * halves * wide + 20 * rows * width,
-            transcendentals=0,
-        ),
-        name="feed",
-    )(lengths, count, activ, hidden, reduce, reduce_bias, teacher)
+    )(
+        lengths, count, x, teacher, gain, shift, merge_bias, gain_2, shift_2, reduce_bias,
+        heads_bias, expand_bias, *parts,
+    )
 
 
 def feed_back(result_b, result_turned, second_turned, expand, reduce, activ, slope, hidden, result_grad, gain):
@@ -1145,17 +1144,17 @@
     count = jnp.sum(lengths).astype(F32)
     line = lambda vector: vector.reshape(1, width)
 
-    a_turned, qkv, mixed, log_total, hidden_state, _, second_turned, activ, slope, *wholes = forward(
-        mine, inputs, line(first_gain), line(first_shift), line(merge_bias), line(second_gain),
-        line(second_shift), heads_bias, expand_bias.reshape(1, -1),
+    (
+        a_turned, qkv, mixed, log_total, second_turned, activ, slope, outputs, result_b, result_turned,
+        reduce_bias_grad, loss, hidden_state, result_grad, *wholes,
+    ) = forward(
+        mine, count.reshape(1), inputs, teacher, line(first_gain), line(first_shift), line(merge_bias),
+        line(second_gain), line(second_shift), line(reduce_bias), heads_bias, expand_bias.reshape(1, -1),
         [query_key_value_weight, merge_weight, expand_weight, reduce_weight],
     )
     expand_full, reduce_full = (whole.reshape(halves, width, -1) for whole in wholes[2:])
     columns = feed_width(halves)
     steps = hidden // halves // columns
-    outputs, result_grad, result_b, result_turned, reduce_bias_grad, loss = feed(
-        mine, count.reshape(1), activ, hidden_state, reduce_full, line(reduce_bias), teacher
-    )
     reduce_grad, expand_grad, expand_bias_grad, hidden_grad, hidden_b, hidden_turned, second_sums = feed_back(
         result_b, result_turned, second_turned, expand_full, reduce_full, activ, slope, hidden_state,
         result_grad, line(second_gain),

time: 438 us -> 411 us (0.938)
  Pallas kernels: 418 us -> 390 us
    pallas_call x1 -> x0, Pallas kernels: 26 us -> none  [feed(): pl.pallas_call(feed_kernel, grid=(steps,), in_specs=[SCALARS, SCALARS, pl...]
    pallas_call x1, Pallas kernels: 126 us -> 114 us  [attend_back(): pl.pallas_call(attend_back_kernel, grid=(groups * images,), in_specs=[SCA...]
    pallas_call x1, Pallas kernels: 162 us -> 173 us  [forward(): pl.pallas_call(partial(forward_kernel, columns, OFFSETS, feed_columns), g...]
    unnamed x17 -> x20, local copies, waits for them, and re-layouts: 10.8 us -> 11.1 us
where the time goes in v5:
time: 411 us; the launch traced here: 410 us
  Pallas kernels  390 us (95%)
  local copies, waits for them, and re-layouts  15.7 us (4%)
    pallas_call x1, Pallas kernels, forward(): pl.pallas_call(partial(forward_kernel, columns, OFFSETS, feed_columns), g...  173 us
    pallas_call x1, Pallas kernels, attend_back(): pl.pallas_call(attend_back_kernel, grid=(groups * images,), in_specs=[SCA...  114 us
    pallas_call x1, Pallas kernels, feed_back(): pl.pallas_call(feed_back_kernel, grid=(steps,), in_specs=[whole, turned,...  103 us
    unnamed x20, local copies, waits for them, and re-layouts  11.1 us

profile of v5, /device:TPU:0, one launch (start us, length us, event | category | flops | bytes accessed | tf_op | source)
XLA Modules:
  0.0 410.5 jit_solution(8359154298841454681)
XLA Ops:
  0.7 1.3 reduce_sum.9
  2.6 1.2 dynamic_slice.9.lengths
  3.8 173.1 %forward.1 = (bf16[1024,1280]{1,0:T(8,128)(2,1)}, bf16[4,1280,768]{2,1,0:T(8,128)(2,1)}, bf16[4,1280,256]{2,1,0:T(8,128)(2,1)}, f32[4,4,2,640]{3,2,1,0:T(2,128)}...) custom-call(s32[4]{0:T(128)} %dynamic_slice.9.lengths, ...), custom_call_target="tpu_custom_call" | custom-call | tf_op jit(solution)/shard_map/forward/pallas_call | solution.py:971
  176.9 103.1 %feed_back.1 = (f32[64,2048]{1,0:T(8,128)}, f32[64,2048]{1,0:T(8,128)}, f32[8,1,512]{2,1,0:T(1,128)}, f32[1280,1024]{1,0:T(8,128)}, bf16[1280,1024]{1,0:T(8,128)...) custom-call(bf16[1280,1024]{1,0:T(8,128)(2,1)} %get-tuple-element.48.result_b, ...), custom_call_target="tpu_custom_call" | custom-call | tf_op jit(solution)/shard_map/feed_back/pallas_call | solution.py:1036
  280.1 114.1 %attend_back.1 = (f32[64,512]{1,0:T(8,128)}, f32[3,64,512]{2,1,0:T(8,128)}, f32[1280,1024]{1,0:T(8,128)}, f32[5,1024]{1,0:T(8,128)}, f32[8,512]{1,0:T(8,128)}, /*index=5*/f32[2,1024]{1,0:T(2,128)}, f32[4,768]{1,0:T(4,128)}) custom-call(s32[4]{0:T(128)} %dynamic_slice.9.lengths, bf16[1024,1280]{1,0:T(8,128)(2,1)} %get-tuple-element.47.a_turned, ...), custom_call_target="tpu_custom_call" | custom-call | tf_op jit(solution)/shard_map/attend_back/pallas_call | solution.py:1075
  394.2 1.2 slice.24
  396.0 0.7 dynamic-slice_bitcast_fusion.1
  396.7 0.7 dynamic-slice_bitcast_fusion
  397.4 0.6 copy.32
  398.0 0.6 slice.27
  398.7 1.6 fusion
  400.2 0.0 copy-start
  400.2 3.6 copy.41
  403.9 0.1 copy-done
  404.0 0.0 copy-start.3
  404.0 0.0 copy-start.4
  404.0 0.0 copy-start.2
  404.0 0.0 copy-start.1
  404.0 2.4 copy.42
  406.3 0.0 copy-done.3
  406.3 0.7 copy.43
  407.1 0.0 copy-done.4
  407.1 0.7 copy.44
  407.8 0.0 copy-done.2
  407.8 0.8 copy.45
  408.6 0.0 copy-done.1
  408.6 0.8 copy.46
  (1 shorter events, 0.0 us)
Async XLA Ops:
  400.2 3.7 copy-start
  404.0 2.4 copy-start.3
  404.0 3.1 copy-start.4
  404.0 3.8 copy-start.2
  404.0 4.6 %copy-start.1 = (f32[64,2048]{1,0:T(8,128)S(1)}, f32[64,2048]{1,0:T(8,128)}, u32[]{:S(2)}) copy-start(f32[64,2048]{1,0:T(8,128)} %get-tuple-element.115) | copy-start | bytes 1572868

commit v6 on v5

--- a/solution.py
+++ b/solution.py
@@ -971,7 +971,9 @@
     return pl.pallas_call(
         partial(forward_kernel, columns, OFFSETS, feed_columns),
         grid=(attention_steps + feed_steps,),
-        in_specs=[SCALARS, SCALARS, whole, whole, *[line] * 6, *[ELSEWHERE] * 6],
+        in_specs=[
+            SCALARS, SCALARS, whole, whole, *[line] * 6, *[ELSEWHERE] * 2, *[once(part.shape) for part in parts]
+        ],
         out_specs=[
             turned,
             pl.BlockSpec((1, rows, halves * 3 * PAIR), lambda s: (group_at(s), 0, 0)),
@@ -1115,6 +1117,51 @@
     )
 
 
+def finish_kernel(count, early, late, expand_sum, heads_sum, *refs):
+    arrays = (len(refs) - 10) // 2
+    sources, targets = refs[:arrays], refs[arrays : 2 * arrays]
+    loss, first_gain, first_shift, second_gain, second_shift, merge_bias, reduce_bias, heads_bias, expand_bias, sem = (
+        refs[2 * arrays :]
+    )
+    copies = [
+        pltpu.make_async_copy(source, target, sem.at[n])
+        for n, (source, target) in enumerate(zip(sources, targets, strict=True))
+    ]
+    for copy in copies:
+        copy.start()
+    tensor = lax.axis_index("tensor")
+    loss[...] = early[4:5, 0:1] / count[0]
+    for k, target in enumerate((second_gain, second_shift, merge_bias, reduce_bias)):
+        target[...] = early[k : k + 1]
+    first_gain[...] = late[0:1]
+    first_shift[...] = late[1:2]
+    for k, e in enumerate((0, 2)):
+        columns = pl.ds(pl.multiple_of((tensor * 3 + e) * PAIR, PAIR), PAIR)
+        for group in range(heads_sum.shape[0]):
+            heads_bias[k : k + 1, group * PAIR : (group + 1) * PAIR] = heads_sum[group : group + 1, columns]
+    wide = expand_bias.shape[1] // expand_sum.shape[0]
+    columns = pl.ds(pl.multiple_of(tensor * wide, wide), wide)
+    for step in range(expand_sum.shape[0]):
+        expand_bias[:, step * wide : (step + 1) * wide] = expand_sum[step : step + 1, columns]
+    for copy in copies:
+        copy.wait()
+
+
+def finish(count, early, late, expand_sum, heads_sum, arrays):
+    width, halves = early.shape[1], lax.axis_size("tensor")
+    small = [(1, 1), *[(1, width)] * 6, (2, heads_sum.shape[0] * PAIR), (1, expand_sum.size // halves)]
+    vmem = pl.BlockSpec(memory_space=pltpu.VMEM)
+    return pl.pallas_call(
+        finish_kernel,
+        in_specs=[SCALARS, *[vmem] * (4 + len(arrays))],
+        out_specs=[*[ELSEWHERE] * len(arrays), *[vmem] * len(small)],
+        out_shape=[*[shape(a.shape, a.dtype) for a in arrays], *[shape(dims, F32) for dims in small]],
+        scratch_shapes=[pltpu.SemaphoreType.DMA((len(arrays),))],
+        compiler_params=pltpu.CompilerParams(vmem_limit_bytes=LIMIT),
+        name="finish",
+    )(count, early, late, expand_sum, heads_sum, *arrays)
+
+
 def body(
     inputs,
     teacher,
@@ -1141,14 +1188,14 @@
     groups = piece_width // PAIR
     place = lax.axis_index("dp") * halves + tensor
     mine = lax.dynamic_slice_in_dim(lengths, place * images, images)
-    count = jnp.sum(lengths).astype(F32)
+    count = jnp.sum(lengths).astype(F32).reshape(1)
     line = lambda vector: vector.reshape(1, width)
 
     (
         a_turned, qkv, mixed, log_total, second_turned, activ, slope, outputs, result_b, result_turned,
         reduce_bias_grad, loss, hidden_state, result_grad, *wholes,
     ) = forward(
-        mine, count.reshape(1), inputs, teacher, line(first_gain), line(first_shift), line(merge_bias),
+        mine, count, inputs, teacher, line(first_gain), line(first_shift), line(merge_bias),
         line(second_gain), line(second_shift), line(reduce_bias), heads_bias, expand_bias.reshape(1, -1),
         [query_key_value_weight, merge_weight, expand_weight, reduce_weight],
     )
@@ -1163,26 +1210,29 @@
         mine, a_turned, hidden_b, hidden_turned, qkv, mixed, log_total, inputs, hidden_grad,
         line(first_gain), wholes[0], wholes[1], second_sums, reduce_bias_grad, loss, expand_bias_grad,
     )
-    heads_sum = jnp.moveaxis(heads_sum.reshape(groups, halves, 3, PAIR), 0, 2)
-    heads_sum = lax.dynamic_index_in_dim(heads_sum, tensor, 0, False).reshape(3, piece_width)
-    expand_sum = jnp.moveaxis(expand_sum.reshape(steps, halves, columns), 0, 1)
-    expand_sum = lax.dynamic_index_in_dim(expand_sum, tensor, 0, False).reshape(-1)
+    outputs, inputs_grad, heads_grad, merge_grad, expand_grad, reduce_grad, loss, *vectors, heads_sum, expand_sum = finish(
+        count, early, late, expand_sum, heads_sum,
+        [outputs, inputs_grad, heads_grad, merge_grad, expand_grad, reduce_grad],
+    )
+    first_gain_grad, first_shift_grad, second_gain_grad, second_shift_grad, merge_bias_grad, reduce_bias_grad = (
+        vector.reshape(width) for vector in vectors
+    )
     return (
-        early[4, 0] / count,
+        loss.reshape(()),
         outputs,
         inputs_grad,
-        late[0],
-        late[1],
+        first_gain_grad,
+        first_shift_grad,
         heads_grad,
-        heads_sum[::2],
+        heads_sum,
         merge_grad,
-        early[2],
-        early[0],
-        early[1],
+        merge_bias_grad,
+        second_gain_grad,
+        second_shift_grad,
         expand_grad,
-        expand_sum,
+        expand_sum.reshape(-1),
         reduce_grad,
-        early[3],
+        reduce_bias_grad,
     )
 
 

time: 411 us -> 403 us (0.981)
  local copies, waits for them, and re-layouts: 15.7 us -> 1.24 us
  Pallas kernels: 390 us -> 398 us
    unnamed x20 -> x0, local copies, waits for them, and re-layouts: 11.1 us -> none
    pallas_call x0 -> x1, Pallas kernels: none -> 8.11 us  [finish(): pl.pallas_call(finish_kernel, in_specs=[SCALARS, *[vmem] * (4 + len(array...]
where the time goes in v6:
time: 403 us
  Pallas kernels  398 us (99%)
    pallas_call x1, Pallas kernels, forward(): pl.pallas_call(partial(forward_kernel, columns, OFFSETS, feed_columns), g...  173 us
    pallas_call x1, Pallas kernels, attend_back(): pl.pallas_call(attend_back_kernel, grid=(groups * images,), in_specs=[SCA...  114 us
    pallas_call x1, Pallas kernels, feed_back(): pl.pallas_call(feed_back_kernel, grid=(steps,), in_specs=[whole, turned,...  103 us
    pallas_call x1, Pallas kernels, finish(): pl.pallas_call(finish_kernel, in_specs=[SCALARS, *[vmem] * (4 + len(array...  8.11 us

profile of v6, /device:TPU:0, one launch (start us, length us, event | category | flops | bytes accessed | tf_op | source)
XLA Modules:
  0.0 402.5 jit_solution(17372188242168169727)
XLA Ops:
  0.7 1.3 reduce_sum.9
  2.6 1.2 dynamic_slice.3.lengths
  3.8 173.1 %forward.1 = (bf16[1024,1280]{1,0:T(8,128)(2,1)}, bf16[4,1280,768]{2,1,0:T(8,128)(2,1)}, bf16[4,1280,256]{2,1,0:T(8,128)(2,1)}, f32[4,4,2,640]{3,2,1,0:T(2,128)}...) custom-call(s32[4]{0:T(128)} %dynamic_slice.3.lengths, ...), custom_call_target="tpu_custom_call" | custom-call | tf_op jit(solution)/shard_map/forward/pallas_call | solution.py:971
  177.0 103.1 %feed_back.1 = (f32[64,2048]{1,0:T(8,128)}, f32[64,2048]{1,0:T(8,128)}, f32[8,1,512]{2,1,0:T(1,128)}, f32[1280,1024]{1,0:T(8,128)}, bf16[1280,1024]{1,0:T(8,128)...) custom-call(bf16[1280,1024]{1,0:T(8,128)(2,1)} %get-tuple-element.63.result_b, ...), custom_call_target="tpu_custom_call" | custom-call | tf_op jit(solution)/shard_map/feed_back/pallas_call | solution.py:1038
  280.1 114.1 %attend_back.1 = (f32[64,512]{1,0:T(8,128)}, f32[3,64,512]{2,1,0:T(8,128)}, f32[1280,1024]{1,0:T(8,128)}, f32[5,1024]{1,0:T(8,128)}, f32[8,512]{1,0:T(8,128)}, /*index=5*/f32[2,1024]{1,0:T(2,128)}, f32[4,768]{1,0:T(4,128)}) custom-call(s32[4]{0:T(128)} %dynamic_slice.3.lengths, bf16[1024,1280]{1,0:T(8,128)(2,1)} %get-tuple-element.62.a_turned, ...), custom_call_target="tpu_custom_call" | custom-call | tf_op jit(solution)/shard_map/attend_back/pallas_call | solution.py:1077
  394.2 8.1 %finish.1 = (bf16[1280,1024]{1,0:T(8,128)(2,1)}, f32[1280,1024]{1,0:T(8,128)}, f32[3,64,512]{2,1,0:T(8,128)}, f32[64,512]{1,0:T(8,128)}, f32[64,2048]{1,0:T(8,12...) custom-call(f32[1]{0:T(128)} %bitcast.count, ...), custom_call_target="tpu_custom_call" | custom-call | tf_op jit(solution)/shard_map/finish/pallas_call | solution.py:1154

commit v7 on v6

--- a/solution.py
+++ b/solution.py
@@ -84,6 +84,9 @@
 def whole_shape(weight):
     size = sizes()
     return (*weight.shape[:-2], *(size[a] for a in AXES), *weight.shape[-2:])
+
+
+LEAD = 4
 
 
 class Gather:
@@ -134,14 +137,17 @@
 
     def begin(self):
         self.here.greet()
+        for n in range(min(LEAD, self.count)):
+            self.start(n, 0)
         for n in range(self.count):
-            self.start(n, 0)
             self.own(n).start()
 
     def ticks(self):
         return self.count + self.offsets[-1]
 
     def tick(self, k):
+        if k + LEAD < self.count:
+            self.start(k + LEAD, 0)
         for stage, offset in enumerate(self.offsets, 1):
             n = k - offset
             if 0 <= n < self.count:

time: 403 us -> 403 us (level)
  no operation moved by 1% of the time
where the time goes in v7:
time: 403 us
  Pallas kernels  399 us (99%)
    pallas_call x1, Pallas kernels, forward(): pl.pallas_call(partial(forward_kernel, columns, OFFSETS, feed_columns), g...  173 us
    pallas_call x1, Pallas kernels, attend_back(): pl.pallas_call(attend_back_kernel, grid=(groups * images,), in_specs=[SCA...  114 us
    pallas_call x1, Pallas kernels, feed_back(): pl.pallas_call(feed_back_kernel, grid=(steps,), in_specs=[whole, turned,...  104 us
    pallas_call x1, Pallas kernels, finish(): pl.pallas_call(finish_kernel, in_specs=[SCALARS, *[vmem] * (4 + len(array...  8.11 us

profile of v7, /device:TPU:0, one launch (start us, length us, event | category | flops | bytes accessed | tf_op | source)
XLA Modules:
  0.0 402.8 jit_solution(3458527571572187467)
XLA Ops:
  0.7 1.3 reduce_sum.9
  2.6 1.2 dynamic_slice.3.lengths
  3.8 172.5 %forward.1 = (bf16[1024,1280]{1,0:T(8,128)(2,1)}, bf16[4,1280,768]{2,1,0:T(8,128)(2,1)}, bf16[4,1280,256]{2,1,0:T(8,128)(2,1)}, f32[4,4,2,640]{3,2,1,0:T(2,128)}...) custom-call(s32[4]{0:T(128)} %dynamic_slice.3.lengths, ...), custom_call_target="tpu_custom_call" | custom-call | tf_op jit(solution)/shard_map/forward/pallas_call | solution.py:977
  176.4 104.0 %feed_back.1 = (f32[64,2048]{1,0:T(8,128)}, f32[64,2048]{1,0:T(8,128)}, f32[8,1,512]{2,1,0:T(1,128)}, f32[1280,1024]{1,0:T(8,128)}, bf16[1280,1024]{1,0:T(8,128)...) custom-call(bf16[1280,1024]{1,0:T(8,128)(2,1)} %get-tuple-element.63.result_b, ...), custom_call_target="tpu_custom_call" | custom-call | tf_op jit(solution)/shard_map/feed_back/pallas_call | solution.py:1044
  280.3 114.2 %attend_back.1 = (f32[64,512]{1,0:T(8,128)}, f32[3,64,512]{2,1,0:T(8,128)}, f32[1280,1024]{1,0:T(8,128)}, f32[5,1024]{1,0:T(8,128)}, f32[8,512]{1,0:T(8,128)}, /*index=5*/f32[2,1024]{1,0:T(2,128)}, f32[4,768]{1,0:T(4,128)}) custom-call(s32[4]{0:T(128)} %dynamic_slice.3.lengths, bf16[1024,1280]{1,0:T(8,128)(2,1)} %get-tuple-element.62.a_turned, ...), custom_call_target="tpu_custom_call" | custom-call | tf_op jit(solution)/shard_map/attend_back/pallas_call | solution.py:1083
  394.5 8.1 %finish.1 = (bf16[1280,1024]{1,0:T(8,128)(2,1)}, f32[1280,1024]{1,0:T(8,128)}, f32[3,64,512]{2,1,0:T(8,128)}, f32[64,512]{1,0:T(8,128)}, f32[64,2048]{1,0:T(8,12...) custom-call(f32[1]{0:T(128)} %bitcast.count, ...), custom_call_target="tpu_custom_call" | custom-call | tf_op jit(solution)/shard_map/finish/pallas_call | solution.py:1160
